TPU v7x, 256 devices: a whole 4x4x8 slice. The times are simulated.
256 devices in a mesh: north: 32 (over y, z), east: 8 (over x, core).
Axes of the slice: x: 4, y: 4, z: 8, core: 2. Of those that a mesh axis runs over, the one named last changes fastest.
Arguments:
- head_ensemble: float32 [2, 64, 1024, 1024], P(None, None, 'north', 'east'), may hold values from -6 to 6
- transmissivity_grid: float32 [2, 1024, 1024], P(None, 'north', 'east'), may hold values from 0.02 to 0.08
- interlayer_leakage_factor: float32 [1024, 1024], P('north', 'east'), may hold values from 0.05 to 0.3
- specific_porosity_release: float32 [1024, 1024], P('north', 'east'), may hold values from 0.3 to 1.5
- infiltration_inflow: float32 [1024, 1024], P('north', 'east'), may hold values from -1.8 to 1.8
- obs_value: float32 [2, 4, 32, 32], replicated, may hold values from -6 to 6
- obs_error: float32 [2, 4, 32, 32], replicated, may hold values from 0.1 to 1
- obs_spot: int32 [2, 4, 32, 32], replicated, may hold values from 0 to 255
- obs_live: int32 [2, 4, 32, 32], replicated, may hold values from 0 to 1
- batch_colour: int32 [2, 4], replicated, may hold values from 0 to 3, as said below
Outputs:
- analysed: float32 [2, 64, 1024, 1024], P(None, None, 'north', 'east')
Inputs may be any that keep to these rules, and one draw needn't show every extreme that they name: `obs_spot`: position of the observation in its coarse cell, as row * 16 + column. `batch_colour`: each row is an order of the four colours.
All inputs are finite; a program needn't handle non-finite values.
Results may differ from a plain program's by a relative error of at most 0.0001.
Values sent between devices are 32-bit elements; how exact they have to be, the bound alone decides.
No kernel may reach another device: no remote copies, remote signals or barrier semaphores. Data moves between devices by JAX's collectives and lax.ppermute only.
A program may use at most 128 MiB of HBM per device.

v0:
```python
import jax
import jax.numpy as jnp
from jax import lax
from jax.sharding import PartitionSpec as P

ITERS = 3
ANALYSES = 2
BATCHES = 4
RADIUS = 8
SPAN = 16


STEP_SIZE = 0.5
STORAGE_FLOOR = 0.5
LOWER_WEIGHT = 0.6
TOP_LEVEL = lax.Precision.HIGHEST


def extended(x, sides, width):
    for axis, dim in sides:
        peers, length = (lax.axis_size(axis), x.shape[dim])
        up = [(i, (i + 1) % peers) for i in range(peers - 1)]
        down = [(j, i) for i, j in up]
        last = lax.slice_in_dim(x, length - width, length, axis=dim)
        leading = lax.slice_in_dim(x, 0, width, axis=dim)
        before = lax.ppermute(last, axis, up)
        after = lax.ppermute(leading, axis, down)
        x = jnp.concatenate([before, x, after], axis=dim)
    return x


def advance(
    current,
    start,
    transmissivity_grid,
    interlayer_leakage_factor,
    specific_porosity_release,
    infiltration_inflow,
    around,
):
    lateral = transmissivity_grid[:, None] * (around - 4.0 * current)
    exchange_flow = interlayer_leakage_factor * (current[1] - current[0])
    vertical = jnp.stack([exchange_flow + infiltration_inflow, -exchange_flow])
    storage_term = specific_porosity_release * jax.nn.sigmoid(current) + STORAGE_FLOOR
    return start + STEP_SIZE * (lateral + vertical) / storage_term


def summed(padded):
    return (
        padded[:, :, 2:, 1:-1]
        + padded[:, :, :-2, 1:-1]
        + padded[:, :, 1:-1, 2:]
        + padded[:, :, 1:-1, :-2]
    )


def predicted_piezometric_ensemble(
    piezometric_elevation,
    transmissivity_grid,
    interlayer_leakage_factor,
    specific_porosity_release,
    infiltration_inflow,
):
    current = piezometric_elevation
    for step in range(ITERS):
        padded = extended(current, (("north", 2), ("east", 3)), 1)
        current = advance(
            current,
            piezometric_elevation,
            transmissivity_grid,
            interlayer_leakage_factor,
            specific_porosity_release,
            infiltration_inflow,
            summed(padded),
        )
    return current


def analyse(piezometric_elevation, value_entries, errors, spots, lives, colours):
    layer_stack, member_count, rows, cols = piezometric_elevation.shape
    lat_rows = rows // (2 * SPAN)
    lat_cols = cols // (2 * SPAN)
    north_at = lax.axis_index("north")
    east_at = lax.axis_index("east")
    margins = ((0, 0), (lat_rows, lat_rows), (lat_cols, lat_cols))
    anchor = jnp.zeros((), jnp.int32)

    def nearby(table, filler):
        padded = jnp.pad(table, margins, constant_values=filler)
        return lax.dynamic_slice(
            padded,
            (anchor, north_at * lat_rows, east_at * lat_cols),
            (BATCHES, 3 * lat_rows, 3 * lat_cols),
        )

    near_value = nearby(value_entries, 0.0)
    near_error = nearby(errors, 1.0)
    near_spot = nearby(spots, 0)
    near_live = nearby(lives, 0).astype(jnp.float32)
    lattice_row = jnp.arange(3 * lat_rows) - lat_rows
    lattice_col = jnp.arange(3 * lat_cols) - lat_cols
    row_index = jnp.arange(rows)
    col_index = jnp.arange(cols)
    reach = SPAN + 2 * RADIUS - 3
    layer_weight = jnp.array([1.0, LOWER_WEIGHT], jnp.float32).reshape(2, 1, 1, 1)
    for batch in range(BATCHES):
        colour = colours[batch]
        row_parity = colour // 2
        col_parity = colour % 2
        spot = near_spot[batch]
        row_base = (2 * lattice_row + row_parity) * SPAN
        col_base = (2 * lattice_col + col_parity) * SPAN
        pos_row = row_base[:, None] + spot // SPAN
        pos_col = col_base[None, :] + spot % SPAN
        own_row = pos_row[lat_rows : 2 * lat_rows, lat_cols : 2 * lat_cols]
        own_col = pos_col[lat_rows : 2 * lat_rows, lat_cols : 2 * lat_cols]
        priors = piezometric_elevation[0][:, own_row, own_col]
        package = priors.reshape(1, 1, member_count * lat_rows * lat_cols)
        near = extended(package, (("north", 0), ("east", 1)), 1)
        near = (
            near.reshape(3, 3, member_count, lat_rows, lat_cols)
            .transpose(2, 0, 3, 1, 4)
            .reshape(member_count, 3 * lat_rows, 3 * lat_cols)
        )
        prior_mean = jnp.mean(near, axis=0)
        prior_anomaly = near - prior_mean[None]
        spread = jnp.sum(prior_anomaly * prior_anomaly, axis=0) / (member_count - 1)
        noise = near_error[batch]
        gain = near_live[batch] / ((spread + noise) * (member_count - 1))
        shrink = 1.0 / (1.0 + jnp.sqrt(noise / (spread + noise)))
        row_start = row_base - (RADIUS - 1)
        col_start = col_base - (RADIUS - 1)
        row_selected = (
            (row_index[None, :] >= row_start[:, None])
            & (row_index[None, :] <= row_start[:, None] + reach)
        ).astype(jnp.float32)
        column_selected = (
            (col_index[None, :] >= col_start[:, None])
            & (col_index[None, :] <= col_start[:, None] + reach)
        ).astype(jnp.float32)

        def spread_out(table):
            return jnp.dot(
                jnp.dot(row_selected.T, table, precision=TOP_LEVEL),
                column_selected,
                precision=TOP_LEVEL,
            )

        cell_row = spread_out(pos_row.astype(jnp.float32))
        cell_col = spread_out(pos_col.astype(jnp.float32))
        cell_shift = spread_out(gain * (near_value[batch] - prior_mean))
        cell_scale = spread_out(shrink * gain)
        valid = jnp.sum(row_selected, axis=0)[:, None] * jnp.sum(column_selected, axis=0)[None, :]
        row_taper = jnp.maximum(
            0.0, 1.0 - jnp.abs(row_index.astype(jnp.float32)[:, None] - cell_row) / RADIUS
        )
        col_taper = jnp.maximum(
            0.0, 1.0 - jnp.abs(col_index.astype(jnp.float32)[None, :] - cell_col) / RADIUS
        )
        taper = row_taper * col_taper * valid
        box = (taper > 0.0).astype(jnp.float32)
        incomplete_rows = jnp.einsum(
            "on,uoy->uny", row_selected, prior_anomaly, precision=TOP_LEVEL
        )
        cell_anomaly = jnp.einsum(
            "adz,zq->adq", incomplete_rows, column_selected, precision=TOP_LEVEL
        )
        matched = cell_anomaly * box
        centre = jnp.mean(piezometric_elevation, axis=1, keepdims=True)
        deviation = piezometric_elevation - centre
        weight = jnp.sum(deviation * matched[None], axis=1, keepdims=True) * layer_weight * taper
        piezometric_elevation = (
            centre + weight * cell_shift + deviation - weight * cell_scale * cell_anomaly[None]
        )
    return piezometric_elevation


def shards(
    head_ensemble,
    transmissivity_grid,
    interlayer_leakage_factor,
    specific_porosity_release,
    infiltration_inflow,
    obs_value,
    obs_error,
    obs_spot,
    obs_live,
    batch_colour,
):
    piezometric_elevation = head_ensemble
    for analysis in range(ANALYSES):
        piezometric_elevation = predicted_piezometric_ensemble(
            piezometric_elevation,
            transmissivity_grid,
            interlayer_leakage_factor,
            specific_porosity_release,
            infiltration_inflow,
        )
        piezometric_elevation = analyse(
            piezometric_elevation,
            obs_value[analysis],
            obs_error[analysis],
            obs_spot[analysis],
            obs_live[analysis],
            batch_colour[analysis],
        )
    return piezometric_elevation


def solution(mesh):
    placed = (
        P(None, None, "north", "east"),
        P(None, "north", "east"),
        P("north", "east"),
        P("north", "east"),
        P("north", "east"),
        P(),
        P(),
        P(),
        P(),
        P(),
    )
    return jax.shard_map(
        shards,
        mesh=mesh,
        in_specs=placed,
        out_specs=P(None, None, "north", "east"),
        check_vma=False,
    )
```

profile of v0, /device:TPU:25, one launch (start us, length us, event | category | flops | bytes accessed | tf_op | source)
XLA Modules:
  0.0 537.6 jit_solution(1410409516232836185)
XLA Ops:
  0.0 4.0 copy.98
  5.0 7.7 %collective-permute-start = (f32[2,64,1,128]{1,3,2,0:T(8,128)S(1)}, f32[2,64,1,128]{1,3,2,0:T(8,128)S(1)}, u32[]{:S(2)}, u32[]{:S(2)}) collective-permute-start(f32[2,64,1,128]{1,3,2,0:T(8,128)S(1)} %get-tuple-element.88), channel_id=1, source_target_pairs={{8,0},{16,8},{24,16},{32,24},{40,32},{48,40},{56,48},{64,56},{72,6... | collective-permute-start | bytes 196616 | tf_op jit(solution)/shard_map/ppermute | solution.py:27
  48.5 4.0 broadcast_add_fusion.5
  59.4 2.9 collective-permute-start.2
  62.3 3.0 collective-permute-start.3
  66.3 9.5 %fusion.51 = f32[2,64,32,128]{1,3,2,0:T(8,128)S(1)} fusion(f32[2,64,32,128]{1,3,2,0:T(8,128)S(1)} %copy-done, f32[2,64,34,1]{1,3,2,0:T(1,128)S(1)} %collective-permute-done.3, f32[2,64,1,128]{1,3,2,0:T(8,128)S(1)} %collective-permute-done, f32[2,64,1,128]{1,3,2,0:T(8,128)S(1)} %collective-permute-done.1, f32[2,64,34,1]{1,3,2,0:T(1,128)S(1)} %collective-permute-done.2, ...), kind=kLoop, calls=%fused_computation.100 | loop fusion | flops 12582912 | bytes 6506496 | tf_op jit(solution)/shard_map/add | solution.py:45
  75.9 5.8 %collective-permute-start.4 = (f32[2,64,1,128]{1,3,2,0:T(8,128)S(1)}, f32[2,64,1,128]{1,3,2,0:T(8,128)S(1)}, u32[]{:S(2)}, u32[]{:S(2)}) collective-permute-start(f32[2,64,1,128]{1,3,2,0:T(8,128)S(1)} %get-tuple-element.86), channel_id=1, source_target_pairs={{8,0},{16,8},{24,16},{32,24},{40,32},{48,40},{56,48},{64,56},{72,6... | collective-permute-start | bytes 196616 | tf_op jit(solution)/shard_map/ppermute | solution.py:27
  84.6 6.5 %collective-permute-done.5 = f32[2,64,1,128]{1,3,2,0:T(8,128)S(1)} collective-permute-done((f32[2,64,1,128]{1,3,2,0:T(8,128)S(1)}, f32[2,64,1,128]{1,3,2,0:T(8,128)S(1)}, u32[]{:S(2)}, u32[]{:S(2)}) %collective-permute-start.5) | collective-permute-done | bytes 65568 | tf_op jit(solution)/shard_map/ppermute | solution.py:26
  93.4 3.7 collective-permute-start.7
  98.5 9.6 %fusion.42 = f32[2,64,32,128]{1,3,2,0:T(8,128)S(1)} fusion(f32[2,64,32,128]{1,3,2,0:T(8,128)S(1)} %copy-done, f32[2,64,34,1]{1,3,2,0:T(1,128)S(1)} %collective-permute-done.7, f32[2,64,1,128]{1,3,2,0:T(8,128)S(1)} %collective-permute-done.4, f32[2,64,32,128]{1,3,2,0:T(8,128)S(1)} %fusion.51, f32[2,64,1,128]{1,3,2,0:T(8,128)S(1)} %collective-permute-done.5, ...), kind=kLoop, calls=%fused_computation.83 | loop fusion | flops 12582912 | bytes 8603648 | tf_op jit(solution)/shard_map/add | solution.py:45
  110.0 3.4 collective-permute-start.9
  114.4 4.0 collective-permute-done.9
  120.5 4.5 collective-permute-start.11
  126.4 9.9 %fusion.451 = (f32[2,32,128]{2,1,0:T(8,128)S(1)}, f32[2,64,32,128]{1,3,2,0:T(8,128)S(1)}) fusion(f32[2,64,32,128]{1,3,2,0:T(8,128)S(1)} %copy-done, f32[2,64,32,128]{1,3,2,0:T(8,128)S(1)} %fusion.42, f32[32,128]{1,0:T(8,128)S(1)} %copy-done.26, f32[1,64,32,128]{1,3,2,0:T(8,128)S(1)} %get-tuple-element.72, f32[1,64,32,128]{1,3,2,0:T(8,128)S(1)} %get-tuple-element.71, ...), kind=kLoop, calls=%fused_computation.895 | loop fusion | flops 13099008 | bytes 8636416 | tf_op jit(solution)/shard_map/reduce_sum | solution.py:169
  141.9 5.5 %collective-permute-start.13 = (f32[1,1,256]{2,1,0:T(1,128)S(1)}, f32[1,1,256]{2,1,0:T(1,128)S(1)}, u32[]{:S(2)}, u32[]{:S(2)}) collective-permute-start(f32[1,1,256]{2,1,0:T(1,128)S(1)} %reshape.693), channel_id=1, source_target_pairs={{8,0},{16,8},{24,16},{32,24},{40,32},{48,40},{56,48},{64,56},{72,6... | collective-permute-start | bytes 3080 | tf_op jit(solution)/shard_map/ppermute | solution.py:27
  148.1 4.9 collective-permute-start.14
  161.6 2.8 broadcast_multiply_fusion.7
  168.3 4.2 multiply_reduce_fusion.7
  172.6 5.2 fusion.449
  183.4 6.0 %collective-permute-start.17 = (f32[1,1,256]{2,1,0:T(1,128)S(1)}, f32[1,1,256]{2,1,0:T(1,128)S(1)}, u32[]{:S(2)}, u32[]{:S(2)}) collective-permute-start(f32[1,1,256]{2,1,0:T(1,128)S(1)} %reshape.696), channel_id=1, source_target_pairs={{8,0},{16,8},{24,16},{32,24},{40,32},{48,40},{56,48},{64,56},{72,6... | collective-permute-start | bytes 3080 | tf_op jit(solution)/shard_map/ppermute | solution.py:27
  190.1 2.8 collective-permute-start.18
  194.8 3.0 collective-permute-done.19
  207.4 4.2 multiply_reduce_fusion.6
  211.8 5.2 fusion.447
  222.5 6.0 %collective-permute-start.21 = (f32[1,1,256]{2,1,0:T(1,128)S(1)}, f32[1,1,256]{2,1,0:T(1,128)S(1)}, u32[]{:S(2)}, u32[]{:S(2)}) collective-permute-start(f32[1,1,256]{2,1,0:T(1,128)S(1)} %reshape.699), channel_id=1, source_target_pairs={{8,0},{16,8},{24,16},{32,24},{40,32},{48,40},{56,48},{64,56},{72,6... | collective-permute-start | bytes 3080 | tf_op jit(solution)/shard_map/ppermute | solution.py:27
  229.2 2.8 collective-permute-start.22
  247.3 4.2 multiply_reduce_fusion.5
  251.6 5.2 fusion.445
  262.3 6.0 %collective-permute-start.25 = (f32[1,1,256]{2,1,0:T(1,128)S(1)}, f32[1,1,256]{2,1,0:T(1,128)S(1)}, u32[]{:S(2)}, u32[]{:S(2)}) collective-permute-start(f32[1,1,256]{2,1,0:T(1,128)S(1)} %reshape.702), channel_id=1, source_target_pairs={{8,0},{16,8},{24,16},{32,24},{40,32},{48,40},{56,48},{64,56},{72,6... | collective-permute-start | bytes 3080 | tf_op jit(solution)/shard_map/ppermute | solution.py:27
  269.0 2.8 collective-permute-start.26
  273.8 3.0 collective-permute-done.27
  284.9 4.5 multiply_reduce_fusion.4
  289.6 3.9 multiply_subtract_fusion.4
  293.5 6.0 %collective-permute-start.28 = (f32[2,64,1,128]{1,3,2,0:T(8,128)S(1)}, f32[2,64,1,128]{1,3,2,0:T(8,128)S(1)}, u32[]{:S(2)}, u32[]{:S(2)}) collective-permute-start(f32[2,64,1,128]{1,3,2,0:T(8,128)S(1)} %get-tuple-element.82), channel_id=1, source_target_pairs={{8,0},{16,8},{24,16},{32,24},{40,32},{48,40},{56,48},{64,56},{72,6... | collective-permute-start | bytes 196616 | tf_op jit(solution)/shard_map/ppermute | solution.py:27
  301.4 6.2 %collective-permute-done.29 = f32[2,64,1,128]{1,3,2,0:T(8,128)S(1)} collective-permute-done((f32[2,64,1,128]{1,3,2,0:T(8,128)S(1)}, f32[2,64,1,128]{1,3,2,0:T(8,128)S(1)}, u32[]{:S(2)}, u32[]{:S(2)}) %collective-permute-start.29) | collective-permute-done | bytes 65568 | tf_op jit(solution)/shard_map/ppermute | solution.py:26
  309.6 4.5 collective-permute-start.31
  315.5 9.3 %fusion.24 = f32[2,64,32,128]{1,3,2,0:T(8,128)S(1)} fusion(f32[2,64,32,128]{1,3,2,0:T(8,128)S(1)} %multiply_subtract_fusion.4, f32[2,64,34,1]{1,3,2,0:T(1,128)S(1)} %collective-permute-done.31, f32[2,64,1,128]{1,3,2,0:T(8,128)S(1)} %collective-permute-done.28, f32[2,64,1,128]{1,3,2,0:T(8,128)S(1)} %collective-permute-done.29, ...), kind=kLoop, calls=%fused_computation.49 | loop fusion | flops 12582912 | bytes 6506496 | tf_op jit(solution)/shard_map/add | solution.py:45
  326.8 3.4 collective-permute-start.33
  330.6 4.0 collective-permute-done.33
  336.6 5.3 collective-permute-start.35
  343.4 10.2 %fusion.15 = f32[2,64,32,128]{1,3,2,0:T(8,128)S(1)} fusion(f32[2,64,34,1]{1,3,2,0:T(1,128)S(1)} %collective-permute-done.35, f32[2,64,1,128]{1,3,2,0:T(8,128)S(1)} %collective-permute-done.32, f32[2,64,32,128]{1,3,2,0:T(8,128)S(1)} %fusion.24, f32[2,64,1,128]{1,3,2,0:T(8,128)S(1)} %collective-permute-done.33, ...), kind=kLoop, calls=%fused_computation.32 | loop fusion | flops 14680064 | bytes 9750528 | tf_op jit(solution)/shard_map/add | solution.py:45
  355.6 3.4 collective-permute-start.37
  359.4 4.0 collective-permute-done.37
  365.4 5.1 collective-permute-start.39
  371.9 11.2 %fusion.442 = (f32[2,32,128]{2,1,0:T(8,128)S(1)}, f32[2,64,32,128]{1,3,2,0:T(8,128)S(1)}) fusion(f32[2,64,32,128]{1,3,2,0:T(8,128)S(1)} %fusion.15, f32[32,128]{1,0:T(8,128)S(1)} %copy-done.26, f32[1,64,32,128]{1,3,2,0:T(8,128)S(1)} %get-tuple-element.66, f32[1,64,32,128]{1,3,2,0:T(8,128)S(1)} %get-tuple-element.65, ...), kind=kLoop, calls=%fused_computation.891 | loop fusion | flops 15196160 | bytes 9783296 | tf_op jit(solution)/shard_map/reduce_sum | solution.py:169
  388.1 5.5 %collective-permute-start.41 = (f32[1,1,256]{2,1,0:T(1,128)S(1)}, f32[1,1,256]{2,1,0:T(1,128)S(1)}, u32[]{:S(2)}, u32[]{:S(2)}) collective-permute-start(f32[1,1,256]{2,1,0:T(1,128)S(1)} %reshape.705), channel_id=1, source_target_pairs={{8,0},{16,8},{24,16},{32,24},{40,32},{48,40},{56,48},{64,56},{72,6... | collective-permute-start | bytes 3080 | tf_op jit(solution)/shard_map/ppermute | solution.py:27
  394.3 4.9 collective-permute-start.42
  401.2 3.0 collective-permute-done.43
  412.6 4.2 multiply_reduce_fusion.3
  416.9 5.2 fusion.440
  427.0 6.0 %collective-permute-start.45 = (f32[1,1,256]{2,1,0:T(1,128)S(1)}, f32[1,1,256]{2,1,0:T(1,128)S(1)}, u32[]{:S(2)}, u32[]{:S(2)}) collective-permute-start(f32[1,1,256]{2,1,0:T(1,128)S(1)} %reshape.708), channel_id=1, source_target_pairs={{8,0},{16,8},{24,16},{32,24},{40,32},{48,40},{56,48},{64,56},{72,6... | collective-permute-start | bytes 3080 | tf_op jit(solution)/shard_map/ppermute | solution.py:27
  433.8 2.8 collective-permute-start.46
  449.9 4.2 multiply_reduce_fusion.2
  454.2 5.2 fusion.438
  464.5 6.0 %collective-permute-start.49 = (f32[1,1,256]{2,1,0:T(1,128)S(1)}, f32[1,1,256]{2,1,0:T(1,128)S(1)}, u32[]{:S(2)}, u32[]{:S(2)}) collective-permute-start(f32[1,1,256]{2,1,0:T(1,128)S(1)} %reshape.711), channel_id=1, source_target_pairs={{8,0},{16,8},{24,16},{32,24},{40,32},{48,40},{56,48},{64,56},{72,6... | collective-permute-start | bytes 3080 | tf_op jit(solution)/shard_map/ppermute | solution.py:27
  471.2 2.8 collective-permute-start.50
  475.9 3.0 collective-permute-done.51
  487.3 4.2 multiply_reduce_fusion.1
  491.6 5.2 fusion.436
  502.1 6.0 %collective-permute-start.53 = (f32[1,1,256]{2,1,0:T(1,128)S(1)}, f32[1,1,256]{2,1,0:T(1,128)S(1)}, u32[]{:S(2)}, u32[]{:S(2)}) collective-permute-start(f32[1,1,256]{2,1,0:T(1,128)S(1)} %reshape.714), channel_id=1, source_target_pairs={{8,0},{16,8},{24,16},{32,24},{40,32},{48,40},{56,48},{64,56},{72,6... | collective-permute-start | bytes 3080 | tf_op jit(solution)/shard_map/ppermute | solution.py:27
  508.8 2.8 collective-permute-start.54
  522.8 4.5 multiply_reduce_fusion
  527.3 5.7 %multiply_subtract_fusion = f32[2,64,32,128]{1,3,2,0:T(8,128)} fusion(f32[2,64,32,128]{1,3,2,0:T(8,128)S(1)} %copy-done.4, f32[64,32,128]{0,2,1:T(8,128)S(1)} %copy.146, f32[2,32,128]{2,1,0:T(8,128)S(1)} %get-tuple-element.110, f32[2,32,128]{2,1,0:T(8,128)S(1)} %get-tuple-element.109, f32[2,32,128]{2,1,0:T(8,128)S(1)} %broadcast_multiply_fusion.8), kind=kLoop, calls=%fused_computation.110 | loop fusion | flops 2097152 | bytes 5341184 | tf_op jit(solution)/shard_map/sub | solution.py:173
  533.0 4.2 copy.147
  (695 shorter events, 196.0 us)
Async XLA Ops:
  0.0 45.6 %copy-start.30 = (s32[2,4,32,32]{3,2,1,0:T(8,128)S(1)}, s32[2,4,32,32]{3,2,1,0:T(8,128)}, u32[]{:S(2)}) copy-start(s32[2,4,32,32]{3,2,1,0:T(8,128)} %param.20) | copy-start | bytes 98308
  0.0 48.4 %copy-start.25 = (f32[32,128]{1,0:T(8,128)S(1)}, f32[32,128]{1,0:T(8,128)}, u32[]{:S(2)}) copy-start(f32[32,128]{1,0:T(8,128)} %param.14) | copy-start | bytes 49156
  0.0 48.4 %copy-start.24 = (f32[32,128]{1,0:T(8,128)S(1)}, f32[32,128]{1,0:T(8,128)}, u32[]{:S(2)}) copy-start(f32[32,128]{1,0:T(8,128)} %param.16) | copy-start | bytes 49156
  5.0 54.3 %collective-permute-start = (f32[2,64,1,128]{1,3,2,0:T(8,128)S(1)}, f32[2,64,1,128]{1,3,2,0:T(8,128)S(1)}, u32[]{:S(2)}, u32[]{:S(2)}) collective-permute-start(f32[2,64,1,128]{1,3,2,0:T(8,128)S(1)} %get-tuple-element.88), channel_id=1, source_target_pairs={{8,0},{16,8},{24,16},{32,24},{40,32},{48,40},{56,48},{64,56},{72,6... | collective-permute-start | bytes 196616 | tf_op jit(solution)/shard_map/ppermute | solution.py:27
  12.6 46.7 %collective-permute-start.1 = (f32[2,64,1,128]{1,3,2,0:T(8,128)S(1)}, f32[2,64,1,128]{1,3,2,0:T(8,128)S(1)}, u32[]{:S(2)}, u32[]{:S(2)}) collective-permute-start(f32[2,64,1,128]{1,3,2,0:T(8,128)S(1)} %get-tuple-element.87), channel_id=1, source_target_pairs={{0,8},{8,16},{16,24},{24,32},{32,40},{40,48},{48,56},{56,64},{64,7... | collective-permute-start | bytes 196616 | tf_op jit(solution)/shard_map/ppermute | solution.py:26
  24.9 135.0 %copy-start.115 = (s32[12]{0:T(128)}, s32[12]{0:T(128)S(1)}, u32[]{:S(2)}) copy-start(s32[12]{0:T(128)S(1)} %get-tuple-element.209) | copy-start | bytes 148
  24.9 135.0 %copy-start.116 = (s32[12]{0:T(128)}, s32[12]{0:T(128)S(1)}, u32[]{:S(2)}) copy-start(s32[12]{0:T(128)S(1)} %get-tuple-element.210) | copy-start | bytes 148
  24.9 33.5 %copy-start.122 = (f32[128]{0:T(128)}, f32[128]{0:T(128)S(1)}, u32[]{:S(2)}) copy-start(f32[128]{0:T(128)S(1)} %iota_convert_fusion) | copy-start | bytes 1540
  26.6 29.3 %copy-start.103 = (s32[12]{0:T(128)}, s32[12]{0:T(128)S(1)}, u32[]{:S(2)}) copy-start(s32[12]{0:T(128)S(1)} %get-tuple-element.213) | copy-start | bytes 148
  26.6 29.3 %copy-start.105 = (s32[12]{0:T(128)}, s32[12]{0:T(128)S(1)}, u32[]{:S(2)}) copy-start(s32[12]{0:T(128)S(1)} %get-tuple-element.214) | copy-start | bytes 148
  59.4 6.5 %collective-permute-start.2 = (f32[2,64,34,1]{1,3,2,0:T(1,128)S(1)}, f32[2,64,34,1]{1,3,2,0:T(1,128)S(1)}, u32[]{:S(2)}, u32[]{:S(2)}) collective-permute-start(f32[2,64,34,1]{1,3,2,0:T(1,128)S(1)} %get-tuple-element.63), channel_id=1, source_target_pairs={{1,0},{2,1},{3,2},{4,3},{5,4},{6,5},{7,6},{9,8},{10,9},{11,10},{12... | collective-permute-start | bytes 52232 | tf_op jit(solution)/shard_map/ppermute | solution.py:27
  62.3 4.0 collective-permute-start.3
  75.9 8.7 %collective-permute-start.4 = (f32[2,64,1,128]{1,3,2,0:T(8,128)S(1)}, f32[2,64,1,128]{1,3,2,0:T(8,128)S(1)}, u32[]{:S(2)}, u32[]{:S(2)}) collective-permute-start(f32[2,64,1,128]{1,3,2,0:T(8,128)S(1)} %get-tuple-element.86), channel_id=1, source_target_pairs={{8,0},{16,8},{24,16},{32,24},{40,32},{48,40},{56,48},{64,56},{72,6... | collective-permute-start | bytes 196616 | tf_op jit(solution)/shard_map/ppermute | solution.py:27
  81.6 9.4 %collective-permute-start.5 = (f32[2,64,1,128]{1,3,2,0:T(8,128)S(1)}, f32[2,64,1,128]{1,3,2,0:T(8,128)S(1)}, u32[]{:S(2)}, u32[]{:S(2)}) collective-permute-start(f32[2,64,1,128]{1,3,2,0:T(8,128)S(1)} %get-tuple-element.85), channel_id=1, source_target_pairs={{0,8},{8,16},{16,24},{24,32},{32,40},{40,48},{48,56},{56,64},{64,7... | collective-permute-start | bytes 196616 | tf_op jit(solution)/shard_map/ppermute | solution.py:26
  91.1 7.4 %collective-permute-start.6 = (f32[2,64,34,1]{1,3,2,0:T(1,128)S(1)}, f32[2,64,34,1]{1,3,2,0:T(1,128)S(1)}, u32[]{:S(2)}, u32[]{:S(2)}) collective-permute-start(f32[2,64,34,1]{1,3,2,0:T(1,128)S(1)} %get-tuple-element.61), channel_id=1, source_target_pairs={{1,0},{2,1},{3,2},{4,3},{5,4},{6,5},{7,6},{9,8},{10,9},{11,10},{12... | collective-permute-start | bytes 52232 | tf_op jit(solution)/shard_map/ppermute | solution.py:27
  93.4 5.1 collective-permute-start.7
  108.1 6.3 %collective-permute-start.8 = (f32[2,64,1,128]{1,3,2,0:T(8,128)S(1)}, f32[2,64,1,128]{1,3,2,0:T(8,128)S(1)}, u32[]{:S(2)}, u32[]{:S(2)}) collective-permute-start(f32[2,64,1,128]{1,3,2,0:T(8,128)S(1)} %get-tuple-element.84), channel_id=1, source_target_pairs={{8,0},{16,8},{24,16},{32,24},{40,32},{48,40},{56,48},{64,56},{72,6... | collective-permute-start | bytes 196616 | tf_op jit(solution)/shard_map/ppermute | solution.py:27
  110.0 8.4 %collective-permute-start.9 = (f32[2,64,1,128]{1,3,2,0:T(8,128)S(1)}, f32[2,64,1,128]{1,3,2,0:T(8,128)S(1)}, u32[]{:S(2)}, u32[]{:S(2)}) collective-permute-start(f32[2,64,1,128]{1,3,2,0:T(8,128)S(1)} %get-tuple-element.83), channel_id=1, source_target_pairs={{0,8},{8,16},{16,24},{24,32},{32,40},{40,48},{48,56},{56,64},{64,7... | collective-permute-start | bytes 196616 | tf_op jit(solution)/shard_map/ppermute | solution.py:26
  118.5 7.8 %collective-permute-start.10 = (f32[2,64,34,1]{1,3,2,0:T(1,128)S(1)}, f32[2,64,34,1]{1,3,2,0:T(1,128)S(1)}, u32[]{:S(2)}, u32[]{:S(2)}) collective-permute-start(f32[2,64,34,1]{1,3,2,0:T(1,128)S(1)} %get-tuple-element.59), channel_id=1, source_target_pairs={{1,0},{2,1},{3,2},{4,3},{5,4},{6,5},{7,6},{9,8},{10,9},{11,10},{12... | collective-permute-start | bytes 52232 | tf_op jit(solution)/shard_map/ppermute | solution.py:27
  120.5 5.9 %collective-permute-start.11 = (f32[2,64,34,1]{1,3,2,0:T(1,128)S(1)}, f32[2,64,34,1]{1,3,2,0:T(1,128)S(1)}, u32[]{:S(2)}, u32[]{:S(2)}) collective-permute-start(f32[2,64,34,1]{1,3,2,0:T(1,128)S(1)} %get-tuple-element.60), channel_id=1, source_target_pairs={{0,1},{1,2},{2,3},{3,4},{4,5},{5,6},{6,7},{8,9},{9,10},{10,11},{11... | collective-permute-start | bytes 52232 | tf_op jit(solution)/shard_map/ppermute | solution.py:26
  139.3 8.1 %collective-permute-start.12 = (f32[1,1,256]{2,1,0:T(1,128)S(1)}, f32[1,1,256]{2,1,0:T(1,128)S(1)}, u32[]{:S(2)}, u32[]{:S(2)}) collective-permute-start(f32[1,1,256]{2,1,0:T(1,128)S(1)} %reshape.693), channel_id=1, source_target_pairs={{0,8},{8,16},{16,24},{24,32},{32,40},{40,48},{48,56},{56,64},{64,7... | collective-permute-start | bytes 3080 | tf_op jit(solution)/shard_map/ppermute | solution.py:26
  141.9 6.2 %collective-permute-start.13 = (f32[1,1,256]{2,1,0:T(1,128)S(1)}, f32[1,1,256]{2,1,0:T(1,128)S(1)}, u32[]{:S(2)}, u32[]{:S(2)}) collective-permute-start(f32[1,1,256]{2,1,0:T(1,128)S(1)} %reshape.693), channel_id=1, source_target_pairs={{8,0},{16,8},{24,16},{32,24},{40,32},{48,40},{56,48},{64,56},{72,6... | collective-permute-start | bytes 3080 | tf_op jit(solution)/shard_map/ppermute | solution.py:27
  148.1 7.1 %collective-permute-start.14 = (f32[3,1,256]{2,1,0:T(1,128)S(1)}, f32[3,1,256]{2,1,0:T(1,128)S(1)}, u32[]{:S(2)}, u32[]{:S(2)}) collective-permute-start(f32[3,1,256]{2,1,0:T(1,128)S(1)} %constant_dynamic-update-slice_fusion), channel_id=1, source_target_pairs={{0,1},{1,2},{2,3},{3,4},{4,5},{5,6},{6,7},{8,9},{9,10},{10,11},{11... | collective-permute-start | bytes 9224 | tf_op jit(solution)/shard_map/ppermute | solution.py:26
  153.0 4.9 collective-permute-start.15
  180.8 8.5 %collective-permute-start.16 = (f32[1,1,256]{2,1,0:T(1,128)S(1)}, f32[1,1,256]{2,1,0:T(1,128)S(1)}, u32[]{:S(2)}, u32[]{:S(2)}) collective-permute-start(f32[1,1,256]{2,1,0:T(1,128)S(1)} %reshape.696), channel_id=1, source_target_pairs={{0,8},{8,16},{16,24},{24,32},{32,40},{40,48},{48,56},{56,64},{64,7... | collective-permute-start | bytes 3080 | tf_op jit(solution)/shard_map/ppermute | solution.py:26
  183.4 6.7 %collective-permute-start.17 = (f32[1,1,256]{2,1,0:T(1,128)S(1)}, f32[1,1,256]{2,1,0:T(1,128)S(1)}, u32[]{:S(2)}, u32[]{:S(2)}) collective-permute-start(f32[1,1,256]{2,1,0:T(1,128)S(1)} %reshape.696), channel_id=1, source_target_pairs={{8,0},{16,8},{24,16},{32,24},{40,32},{48,40},{56,48},{64,56},{72,6... | collective-permute-start | bytes 3080 | tf_op jit(solution)/shard_map/ppermute | solution.py:27
  190.1 4.7 collective-permute-start.18
  192.9 4.9 collective-permute-start.19
  220.0 8.5 %collective-permute-start.20 = (f32[1,1,256]{2,1,0:T(1,128)S(1)}, f32[1,1,256]{2,1,0:T(1,128)S(1)}, u32[]{:S(2)}, u32[]{:S(2)}) collective-permute-start(f32[1,1,256]{2,1,0:T(1,128)S(1)} %reshape.699), channel_id=1, source_target_pairs={{0,8},{8,16},{16,24},{24,32},{32,40},{40,48},{48,56},{56,64},{64,7... | collective-permute-start | bytes 3080 | tf_op jit(solution)/shard_map/ppermute | solution.py:26
  222.5 6.7 %collective-permute-start.21 = (f32[1,1,256]{2,1,0:T(1,128)S(1)}, f32[1,1,256]{2,1,0:T(1,128)S(1)}, u32[]{:S(2)}, u32[]{:S(2)}) collective-permute-start(f32[1,1,256]{2,1,0:T(1,128)S(1)} %reshape.699), channel_id=1, source_target_pairs={{8,0},{16,8},{24,16},{32,24},{40,32},{48,40},{56,48},{64,56},{72,6... | collective-permute-start | bytes 3080 | tf_op jit(solution)/shard_map/ppermute | solution.py:27
  229.2 5.2 collective-permute-start.22
  232.0 4.9 collective-permute-start.23
  259.8 8.5 %collective-permute-start.24 = (f32[1,1,256]{2,1,0:T(1,128)S(1)}, f32[1,1,256]{2,1,0:T(1,128)S(1)}, u32[]{:S(2)}, u32[]{:S(2)}) collective-permute-start(f32[1,1,256]{2,1,0:T(1,128)S(1)} %reshape.702), channel_id=1, source_target_pairs={{0,8},{8,16},{16,24},{24,32},{32,40},{40,48},{48,56},{56,64},{64,7... | collective-permute-start | bytes 3080 | tf_op jit(solution)/shard_map/ppermute | solution.py:26
  262.3 6.7 %collective-permute-start.25 = (f32[1,1,256]{2,1,0:T(1,128)S(1)}, f32[1,1,256]{2,1,0:T(1,128)S(1)}, u32[]{:S(2)}, u32[]{:S(2)}) collective-permute-start(f32[1,1,256]{2,1,0:T(1,128)S(1)} %reshape.702), channel_id=1, source_target_pairs={{8,0},{16,8},{24,16},{32,24},{40,32},{48,40},{56,48},{64,56},{72,6... | collective-permute-start | bytes 3080 | tf_op jit(solution)/shard_map/ppermute | solution.py:27
  269.0 4.7 collective-permute-start.26
  271.8 4.9 collective-permute-start.27
  293.5 8.0 %collective-permute-start.28 = (f32[2,64,1,128]{1,3,2,0:T(8,128)S(1)}, f32[2,64,1,128]{1,3,2,0:T(8,128)S(1)}, u32[]{:S(2)}, u32[]{:S(2)}) collective-permute-start(f32[2,64,1,128]{1,3,2,0:T(8,128)S(1)} %get-tuple-element.82), channel_id=1, source_target_pairs={{8,0},{16,8},{24,16},{32,24},{40,32},{48,40},{56,48},{64,56},{72,6... | collective-permute-start | bytes 196616 | tf_op jit(solution)/shard_map/ppermute | solution.py:27
  299.5 8.1 %collective-permute-start.29 = (f32[2,64,1,128]{1,3,2,0:T(8,128)S(1)}, f32[2,64,1,128]{1,3,2,0:T(8,128)S(1)}, u32[]{:S(2)}, u32[]{:S(2)}) collective-permute-start(f32[2,64,1,128]{1,3,2,0:T(8,128)S(1)} %get-tuple-element.81), channel_id=1, source_target_pairs={{0,8},{8,16},{16,24},{24,32},{32,40},{40,48},{48,56},{56,64},{64,7... | collective-permute-start | bytes 196616 | tf_op jit(solution)/shard_map/ppermute | solution.py:26
  307.7 7.8 %collective-permute-start.30 = (f32[2,64,34,1]{1,3,2,0:T(1,128)S(1)}, f32[2,64,34,1]{1,3,2,0:T(1,128)S(1)}, u32[]{:S(2)}, u32[]{:S(2)}) collective-permute-start(f32[2,64,34,1]{1,3,2,0:T(1,128)S(1)} %get-tuple-element.57), channel_id=1, source_target_pairs={{1,0},{2,1},{3,2},{4,3},{5,4},{6,5},{7,6},{9,8},{10,9},{11,10},{12... | collective-permute-start | bytes 52232 | tf_op jit(solution)/shard_map/ppermute | solution.py:27
  309.6 5.9 %collective-permute-start.31 = (f32[2,64,34,1]{1,3,2,0:T(1,128)S(1)}, f32[2,64,34,1]{1,3,2,0:T(1,128)S(1)}, u32[]{:S(2)}, u32[]{:S(2)}) collective-permute-start(f32[2,64,34,1]{1,3,2,0:T(1,128)S(1)} %get-tuple-element.58), channel_id=1, source_target_pairs={{0,1},{1,2},{2,3},{3,4},{4,5},{5,6},{6,7},{8,9},{9,10},{10,11},{11... | collective-permute-start | bytes 52232 | tf_op jit(solution)/shard_map/ppermute | solution.py:26
  324.9 5.7 %collective-permute-start.32 = (f32[2,64,1,128]{1,3,2,0:T(8,128)S(1)}, f32[2,64,1,128]{1,3,2,0:T(8,128)S(1)}, u32[]{:S(2)}, u32[]{:S(2)}) collective-permute-start(f32[2,64,1,128]{1,3,2,0:T(8,128)S(1)} %get-tuple-element.80), channel_id=1, source_target_pairs={{8,0},{16,8},{24,16},{32,24},{40,32},{48,40},{56,48},{64,56},{72,6... | collective-permute-start | bytes 196616 | tf_op jit(solution)/shard_map/ppermute | solution.py:27
  326.8 7.8 %collective-permute-start.33 = (f32[2,64,1,128]{1,3,2,0:T(8,128)S(1)}, f32[2,64,1,128]{1,3,2,0:T(8,128)S(1)}, u32[]{:S(2)}, u32[]{:S(2)}) collective-permute-start(f32[2,64,1,128]{1,3,2,0:T(8,128)S(1)} %get-tuple-element.79), channel_id=1, source_target_pairs={{0,8},{8,16},{16,24},{24,32},{32,40},{40,48},{48,56},{56,64},{64,7... | collective-permute-start | bytes 196616 | tf_op jit(solution)/shard_map/ppermute | solution.py:26
  334.7 8.7 %collective-permute-start.34 = (f32[2,64,34,1]{1,3,2,0:T(1,128)S(1)}, f32[2,64,34,1]{1,3,2,0:T(1,128)S(1)}, u32[]{:S(2)}, u32[]{:S(2)}) collective-permute-start(f32[2,64,34,1]{1,3,2,0:T(1,128)S(1)} %get-tuple-element.55), channel_id=1, source_target_pairs={{1,0},{2,1},{3,2},{4,3},{5,4},{6,5},{7,6},{9,8},{10,9},{11,10},{12... | collective-permute-start | bytes 52232 | tf_op jit(solution)/shard_map/ppermute | solution.py:27
  336.6 6.8 %collective-permute-start.35 = (f32[2,64,34,1]{1,3,2,0:T(1,128)S(1)}, f32[2,64,34,1]{1,3,2,0:T(1,128)S(1)}, u32[]{:S(2)}, u32[]{:S(2)}) collective-permute-start(f32[2,64,34,1]{1,3,2,0:T(1,128)S(1)} %get-tuple-element.56), channel_id=1, source_target_pairs={{0,1},{1,2},{2,3},{3,4},{4,5},{5,6},{6,7},{8,9},{9,10},{10,11},{11... | collective-permute-start | bytes 52232 | tf_op jit(solution)/shard_map/ppermute | solution.py:26
  353.7 5.7 %collective-permute-start.36 = (f32[2,64,1,128]{1,3,2,0:T(8,128)S(1)}, f32[2,64,1,128]{1,3,2,0:T(8,128)S(1)}, u32[]{:S(2)}, u32[]{:S(2)}) collective-permute-start(f32[2,64,1,128]{1,3,2,0:T(8,128)S(1)} %get-tuple-element.78), channel_id=1, source_target_pairs={{8,0},{16,8},{24,16},{32,24},{40,32},{48,40},{56,48},{64,56},{72,6... | collective-permute-start | bytes 196616 | tf_op jit(solution)/shard_map/ppermute | solution.py:27
  355.6 7.8 %collective-permute-start.37 = (f32[2,64,1,128]{1,3,2,0:T(8,128)S(1)}, f32[2,64,1,128]{1,3,2,0:T(8,128)S(1)}, u32[]{:S(2)}, u32[]{:S(2)}) collective-permute-start(f32[2,64,1,128]{1,3,2,0:T(8,128)S(1)} %get-tuple-element.77), channel_id=1, source_target_pairs={{0,8},{8,16},{16,24},{24,32},{32,40},{40,48},{48,56},{56,64},{64,7... | collective-permute-start | bytes 196616 | tf_op jit(solution)/shard_map/ppermute | solution.py:26
  363.5 8.4 %collective-permute-start.38 = (f32[2,64,34,1]{1,3,2,0:T(1,128)S(1)}, f32[2,64,34,1]{1,3,2,0:T(1,128)S(1)}, u32[]{:S(2)}, u32[]{:S(2)}) collective-permute-start(f32[2,64,34,1]{1,3,2,0:T(1,128)S(1)} %get-tuple-element.53), channel_id=1, source_target_pairs={{1,0},{2,1},{3,2},{4,3},{5,4},{6,5},{7,6},{9,8},{10,9},{11,10},{12... | collective-permute-start | bytes 52232 | tf_op jit(solution)/shard_map/ppermute | solution.py:27
  365.4 6.5 %collective-permute-start.39 = (f32[2,64,34,1]{1,3,2,0:T(1,128)S(1)}, f32[2,64,34,1]{1,3,2,0:T(1,128)S(1)}, u32[]{:S(2)}, u32[]{:S(2)}) collective-permute-start(f32[2,64,34,1]{1,3,2,0:T(1,128)S(1)} %get-tuple-element.54), channel_id=1, source_target_pairs={{0,1},{1,2},{2,3},{3,4},{4,5},{5,6},{6,7},{8,9},{9,10},{10,11},{11... | collective-permute-start | bytes 52232 | tf_op jit(solution)/shard_map/ppermute | solution.py:26
  386.1 7.4 %collective-permute-start.40 = (f32[1,1,256]{2,1,0:T(1,128)S(1)}, f32[1,1,256]{2,1,0:T(1,128)S(1)}, u32[]{:S(2)}, u32[]{:S(2)}) collective-permute-start(f32[1,1,256]{2,1,0:T(1,128)S(1)} %reshape.705), channel_id=1, source_target_pairs={{0,8},{8,16},{16,24},{24,32},{32,40},{40,48},{48,56},{56,64},{64,7... | collective-permute-start | bytes 3080 | tf_op jit(solution)/shard_map/ppermute | solution.py:26
  388.1 6.2 %collective-permute-start.41 = (f32[1,1,256]{2,1,0:T(1,128)S(1)}, f32[1,1,256]{2,1,0:T(1,128)S(1)}, u32[]{:S(2)}, u32[]{:S(2)}) collective-permute-start(f32[1,1,256]{2,1,0:T(1,128)S(1)} %reshape.705), channel_id=1, source_target_pairs={{8,0},{16,8},{24,16},{32,24},{40,32},{48,40},{56,48},{64,56},{72,6... | collective-permute-start | bytes 3080 | tf_op jit(solution)/shard_map/ppermute | solution.py:27
  394.3 6.9 %collective-permute-start.42 = (f32[3,1,256]{2,1,0:T(1,128)S(1)}, f32[3,1,256]{2,1,0:T(1,128)S(1)}, u32[]{:S(2)}, u32[]{:S(2)}) collective-permute-start(f32[3,1,256]{2,1,0:T(1,128)S(1)} %constant_dynamic-update-slice_fusion.12), channel_id=1, source_target_pairs={{0,1},{1,2},{2,3},{3,4},{4,5},{5,6},{6,7},{8,9},{9,10},{10,11},{11... | collective-permute-start | bytes 9224 | tf_op jit(solution)/shard_map/ppermute | solution.py:26
  399.2 4.9 collective-permute-start.43
  425.1 8.0 %collective-permute-start.44 = (f32[1,1,256]{2,1,0:T(1,128)S(1)}, f32[1,1,256]{2,1,0:T(1,128)S(1)}, u32[]{:S(2)}, u32[]{:S(2)}) collective-permute-start(f32[1,1,256]{2,1,0:T(1,128)S(1)} %reshape.708), channel_id=1, source_target_pairs={{0,8},{8,16},{16,24},{24,32},{32,40},{40,48},{48,56},{56,64},{64,7... | collective-permute-start | bytes 3080 | tf_op jit(solution)/shard_map/ppermute | solution.py:26
  427.0 6.7 %collective-permute-start.45 = (f32[1,1,256]{2,1,0:T(1,128)S(1)}, f32[1,1,256]{2,1,0:T(1,128)S(1)}, u32[]{:S(2)}, u32[]{:S(2)}) collective-permute-start(f32[1,1,256]{2,1,0:T(1,128)S(1)} %reshape.708), channel_id=1, source_target_pairs={{8,0},{16,8},{24,16},{32,24},{40,32},{48,40},{56,48},{64,56},{72,6... | collective-permute-start | bytes 3080 | tf_op jit(solution)/shard_map/ppermute | solution.py:27
  433.8 5.0 collective-permute-start.46
  436.6 4.9 collective-permute-start.47
  462.4 8.1 %collective-permute-start.48 = (f32[1,1,256]{2,1,0:T(1,128)S(1)}, f32[1,1,256]{2,1,0:T(1,128)S(1)}, u32[]{:S(2)}, u32[]{:S(2)}) collective-permute-start(f32[1,1,256]{2,1,0:T(1,128)S(1)} %reshape.711), channel_id=1, source_target_pairs={{0,8},{8,16},{16,24},{24,32},{32,40},{40,48},{48,56},{56,64},{64,7... | collective-permute-start | bytes 3080 | tf_op jit(solution)/shard_map/ppermute | solution.py:26
  464.5 6.7 %collective-permute-start.49 = (f32[1,1,256]{2,1,0:T(1,128)S(1)}, f32[1,1,256]{2,1,0:T(1,128)S(1)}, u32[]{:S(2)}, u32[]{:S(2)}) collective-permute-start(f32[1,1,256]{2,1,0:T(1,128)S(1)} %reshape.711), channel_id=1, source_target_pairs={{8,0},{16,8},{24,16},{32,24},{40,32},{48,40},{56,48},{64,56},{72,6... | collective-permute-start | bytes 3080 | tf_op jit(solution)/shard_map/ppermute | solution.py:27
  471.2 4.7 collective-permute-start.50
  474.0 4.9 collective-permute-start.51
  499.9 8.2 %collective-permute-start.52 = (f32[1,1,256]{2,1,0:T(1,128)S(1)}, f32[1,1,256]{2,1,0:T(1,128)S(1)}, u32[]{:S(2)}, u32[]{:S(2)}) collective-permute-start(f32[1,1,256]{2,1,0:T(1,128)S(1)} %reshape.714), channel_id=1, source_target_pairs={{0,8},{8,16},{16,24},{24,32},{32,40},{40,48},{48,56},{56,64},{64,7... | collective-permute-start | bytes 3080 | tf_op jit(solution)/shard_map/ppermute | solution.py:26
  502.1 6.7 %collective-permute-start.53 = (f32[1,1,256]{2,1,0:T(1,128)S(1)}, f32[1,1,256]{2,1,0:T(1,128)S(1)}, u32[]{:S(2)}, u32[]{:S(2)}) collective-permute-start(f32[1,1,256]{2,1,0:T(1,128)S(1)} %reshape.714), channel_id=1, source_target_pairs={{8,0},{16,8},{24,16},{32,24},{40,32},{48,40},{56,48},{64,56},{72,6... | collective-permute-start | bytes 3080 | tf_op jit(solution)/shard_map/ppermute | solution.py:27
  508.8 5.0 collective-permute-start.54
  511.6 4.9 collective-permute-start.55
  (118 other events, 1276.2 us)
where the time goes:
time: 547 us; the launch traced here: 538 us
  starting transfers between devices  185 us (34%)
  other arithmetic  159 us (29%)
  local copies, waits for them, and re-layouts  70.2 us (13%)
  waiting for transfers between devices  55.5 us (10%)
  matrix products  43.8 us (8%)
  between operations  23.9 us (4%)
    ppermute x28, starting transfers between devices, extended(): after = lax.ppermute(leading, axis, down)  101 us
    ppermute x28, starting transfers between devices, extended(): before = lax.ppermute(last, axis, up)  83.9 us
    reduce_sum x8, other arithmetic, analyse(): centre = jnp.mean(piezometric_elevation, axis=1, keepdims=True)  52.2 us
    add x4, other arithmetic, advance(): return start + STEP_SIZE * (lateral + vertical) / storage_term  38.6 us
    reduce_sum x8, other arithmetic, analyse(): jnp.sum(deviation * matched[None], axis=1, keepdims=True) * layer_weight  34 us
    ppermute x28, waiting for transfers between devices, extended(): after = lax.ppermute(leading, axis, down)  30.3 us
    ppermute x28, waiting for transfers between devices, extended(): before = lax.ppermute(last, axis, up)  25.2 us
    unnamed x269, local copies, waits for them, and re-layouts  20.4 us
  transfers between devices with their start and end apart: 56, of which 26 were waited for; matrix products, arithmetic and copies ran while one was open for 6% of the time, Pallas kernels for 0%

commit v1 on v0

v1 whole, which is shorter than its diff:
```python
import jax
import jax.numpy as jnp
from jax import lax
from jax.experimental import pallas as pl
from jax.experimental.pallas import tpu as pltpu
from jax.sharding import PartitionSpec as P

ITERS = 3
ANALYSES = 2
BATCHES = 4
MEMBERS = 64
RADIUS = 8
SPAN = 16
LOWER_WEIGHT = 0.6
LANES = 128

ROWS = 32
COLS = 128
HALO = 6
EDGE = 8
SKIRT = 3
EXT_ROWS = ROWS + 2 * HALO
EXT_COLS = COLS + 2 * EDGE
WIDE_COLS = EXT_COLS + 2 * EDGE
SIDE = 24
PAD_ROWS = 80
PAD_COLS = 184
CELL_ROWS = 6
CELL_COLS = 12
SLOTS = CELL_ROWS * CELL_COLS
OWN_ROWS = 2
OWN_COLS = 8
OWN = OWN_ROWS * OWN_COLS
KINDS = 8
WINDOW = 2 * RADIUS - 1

F32 = jnp.float32
BF16 = jnp.bfloat16
SMEM = pl.BlockSpec(memory_space=pltpu.SMEM)
VMEM = pl.BlockSpec(memory_space=pltpu.VMEM)
HBM = pl.BlockSpec(memory_space=pl.ANY)


def params():
    return pltpu.CompilerParams(vmem_limit_bytes=56 * 2**20)


def turn_kernel(place, heads, coefs, turned, tiles, give_even, give_odd):
    def body(row, carry):
        turned[row] = heads[pl.ds(row, LANES, stride=ROWS), :].T
        return carry

    lax.fori_loop(0, ROWS, body, 0, unroll=4)
    for half in range(2):
        tiles[half] = coefs[half].T
    odd = place[0]
    even_from = (1 - odd) * (ROWS - HALO)
    odd_from = odd * (ROWS - HALO)
    give_even[0:HALO] = turned[pl.ds(even_from, HALO)]
    give_odd[0:HALO] = turned[pl.ds(odd_from, HALO)]
    give_even[HALO] = tiles[1 - odd]
    give_odd[HALO] = tiles[odd]


def turn(place, heads, coefs):
    return pl.pallas_call(
        turn_kernel,
        out_shape=(
            jax.ShapeDtypeStruct((ROWS, COLS, LANES), F32),
            jax.ShapeDtypeStruct((2, COLS, LANES), F32),
            jax.ShapeDtypeStruct((HALO + 1, COLS, LANES), F32),
            jax.ShapeDtypeStruct((HALO + 1, COLS, LANES), F32),
        ),
        in_specs=[SMEM, VMEM, VMEM],
        out_specs=(VMEM, VMEM, VMEM, VMEM),
        compiler_params=params(),
        name="turn",
    )(place, heads, coefs)


def strip_kernel(place, left, right, tiles_left, tiles_right, even_left, even_right, odd_left, odd_right, give_even, give_odd):
    def strip(inner, tiles, even, odd):
        south = jnp.where(place[0] == 0, even[...], odd[...])
        north = jnp.where(place[0] == 0, odd[...], even[...])
        return jnp.concatenate(
            [north[:HALO], inner[...], south[:HALO], north[HALO:], tiles[...], south[HALO:]], axis=0
        )

    west = strip(left, tiles_left, even_left, odd_left)
    east = strip(right, tiles_right, even_right, odd_right)
    give_even[...] = jnp.where(place[1] == 0, east, west)
    give_odd[...] = jnp.where(place[1] == 0, west, east)


def strips(place, turned, tiles, got_even, got_odd):
    last = COLS // EDGE - 1

    def cut(depth, at):
        return pl.BlockSpec((depth, EDGE, LANES), lambda i: (0, at, 0))

    whole = pl.BlockSpec((EXT_ROWS + 4, EDGE, LANES), lambda i: (0, 0, 0))
    shape = jax.ShapeDtypeStruct((EXT_ROWS + 4, EDGE, LANES), F32)
    return pl.pallas_call(
        strip_kernel,
        grid=(1,),
        out_shape=(shape, shape),
        in_specs=[
            SMEM,
            cut(ROWS, 0),
            cut(ROWS, last),
            cut(2, 0),
            cut(2, last),
            cut(HALO + 1, 0),
            cut(HALO + 1, last),
            cut(HALO + 1, 0),
            cut(HALO + 1, last),
        ],
        out_specs=(whole, whole),
        compiler_params=params(),
        name="strips",
    )(place, turned, turned, tiles, tiles, got_even, got_even, got_odd, got_odd)


def spread_matrix():
    lane = lax.broadcasted_iota(jnp.int32, (2 * LANES, 4 * LANES), 0) % KINDS
    out = lax.broadcasted_iota(jnp.int32, (2 * LANES, 4 * LANES), 1)
    group = out // LANES
    lower = out % LANES >= MEMBERS
    wanted = jnp.where(group == 0, jnp.where(lower, 1, 0), group + 1)
    wanted = jnp.where((group == 3) & lower, KINDS, wanted)
    return (lane == wanted).astype(BF16)


def spread_coefs(tiles, coef, first, count):
    matrix = spread_matrix()
    owner = lax.broadcasted_iota(jnp.int32, (EXT_COLS, LANES), 1) // KINDS

    def body(step, carry):
        row = step + first + SPAN
        tile = jnp.where(owner == row % SPAN, tiles[row // SPAN], 0.0)
        high = tile.astype(BF16)
        low = (tile - high.astype(F32)).astype(BF16)
        wide = jnp.dot(jnp.concatenate([high, low], axis=1), matrix, preferred_element_type=F32)
        for kind in range(4):
            coef[kind, step] = wide[:, kind * LANES : (kind + 1) * LANES]
        return carry

    lax.fori_loop(0, count, body, 0, unroll=2)


def storage_step(src, src_at, start, start_at, dst, dst_at, coef, coef_at, low, high, col, width):
    def body(row, carry):
        def read(ref, at, dr, dc):
            return ref[row + (at[0] + dr), at[1] + col + dc : at[1] + col + dc + width, :]

        def factor(kind):
            return coef[kind, row + coef_at, EDGE + col : EDGE + col + width, :]

        u = read(src, src_at, 0, 0)
        around = read(src, src_at, -1, 0) + read(src, src_at, 1, 0) + read(src, src_at, 0, -1) + read(src, src_at, 0, 1)
        exchange = pltpu.roll(u, MEMBERS, 1) - u
        top = factor(0) * (around - 4.0 * u) + factor(1) * exchange + factor(3)
        bottom = factor(2) * (1.0 + jnp.tanh(0.5 * u)) + 1.0
        value = read(start, start_at, 0, 0) + top / bottom
        dst[row + dst_at[0], dst_at[1] + col : dst_at[1] + col + width, :] = value
        return carry

    lax.fori_loop(low, high, body, 0, unroll=4 if (high - low) % 4 == 0 else 2)


def pick_slots(src, at, rows, cols, out):
    for slot in range(OWN):
        cell = (2 + slot // OWN_COLS) * CELL_COLS + 2 + slot % OWN_COLS
        out[slot : slot + 1, :] = src[rows[cell] + at[0], pl.ds(cols[cell] + at[1], 1), :]


def first_kernel(place, rows, cols, turned, tiles, ns_even, ns_odd, ew_even, ew_odd, cast, slots, ext_tiles, start, one, two, coef):
    odd_n, odd_e = place[0], place[1]
    inner = pl.ds(2 * EDGE, COLS)
    even_row = (1 - odd_n) * (ROWS + HALO)
    odd_row = odd_n * (ROWS + HALO)
    start[HALO : HALO + ROWS, inner, :] = turned[...]
    start[pl.ds(even_row, HALO), inner, :] = ns_even[:HALO]
    start[pl.ds(odd_row, HALO), inner, :] = ns_odd[:HALO]
    even_col = pl.multiple_of(EDGE + (1 - odd_e) * (COLS + EDGE), EDGE)
    odd_col = pl.multiple_of(EDGE + odd_e * (COLS + EDGE), EDGE)
    start[:, pl.ds(even_col, EDGE), :] = ew_even[:EXT_ROWS]
    start[:, pl.ds(odd_col, EDGE), :] = ew_odd[:EXT_ROWS]
    ext_tiles[1:3, EDGE : EDGE + COLS, :] = tiles[...]
    ext_tiles[(1 - odd_n) * 3, EDGE : EDGE + COLS, :] = ns_even[HALO]
    ext_tiles[odd_n * 3, EDGE : EDGE + COLS, :] = ns_odd[HALO]
    ext_tiles[:, pl.ds(pl.multiple_of(even_col - EDGE, EDGE), EDGE), :] = ew_even[EXT_ROWS:]
    ext_tiles[:, pl.ds(pl.multiple_of(odd_col - EDGE, EDGE), EDGE), :] = ew_odd[EXT_ROWS:]
    spread_coefs(ext_tiles, coef, -HALO, EXT_ROWS)
    at = (HALO, 2 * EDGE)
    storage_step(start, at, start, at, one, at, coef, HALO, -5, ROWS + 5, -EDGE, EXT_COLS)
    storage_step(one, at, start, at, two, at, coef, HALO, -4, ROWS + 4, -EDGE, EXT_COLS)
    out_at = (SKIRT, EDGE)
    storage_step(two, at, start, at, cast, out_at, coef, HALO, -SKIRT, ROWS + SKIRT, -EDGE, EXT_COLS)
    pick_slots(cast, out_at, rows, cols, slots)


def first_forecast(place, rows, cols, turned, tiles, ns_even, ns_odd, ew_even, ew_odd):
    return pl.pallas_call(
        first_kernel,
        out_shape=(
            jax.ShapeDtypeStruct((ROWS + 2 * SKIRT, EXT_COLS, LANES), F32),
            jax.ShapeDtypeStruct((OWN, LANES), F32),
            jax.ShapeDtypeStruct((4, EXT_COLS, LANES), F32),
        ),
        in_specs=[SMEM, SMEM, SMEM] + [VMEM] * 6,
        out_specs=(VMEM, VMEM, VMEM),
        scratch_shapes=[pltpu.VMEM((EXT_ROWS, WIDE_COLS, LANES), F32)] * 3
        + [pltpu.VMEM((4, EXT_ROWS, EXT_COLS, LANES), F32)],
        compiler_params=params(),
        name="first_forecast",
    )(place, rows, cols, turned, tiles, ns_even, ns_odd, ew_even, ew_odd)


def serial_slots(place, mid, got_even, got_odd, table, across, members, anomaly, change):
    odd = place[0] == 1
    south = jnp.where(odd, got_odd[...], got_even[...])
    north = jnp.where(odd, got_even[...], got_odd[...])
    for third, source in enumerate((north, mid[...], south)):
        for half in range(OWN_ROWS):
            base = (third * OWN_ROWS + half) * CELL_COLS
            own = half * OWN_COLS
            members[base : base + 2, :] = source[own + OWN_COLS - 2 : own + OWN_COLS]
            members[base + 2 : base + 2 + OWN_COLS, :] = source[OWN + own : OWN + own + OWN_COLS]
            members[base + 2 + OWN_COLS : base + CELL_COLS, :] = source[2 * OWN + own : 2 * OWN + own + 2]
    lane = lax.broadcasted_iota(jnp.int32, (SLOTS, LANES), 1)
    prior = members[...]
    prior = jnp.where(lane < MEMBERS, prior, pltpu.roll(prior, MEMBERS, 1))
    value, noise, live = table[:, 0:1], table[:, 1:2], table[:, 2:3]
    near = jnp.maximum(0.0, 1.0 - jnp.abs(table[:, 3:4] - across[3:4, :]) / RADIUS)
    near = near * jnp.maximum(0.0, 1.0 - jnp.abs(table[:, 4:5] - across[4:5, :]) / RADIUS)
    turn_of = table[:, 5:6]
    kept_anomaly = jnp.zeros((SLOTS, LANES), F32)
    kept_change = jnp.zeros((SLOTS, LANES), F32)
    for batch in range(BATCHES):
        now = turn_of == float(batch)
        mean = jnp.sum(prior, axis=1, keepdims=True) / LANES
        off = prior - mean
        spread = jnp.sum(off * off, axis=1, keepdims=True) / (2.0 * (MEMBERS - 1))
        gain = live / ((spread + noise) * (MEMBERS - 1))
        shrink = 1.0 / (1.0 + jnp.sqrt(noise / (spread + noise)))
        delta = jnp.where(now, gain * ((value - mean) - shrink * off), 0.0)
        kept_anomaly = jnp.where(now, off, kept_anomaly)
        kept_change = jnp.where(now, delta, kept_change)
        if batch < BATCHES - 1:
            cross = lax.dot_general(
                prior, off, (((1,), (1,)), ((), ())), precision=lax.Precision.HIGHEST, preferred_element_type=F32
            )
            prior = prior + jnp.dot(
                0.5 * near * cross, delta, precision=lax.Precision.HIGHEST, preferred_element_type=F32
            )
    anomaly[...] = kept_anomaly
    change[...] = kept_change


def windows(rows, cols, live, colours, state, anomaly, change, skirt):
    lane_in = lax.broadcasted_iota(jnp.int32, (2 * LANES, LANES), 0) % LANES
    lane_out = lax.broadcasted_iota(jnp.int32, (2 * LANES, LANES), 1)
    ones = ((lane_in // MEMBERS) == (lane_out // MEMBERS)).astype(BF16)
    offset = lax.broadcasted_iota(jnp.int32, (2 * RADIUS, LANES), 0) - (RADIUS - 1)
    lane = lax.broadcasted_iota(jnp.int32, (2 * RADIUS, LANES), 1)
    taper = jnp.maximum(0.0, 1.0 - jnp.abs(offset).astype(F32) / RADIUS)
    taper = taper * jnp.where(lane < MEMBERS, 1.0, LOWER_WEIGHT)
    count = CELL_COLS // 2 - 1
    shift = SIDE - (RADIUS - 1)

    def group(step, carry):
        colour = colours[step // 2]
        down = colour // 2
        right = colour % 2
        cell_row = 2 - down + 2 * (step % 2)
        first = cell_row * CELL_COLS + 2 - right
        cells = [first + 2 * i for i in range(count)]
        wanted = jnp.zeros((), jnp.bool_)
        for cell in cells:
            meets = (rows[cell] + RADIUS > -skirt) & (rows[cell] - RADIUS < ROWS - 1 + skirt)
            wanted = wanted | (meets & (live[cell] != 0))

        @pl.when(wanted)
        def _():
            held, products = [], []
            for cell in cells:
                row, col = rows[cell] + shift, cols[cell] + shift
                pattern = anomaly[pl.ds(cell, 1), :]
                for i in range(WINDOW):
                    x = state[row + i, pl.ds(col, 2 * RADIUS), :]
                    held.append(x)
                    products.append(x * pattern)
            product = jnp.concatenate(products, axis=0)
            high = product.astype(BF16)
            low = (product - high.astype(F32)).astype(BF16)
            moment = jnp.dot(jnp.concatenate([high, low], axis=1), ones, preferred_element_type=F32)
            for n, cell in enumerate(cells):
                row, col = rows[cell] + shift, cols[cell] + shift
                delta = change[pl.ds(cell, 1), :]
                for i in range(WINDOW):
                    at = n * WINDOW + i
                    weight = taper * (1.0 - abs(i - (RADIUS - 1)) / RADIUS)
                    part = moment[at * 2 * RADIUS : (at + 1) * 2 * RADIUS]
                    state[row + i, pl.ds(col, 2 * RADIUS), :] = held[at] + part * weight * delta

        return carry

    lax.fori_loop(0, 2 * BATCHES, group, 0)


def middle_kernel(
    place, rows, cols, live, colours, next_rows, next_cols, table, across, mid, got_even, got_odd, ext_tiles, cast,
    result, slots, state, members, anomaly, change, one, two, coef, arrived,
):
    copy = pltpu.make_async_copy(
        cast, state.at[pl.ds(SIDE - SKIRT, ROWS + 2 * SKIRT), pl.ds(SIDE - EDGE, EXT_COLS), :], arrived
    )
    copy.start()
    serial_slots(place, mid, got_even, got_odd, table, across, members, anomaly, change)
    spread_coefs(ext_tiles, coef, -SKIRT, ROWS + 2 * SKIRT)
    copy.wait()
    windows(rows, cols, live, colours, state, anomaly, change, SKIRT)
    big = (SIDE, SIDE)
    at = (SKIRT, 2 * EDGE)
    storage_step(state, big, state, big, one, at, coef, SKIRT, -2, ROWS + 2, -EDGE, EXT_COLS)
    storage_step(one, at, state, big, two, at, coef, SKIRT, -1, ROWS + 1, -EDGE, EXT_COLS)
    storage_step(two, at, state, big, result, (0, 0), coef, SKIRT, 0, ROWS, 0, COLS)
    pick_slots(result, (0, 0), next_rows, next_cols, slots)


def middle(place, rows, cols, live, colours, next_rows, next_cols, table, across, mid, got_even, got_odd, ext_tiles, cast):
    return pl.pallas_call(
        middle_kernel,
        out_shape=(
            jax.ShapeDtypeStruct((ROWS, COLS, LANES), F32),
            jax.ShapeDtypeStruct((OWN, LANES), F32),
        ),
        in_specs=[SMEM] * 7 + [VMEM] * 6 + [HBM],
        out_specs=(VMEM, VMEM),
        scratch_shapes=[pltpu.VMEM((PAD_ROWS, PAD_COLS, LANES), F32)]
        + [pltpu.VMEM((SLOTS, LANES), F32)] * 3
        + [pltpu.VMEM((ROWS + 2 * SKIRT, WIDE_COLS, LANES), F32)] * 2
        + [pltpu.VMEM((4, ROWS + 2 * SKIRT, EXT_COLS, LANES), F32), pltpu.SemaphoreType.DMA(())],
        compiler_params=params(),
        name="middle",
    )(place, rows, cols, live, colours, next_rows, next_cols, table, across, mid, got_even, got_odd, ext_tiles, cast)


def last_kernel(
    place, rows, cols, live, colours, table, across, mid, got_even, got_odd, cast, heads, state, members, anomaly, change, arrived
):
    copy = pltpu.make_async_copy(cast, state.at[pl.ds(SIDE, ROWS), pl.ds(SIDE, COLS), :], arrived)
    copy.start()
    serial_slots(place, mid, got_even, got_odd, table, across, members, anomaly, change)
    copy.wait()
    windows(rows, cols, live, colours, state, anomaly, change, 0)

    def body(row, carry):
        heads[pl.ds(row, LANES, stride=ROWS), :] = state[row + SIDE, SIDE : SIDE + COLS, :].T
        return carry

    lax.fori_loop(0, ROWS, body, 0, unroll=4)


def last(place, rows, cols, live, colours, table, across, mid, got_even, got_odd, cast):
    return pl.pallas_call(
        last_kernel,
        out_shape=jax.ShapeDtypeStruct((LANES * ROWS, COLS), F32),
        in_specs=[SMEM] * 5 + [VMEM] * 5 + [HBM],
        out_specs=VMEM,
        scratch_shapes=[pltpu.VMEM((PAD_ROWS, PAD_COLS, LANES), F32)]
        + [pltpu.VMEM((SLOTS, LANES), F32)] * 3
        + [pltpu.SemaphoreType.DMA(())],
        compiler_params=params(),
        name="last",
    )(place, rows, cols, live, colours, table, across, mid, got_even, got_odd, cast)


def swap(x, axis, odd):
    peers = lax.axis_size(axis)
    low = range(odd, peers - 1, 2)
    return lax.ppermute(x, axis, [(i, i + 1) for i in low] + [(i + 1, i) for i in low])


def gather_slots(slots, odd_e):
    even = swap(slots, "east", 0)
    odd = swap(slots, "east", 1)
    west = jnp.where(odd_e == 0, odd, even)
    east = jnp.where(odd_e == 0, even, odd)
    mid = jnp.concatenate([west, slots, east], axis=0)
    return mid, swap(mid, "north", 0), swap(mid, "north", 1)


def slot_tables(obs_value, obs_error, obs_spot, obs_live, batch_colour, north_at, east_at):
    margins = ((0, 0), (0, 0), (1, 1), (1, 1))
    lat_cols = COLS // (2 * SPAN)
    stacked = jnp.stack(
        [
            jnp.pad(obs_value, margins),
            jnp.pad(obs_error, margins, constant_values=1.0),
            jnp.pad(obs_spot, margins).astype(F32),
            jnp.pad(obs_live, margins).astype(F32),
        ]
    )
    near = lax.dynamic_slice(
        stacked, (0, 0, 0, north_at, east_at * lat_cols), (4, ANALYSES, BATCHES, CELL_ROWS // 2, CELL_COLS // 2)
    )
    is_colour = batch_colour[:, None, :] == jnp.arange(4)[None, :, None]
    coloured = jnp.sum(jnp.where(is_colour[None, :, :, :, None, None], near[:, :, None], 0.0), axis=3)
    coloured = coloured.reshape(4, ANALYSES, 2, 2, CELL_ROWS // 2, CELL_COLS // 2)
    grid = coloured.transpose(0, 1, 4, 2, 5, 3).reshape(4, ANALYSES, CELL_ROWS, CELL_COLS)
    value, noise, spot, live = grid
    spot = spot.astype(jnp.int32)
    cell_row = jnp.arange(CELL_ROWS)[:, None]
    cell_col = jnp.arange(CELL_COLS)[None, :]
    row = (cell_row - 2) * SPAN + spot // SPAN
    col = (cell_col - 2) * SPAN + spot % SPAN
    turns = jnp.sum(jnp.where(is_colour, jnp.arange(BATCHES)[None, None, :], 0), axis=2)
    turns = turns.reshape(ANALYSES, 2, 2)
    turns = jnp.tile(turns, (1, CELL_ROWS // 2, CELL_COLS // 2))
    fields = jnp.stack(
        [value, noise, live, row.astype(F32), col.astype(F32), turns.astype(F32), live, live], axis=1
    ).reshape(ANALYSES, 8, SLOTS)
    flat = (ANALYSES, SLOTS)
    return (
        fields,
        fields.transpose(0, 2, 1),
        row.reshape(flat).astype(jnp.int32),
        col.reshape(flat).astype(jnp.int32),
        live.reshape(flat).astype(jnp.int32),
    )


def shards(
    head_ensemble,
    transmissivity_grid,
    interlayer_leakage_factor,
    specific_porosity_release,
    infiltration_inflow,
    obs_value,
    obs_error,
    obs_spot,
    obs_live,
    batch_colour,
):
    north_at = lax.axis_index("north")
    east_at = lax.axis_index("east")
    odd_n = north_at % 2
    odd_e = east_at % 2
    place = jnp.stack([odd_n, odd_e]).astype(jnp.int32)
    zero = jnp.zeros((ROWS, COLS), F32)
    coefs = jnp.stack(
        [
            transmissivity_grid[0],
            transmissivity_grid[1],
            interlayer_leakage_factor,
            specific_porosity_release,
            infiltration_inflow,
            zero,
            zero,
            zero,
        ],
        axis=1,
    ).reshape(2, LANES, COLS)
    across, table, rows, cols, live = slot_tables(
        obs_value, obs_error, obs_spot, obs_live, batch_colour, north_at, east_at
    )
    colours = batch_colour.astype(jnp.int32)

    turned, tiles, give_even, give_odd = turn(place, head_ensemble.reshape(LANES * ROWS, COLS), coefs)
    ns_even = swap(give_even, "north", 0)
    ns_odd = swap(give_odd, "north", 1)
    give_even, give_odd = strips(place, turned, tiles, ns_even, ns_odd)
    ew_even = swap(give_even, "east", 0)
    ew_odd = swap(give_odd, "east", 1)
    cast, slots, ext_tiles = first_forecast(
        place, rows[0], cols[0], turned, tiles, ns_even, ns_odd, ew_even, ew_odd
    )
    mid, got_even, got_odd = gather_slots(slots, odd_e)
    cast, slots = middle(
        place, rows[0], cols[0], live[0], colours[0], rows[1], cols[1], table[0], across[0], mid, got_even, got_odd,
        ext_tiles, cast,
    )
    mid, got_even, got_odd = gather_slots(slots, odd_e)
    heads = last(
        place, rows[1], cols[1], live[1], colours[1], table[1], across[1], mid, got_even, got_odd, cast
    )
    return heads.reshape(2, MEMBERS, ROWS, COLS)


def solution(mesh):
    placed = (
        P(None, None, "north", "east"),
        P(None, "north", "east"),
        P("north", "east"),
        P("north", "east"),
        P("north", "east"),
        P(),
        P(),
        P(),
        P(),
        P(),
    )
    return jax.shard_map(
        shards,
        mesh=mesh,
        in_specs=placed,
        out_specs=P(None, None, "north", "east"),
        check_vma=False,
    )
```

time: 547 us -> 115 us (0.21)
  the two profiles are of different devices: /device:TPU:25 before, /device:TPU:26 now
where the time goes in v1:
time: 115 us; the launch traced here: 113 us
  Pallas kernels  51.1 us (44%)
  starting transfers between devices  25.2 us (22%)
  waiting for transfers between devices  18.8 us (16%)
  local copies, waits for them, and re-layouts  14.8 us (13%)
  other arithmetic  2.99 us (3%)
    ppermute x12, starting transfers between devices, swap(): lax.ppermute(x, axis, [(i, i + 1) for i in low] + [(i + 1, i) for i in low])  25.2 us
    pallas_call x1, Pallas kernels, middle(): pl.pallas_call(middle_kernel, out_shape=(jax.ShapeDtypeStruct((ROWS, COLS...  18.9 us
    ppermute x12, waiting for transfers between devices, swap(): lax.ppermute(x, axis, [(i, i + 1) for i in low] + [(i + 1, i) for i in low])  18.8 us
    pallas_call x1, Pallas kernels, first_forecast(): pl.pallas_call(first_kernel, out_shape=(jax.ShapeDtypeStruct((ROWS + 2 *...  17.1 us
    pallas_call x1, Pallas kernels, last(): pl.pallas_call(last_kernel, out_shape=jax.ShapeDtypeStruct((LANES * ROWS,...  8.38 us
    pallas_call x1, Pallas kernels, turn(): pl.pallas_call(turn_kernel, out_shape=(jax.ShapeDtypeStruct((ROWS, COLS,...  4.92 us
    unnamed x35, local copies, waits for them, and re-layouts  2.73 us
  transfers between devices with their start and end apart: 12, of which 6 were waited for; matrix products, arithmetic and copies ran while one was open for 9% of the time, Pallas kernels for 0%

profile of v1, /device:TPU:26, one launch (start us, length us, event | category | flops | bytes accessed | tf_op | source)
XLA Modules:
  0.0 113.2 jit_solution(4136943062881110063)
XLA Ops:
  0.0 0.8 fusion.13
  0.9 0.6 pad_add_fusion.place
  1.5 1.6 %stack.70 = f32[32,8,128]{2,1,0:T(8,128)} concatenate(f32[32,1,128]{2,1,0:T(1,128)S(1)} %bitcast.57, f32[32,1,128]{2,1,0:T(1,128)S(1)} %bitcast.56, f32[32,1,128]{2,1,0:T(1,128)} %bitcast.58, f32[32,1,128]{2,1,0:T(1,128)} %bitcast.59, f32[32,1,128]{2,1,0:T(1,128)} %bitcast.60, f32[32,1,128]{2,1,0:T(1,128)S(1)} %stack_broadcast_in_dim.3, f32[32,2,128]{2,1,0:T(2,128)S(1)} %stack.69), dimensions={1} | concatenate | bytes 262144 | tf_op jit(solution)/shard_map/stack | solution.py:453
  3.1 4.9 %turn.1 = (f32[32,128,128]{2,1,0:T(8,128)}, f32[2,128,128]{2,1,0:T(8,128)}, f32[7,128,128]{2,1,0:T(8,128)}, f32[7,128,128]{2,1,0:T(8,128)}) custom-call(s32[2]{0:T(128)} %pad_add_fusion.place, f32[4096,128]{1,0:T(8,128)} %bitcast.52, f32[2,128,128]{2,1,0:T(8,128)} %bitcast.53), custom_call_target="tpu_custom_call" | custom-call | tf_op jit(solution)/shard_map/turn/pallas_call | solution.py:66
  8.0 1.9 %collective-permute-start = (f32[7,128,128]{2,1,0:T(8,128)}, f32[7,128,128]{2,1,0:T(8,128)S(1)}, u32[]{:S(2)}, u32[]{:S(2)}) collective-permute-start(f32[7,128,128]{2,1,0:T(8,128)} %get-tuple-element.18), channel_id=1, source_target_pairs={{0,8},{16,24},{32,40},{48,56},{64,72},{80,88},{96,104},{112,120},{... | collective-permute-start | bytes 1376264 | tf_op jit(solution)/shard_map/ppermute | solution.py:383
  9.9 7.0 %collective-permute-start.1 = (f32[7,128,128]{2,1,0:T(8,128)}, f32[7,128,128]{2,1,0:T(8,128)S(1)}, u32[]{:S(2)}, u32[]{:S(2)}) collective-permute-start(f32[7,128,128]{2,1,0:T(8,128)} %get-tuple-element.19), channel_id=1, source_target_pairs={{8,16},{24,32},{40,48},{56,64},{72,80},{88,96},{104,112},{120,128}... | collective-permute-start | bytes 1376264 | tf_op jit(solution)/shard_map/ppermute | solution.py:383
  17.0 0.1 select_reduce_fusion.1
  17.1 0.1 pad_bitcast_fusion
  17.3 0.2 convert_bitcast_fusion
  17.5 0.1 fusion.7
  17.6 0.2 select_reduce_fusion
  17.9 0.2 copy.82
  18.1 0.1 convert_element_type.124
  18.2 0.2 copy.87
  18.7 0.1 convert_element_type.127
  19.0 0.2 copy.102
  19.2 0.1 stack_unstack.13
  19.3 0.2 copy.101
  19.5 0.1 stack_unstack.12
  19.5 0.2 copy.100
  19.7 0.1 stack_unstack.11
  19.9 0.1 fusion.3
  20.0 0.2 copy.86
  20.2 0.2 copy.85
  20.4 0.2 copy.84
  20.6 0.6 squeeze.47.cols
  21.3 0.6 squeeze.46.rows
  22.1 0.2 stack.64
  22.3 0.6 slice_bitcast_fusion
  23.0 4.4 %collective-permute-done.1.odd_left.odd_right.ns_odd = f32[7,128,128]{2,1,0:T(8,128)S(1)} collective-permute-done((f32[7,128,128]{2,1,0:T(8,128)}, f32[7,128,128]{2,1,0:T(8,128)S(1)}, u32[]{:S(2)}, u32[]{:S(2)}) %collective-permute-start.1) | collective-permute-done | bytes 458784 | tf_op jit(solution)/shard_map/ppermute | solution.py:383
  27.4 0.8 copy-done.1
  28.1 1.8 %strips.1 = (f32[48,8,128]{2,1,0:T(8,128)}, f32[48,8,128]{2,1,0:T(8,128)}) custom-call(s32[2]{0:T(128)} %pad_add_fusion.place, f32[32,128,128]{2,1,0:T(8,128)} %get-tuple-element.16.left.right.turned, f32[32,128,128]{2,1,0:T(8,128)} %get-tuple-element.16.left.right.turned, f32[2,128,128]{2,1,0:T(8,128)} %get-tuple-element.17.tiles_left.tiles_right.tiles, ...), custom_call_target="tpu_custom_call" | custom-call | tf_op jit(solution)/shard_map/strips/pallas_call | solution.py:103
  29.9 2.5 %collective-permute-start.3 = (f32[48,8,128]{2,1,0:T(8,128)}, f32[48,8,128]{2,1,0:T(8,128)S(1)}, u32[]{:S(2)}, u32[]{:S(2)}) collective-permute-start(f32[48,8,128]{2,1,0:T(8,128)} %get-tuple-element.21), channel_id=1, source_target_pairs={{1,2},{3,4},{5,6},{2,1},{4,3},{6,5},{9,10},{11,12},{13,14},{10,9},... | collective-permute-start | bytes 589832 | tf_op jit(solution)/shard_map/ppermute | solution.py:383
  32.5 0.6 slice_bitcast_fusion.2
  33.1 4.0 %collective-permute-done.3.ew_odd = f32[48,8,128]{2,1,0:T(8,128)S(1)} collective-permute-done((f32[48,8,128]{2,1,0:T(8,128)}, f32[48,8,128]{2,1,0:T(8,128)S(1)}, u32[]{:S(2)}, u32[]{:S(2)}) %collective-permute-start.3) | collective-permute-done | bytes 196640 | tf_op jit(solution)/shard_map/ppermute | solution.py:383
  37.1 0.7 copy-done.3
  37.8 17.1 %first_forecast.1 = (f32[38,144,128]{2,1,0:T(8,128)}, f32[16,128]{1,0:T(8,128)}, f32[4,144,128]{2,1,0:T(8,128)}) custom-call(s32[2]{0:T(128)} %pad_add_fusion.place, s32[72]{0:T(128)} %squeeze.46.rows, s32[72]{0:T(128)} %squeeze.47.cols, f32[32,128,128]{2,1,0:T(8,128)} %get-tuple-element.16.left.right.turned, ...), custom_call_target="tpu_custom_call" | custom-call | tf_op jit(solution)/shard_map/first_forecast/pallas_call | solution.py:204
  54.8 0.5 collective-permute-start.5
  55.3 2.0 %collective-permute-start.4 = (f32[16,128]{1,0:T(8,128)}, f32[16,128]{1,0:T(8,128)S(1)}, u32[]{:S(2)}, u32[]{:S(2)}) collective-permute-start(f32[16,128]{1,0:T(8,128)} %get-tuple-element.22), channel_id=1, source_target_pairs={{1,2},{3,4},{5,6},{2,1},{4,3},{6,5},{9,10},{11,12},{13,14},{10,9},... | collective-permute-start | bytes 24584 | tf_op jit(solution)/shard_map/ppermute | solution.py:383
  57.4 3.1 %collective-permute-done.4 = f32[16,128]{1,0:T(8,128)S(1)} collective-permute-done((f32[16,128]{1,0:T(8,128)}, f32[16,128]{1,0:T(8,128)S(1)}, u32[]{:S(2)}, u32[]{:S(2)}) %collective-permute-start.4) | collective-permute-done | bytes 8224 | tf_op jit(solution)/shard_map/ppermute | solution.py:383
  60.5 0.7 pad_maximum_fusion.mid
  61.2 5.7 %collective-permute-start.7 = (f32[48,128]{1,0:T(8,128)S(1)}, f32[48,128]{1,0:T(8,128)S(1)}, u32[]{:S(2)}, u32[]{:S(2)}) collective-permute-start(f32[48,128]{1,0:T(8,128)S(1)} %pad_maximum_fusion.mid), channel_id=1, source_target_pairs={{8,16},{24,32},{40,48},{56,64},{72,80},{88,96},{104,112},{120,128}... | collective-permute-start | bytes 73736 | tf_op jit(solution)/shard_map/ppermute | solution.py:383
  67.0 0.1 collective-permute-start.6
  67.1 0.1 slice_reduce_fusion
  67.2 0.1 copy.104
  67.3 0.7 squeeze.48.live
  68.0 0.6 squeeze.41.next_cols.cols
  68.7 0.7 squeeze.40.next_rows.rows
  69.3 0.7 squeeze.51.across
  70.0 0.9 collective-permute-done.6.got_even
  70.9 0.6 copy-done.11
  71.5 18.9 %middle.1 = (f32[32,128,128]{2,1,0:T(8,128)}, f32[16,128]{1,0:T(8,128)}) custom-call(s32[2]{0:T(128)} %pad_add_fusion.place, s32[72]{0:T(128)} %squeeze.46.rows, s32[72]{0:T(128)} %squeeze.47.cols, s32[72]{0:T(128)} %squeeze.48.live, s32[4]{0:T(128)} %get-tuple-element.52.colours, s32[72]{0:T(128)} %squeeze.40.next_rows.rows, s32[72]{0:T(128)} %squeeze.41.next_cols.cols, ...), custom_call_target="tpu_custom_call" | custom-call | tf_op jit(solution)/shard_map/middle/pallas_call | solution.py:333
  90.4 0.1 collective-permute-start.9
  90.5 1.9 %collective-permute-start.8 = (f32[16,128]{1,0:T(8,128)}, f32[16,128]{1,0:T(8,128)S(1)}, u32[]{:S(2)}, u32[]{:S(2)}) collective-permute-start(f32[16,128]{1,0:T(8,128)} %get-tuple-element.25), channel_id=1, source_target_pairs={{1,2},{3,4},{5,6},{2,1},{4,3},{6,5},{9,10},{11,12},{13,14},{10,9},... | collective-permute-start | bytes 24584 | tf_op jit(solution)/shard_map/ppermute | solution.py:383
  92.5 3.2 %collective-permute-done.8 = f32[16,128]{1,0:T(8,128)S(1)} collective-permute-done((f32[16,128]{1,0:T(8,128)}, f32[16,128]{1,0:T(8,128)S(1)}, u32[]{:S(2)}, u32[]{:S(2)}) %collective-permute-start.8) | collective-permute-done | bytes 8224 | tf_op jit(solution)/shard_map/ppermute | solution.py:383
  95.7 0.7 pad_maximum_fusion.1.mid
  96.4 3.2 %collective-permute-start.11 = (f32[48,128]{1,0:T(8,128)S(1)}, f32[48,128]{1,0:T(8,128)S(1)}, u32[]{:S(2)}, u32[]{:S(2)}) collective-permute-start(f32[48,128]{1,0:T(8,128)S(1)} %pad_maximum_fusion.1.mid), channel_id=1, source_target_pairs={{8,16},{24,32},{40,48},{56,64},{72,80},{88,96},{104,112},{120,128}... | collective-permute-start | bytes 73736 | tf_op jit(solution)/shard_map/ppermute | solution.py:383
  99.6 0.1 collective-permute-start.10
  99.7 0.1 copy.83
  99.9 0.6 squeeze.42.live
  100.5 0.7 squeeze.45.across
  101.1 3.1 %collective-permute-done.11.got_odd = f32[48,128]{1,0:T(8,128)S(1)} collective-permute-done((f32[48,128]{1,0:T(8,128)S(1)}, f32[48,128]{1,0:T(8,128)S(1)}, u32[]{:S(2)}, u32[]{:S(2)}) %collective-permute-start.11) | collective-permute-done | bytes 24608 | tf_op jit(solution)/shard_map/ppermute | solution.py:383
  104.3 0.6 copy-done.12
  104.9 8.4 %last.1 = f32[4096,128]{1,0:T(8,128)} custom-call(s32[2]{0:T(128)} %pad_add_fusion.place, s32[72]{0:T(128)} %squeeze.40.next_rows.rows, s32[72]{0:T(128)} %squeeze.41.next_cols.cols, s32[72]{0:T(128)} %squeeze.42.live, s32[4]{0:T(128)} %get-tuple-element.53.colours, f32[72,8]{1,0:T(8,128)} %get-tuple-element.34.table, f32[8,72]{1,0:T(8,128)} %squeeze.45.across, ...), custom_call_target="tpu_custom_call" | custom-call | tf_op jit(solution)/shard_map/last/pallas_call | solution.py:367
  (70 shorter events, 1.3 us)
Async XLA Ops:
  0.0 16.9 %copy-start.14 = (s32[2,4]{1,0:T(2,128)S(1)}, s32[2,4]{1,0:T(2,128)}, u32[]{:S(2)}) copy-start(s32[2,4]{1,0:T(2,128)} %param.19) | copy-start | bytes 100
  0.0 17.1 %copy-start.4 = (f32[2,4,32,32]{3,2,1,0:T(8,128)S(1)}, f32[2,4,32,32]{3,2,1,0:T(8,128)}, u32[]{:S(2)}) copy-start(f32[2,4,32,32]{3,2,1,0:T(8,128)} %param.16) | copy-start | bytes 98308
  0.0 17.1 %copy-start.5 = (f32[2,4,32,32]{3,2,1,0:T(8,128)S(1)}, f32[2,4,32,32]{3,2,1,0:T(8,128)}, u32[]{:S(2)}) copy-start(f32[2,4,32,32]{3,2,1,0:T(8,128)} %param.15) | copy-start | bytes 98308
  0.0 17.3 %copy-start.6 = (s32[2,4,32,32]{3,2,1,0:T(8,128)S(1)}, s32[2,4,32,32]{3,2,1,0:T(8,128)}, u32[]{:S(2)}) copy-start(s32[2,4,32,32]{3,2,1,0:T(8,128)} %param.18) | copy-start | bytes 98308
  0.0 17.3 %copy-start.7 = (s32[2,4,32,32]{3,2,1,0:T(8,128)S(1)}, s32[2,4,32,32]{3,2,1,0:T(8,128)}, u32[]{:S(2)}) copy-start(s32[2,4,32,32]{3,2,1,0:T(8,128)} %param.17) | copy-start | bytes 98308
  8.0 15.0 %collective-permute-start = (f32[7,128,128]{2,1,0:T(8,128)}, f32[7,128,128]{2,1,0:T(8,128)S(1)}, u32[]{:S(2)}, u32[]{:S(2)}) collective-permute-start(f32[7,128,128]{2,1,0:T(8,128)} %get-tuple-element.18), channel_id=1, source_target_pairs={{0,8},{16,24},{32,40},{48,56},{64,72},{80,88},{96,104},{112,120},{... | collective-permute-start | bytes 1376264 | tf_op jit(solution)/shard_map/ppermute | solution.py:383
  9.9 17.5 %collective-permute-start.1 = (f32[7,128,128]{2,1,0:T(8,128)}, f32[7,128,128]{2,1,0:T(8,128)S(1)}, u32[]{:S(2)}, u32[]{:S(2)}) collective-permute-start(f32[7,128,128]{2,1,0:T(8,128)} %get-tuple-element.19), channel_id=1, source_target_pairs={{8,16},{24,32},{40,48},{56,64},{72,80},{88,96},{104,112},{120,128}... | collective-permute-start | bytes 1376264 | tf_op jit(solution)/shard_map/ppermute | solution.py:383
  23.0 4.4 %copy-start = (f32[7,128,128]{2,1,0:T(8,128)}, f32[7,128,128]{2,1,0:T(8,128)S(1)}, u32[]{:S(2)}) copy-start(f32[7,128,128]{2,1,0:T(8,128)S(1)} %collective-permute-done.even_left.even_right.ns_even) | copy-start | bytes 1376260
  27.4 0.8 copy-start.1
  29.9 3.2 %collective-permute-start.2 = (f32[48,8,128]{2,1,0:T(8,128)}, f32[48,8,128]{2,1,0:T(8,128)S(1)}, u32[]{:S(2)}, u32[]{:S(2)}) collective-permute-start(f32[48,8,128]{2,1,0:T(8,128)} %get-tuple-element.20), channel_id=1, source_target_pairs={{0,1},{2,3},{4,5},{6,7},{1,0},{3,2},{5,4},{7,6},{8,9},{10,11},{12,... | collective-permute-start | bytes 589832 | tf_op jit(solution)/shard_map/ppermute | solution.py:383
  29.9 7.2 %collective-permute-start.3 = (f32[48,8,128]{2,1,0:T(8,128)}, f32[48,8,128]{2,1,0:T(8,128)S(1)}, u32[]{:S(2)}, u32[]{:S(2)}) collective-permute-start(f32[48,8,128]{2,1,0:T(8,128)} %get-tuple-element.21), channel_id=1, source_target_pairs={{1,2},{3,4},{5,6},{2,1},{4,3},{6,5},{9,10},{11,12},{13,14},{10,9},... | collective-permute-start | bytes 589832 | tf_op jit(solution)/shard_map/ppermute | solution.py:383
  33.1 4.0 %copy-start.2 = (f32[48,8,128]{2,1,0:T(8,128)}, f32[48,8,128]{2,1,0:T(8,128)S(1)}, u32[]{:S(2)}) copy-start(f32[48,8,128]{2,1,0:T(8,128)S(1)} %collective-permute-done.2.ew_even) | copy-start | bytes 589828
  37.1 0.7 copy-start.3
  54.8 2.6 %collective-permute-start.5 = (f32[16,128]{1,0:T(8,128)}, f32[16,128]{1,0:T(8,128)S(1)}, u32[]{:S(2)}, u32[]{:S(2)}) collective-permute-start(f32[16,128]{1,0:T(8,128)} %get-tuple-element.22), channel_id=1, source_target_pairs={{0,1},{2,3},{4,5},{6,7},{1,0},{3,2},{5,4},{7,6},{8,9},{10,11},{12,... | collective-permute-start | bytes 24584 | tf_op jit(solution)/shard_map/ppermute | solution.py:383
  55.3 5.2 %collective-permute-start.4 = (f32[16,128]{1,0:T(8,128)}, f32[16,128]{1,0:T(8,128)S(1)}, u32[]{:S(2)}, u32[]{:S(2)}) collective-permute-start(f32[16,128]{1,0:T(8,128)} %get-tuple-element.22), channel_id=1, source_target_pairs={{1,2},{3,4},{5,6},{2,1},{4,3},{6,5},{9,10},{11,12},{13,14},{10,9},... | collective-permute-start | bytes 24584 | tf_op jit(solution)/shard_map/ppermute | solution.py:383
  61.2 9.7 %copy-start.8 = (f32[48,128]{1,0:T(8,128)}, f32[48,128]{1,0:T(8,128)S(1)}, u32[]{:S(2)}) copy-start(f32[48,128]{1,0:T(8,128)S(1)} %pad_maximum_fusion.mid) | copy-start | bytes 73732
  61.2 8.8 %collective-permute-start.7 = (f32[48,128]{1,0:T(8,128)S(1)}, f32[48,128]{1,0:T(8,128)S(1)}, u32[]{:S(2)}, u32[]{:S(2)}) collective-permute-start(f32[48,128]{1,0:T(8,128)S(1)} %pad_maximum_fusion.mid), channel_id=1, source_target_pairs={{8,16},{24,32},{40,48},{56,64},{72,80},{88,96},{104,112},{120,128}... | collective-permute-start | bytes 73736 | tf_op jit(solution)/shard_map/ppermute | solution.py:383
  67.0 3.9 %collective-permute-start.6 = (f32[48,128]{1,0:T(8,128)S(1)}, f32[48,128]{1,0:T(8,128)S(1)}, u32[]{:S(2)}, u32[]{:S(2)}) collective-permute-start(f32[48,128]{1,0:T(8,128)S(1)} %pad_maximum_fusion.mid), channel_id=1, source_target_pairs={{0,8},{16,24},{32,40},{48,56},{64,72},{80,88},{96,104},{112,120},{... | collective-permute-start | bytes 73736 | tf_op jit(solution)/shard_map/ppermute | solution.py:383
  70.0 0.9 copy-start.10
  70.9 0.6 copy-start.11
  90.4 2.0 %collective-permute-start.9 = (f32[16,128]{1,0:T(8,128)}, f32[16,128]{1,0:T(8,128)S(1)}, u32[]{:S(2)}, u32[]{:S(2)}) collective-permute-start(f32[16,128]{1,0:T(8,128)} %get-tuple-element.25), channel_id=1, source_target_pairs={{0,1},{2,3},{4,5},{6,7},{1,0},{3,2},{5,4},{7,6},{8,9},{10,11},{12,... | collective-permute-start | bytes 24584 | tf_op jit(solution)/shard_map/ppermute | solution.py:383
  90.5 5.2 %collective-permute-start.8 = (f32[16,128]{1,0:T(8,128)}, f32[16,128]{1,0:T(8,128)S(1)}, u32[]{:S(2)}, u32[]{:S(2)}) collective-permute-start(f32[16,128]{1,0:T(8,128)} %get-tuple-element.25), channel_id=1, source_target_pairs={{1,2},{3,4},{5,6},{2,1},{4,3},{6,5},{9,10},{11,12},{13,14},{10,9},... | collective-permute-start | bytes 24584 | tf_op jit(solution)/shard_map/ppermute | solution.py:383
  96.4 7.8 %copy-start.9 = (f32[48,128]{1,0:T(8,128)}, f32[48,128]{1,0:T(8,128)S(1)}, u32[]{:S(2)}) copy-start(f32[48,128]{1,0:T(8,128)S(1)} %pad_maximum_fusion.1.mid) | copy-start | bytes 73732
  96.4 7.8 %collective-permute-start.11 = (f32[48,128]{1,0:T(8,128)S(1)}, f32[48,128]{1,0:T(8,128)S(1)}, u32[]{:S(2)}, u32[]{:S(2)}) collective-permute-start(f32[48,128]{1,0:T(8,128)S(1)} %pad_maximum_fusion.1.mid), channel_id=1, source_target_pairs={{8,16},{24,32},{40,48},{56,64},{72,80},{88,96},{104,112},{120,128}... | collective-permute-start | bytes 73736 | tf_op jit(solution)/shard_map/ppermute | solution.py:383
  99.6 4.6 %collective-permute-start.10 = (f32[48,128]{1,0:T(8,128)S(1)}, f32[48,128]{1,0:T(8,128)S(1)}, u32[]{:S(2)}, u32[]{:S(2)}) collective-permute-start(f32[48,128]{1,0:T(8,128)S(1)} %pad_maximum_fusion.1.mid), channel_id=1, source_target_pairs={{0,8},{16,24},{32,40},{48,56},{64,72},{80,88},{96,104},{112,120},{... | collective-permute-start | bytes 73736 | tf_op jit(solution)/shard_map/ppermute | solution.py:383
  104.2 0.6 copy-start.12
  104.2 0.6 copy-start.13

commit v2 on v1

v2 whole, which is shorter than its diff:
```python
import jax
import jax.numpy as jnp
from jax import lax
from jax.experimental import pallas as pl
from jax.experimental.pallas import tpu as pltpu
from jax.sharding import PartitionSpec as P

ITERS = 3
ANALYSES = 2
BATCHES = 4
MEMBERS = 64
RADIUS = 8
SPAN = 16
LOWER_WEIGHT = 0.6
LANES = 128

ROWS = 32
COLS = 128
HALO = 6
EDGE = 8
SKIRT = 3
EXT_ROWS = ROWS + 2 * HALO
EXT_COLS = COLS + 2 * EDGE
WIDE_COLS = EXT_COLS + 2 * EDGE
SIDE = 24
PAD_ROWS = 80
PAD_COLS = 184
CELL_ROWS = 6
CELL_COLS = 12
SLOTS = CELL_ROWS * CELL_COLS
OWN_ROWS = 2
OWN_COLS = 8
OWN = OWN_ROWS * OWN_COLS
KINDS = 8
WINDOW = 2 * RADIUS - 1

VMEM_BYTES = 64 * 2**20

F32 = jnp.float32
BF16 = jnp.bfloat16
SMEM = pl.BlockSpec(memory_space=pltpu.SMEM)
VMEM = pl.BlockSpec(memory_space=pltpu.VMEM)
HBM = pl.BlockSpec(memory_space=pl.ANY)
MARKS = pltpu.SMEM((8, LANES), jnp.int32)


def params():
    return pltpu.CompilerParams(vmem_limit_bytes=VMEM_BYTES)


def weight(microseconds):
    return pl.CostEstimate(flops=0, bytes_accessed=int(microseconds * 3.5e6), transcendentals=0)


def parity(axis):
    return lax.axis_index(axis) % 2


def edge_kernel(top, bottom, transmissivity, leakage, release, inflow, tiles, give_even, give_odd, stacked):
    stacked[...] = jnp.zeros_like(stacked)
    for half in range(2):
        part = slice(half * SPAN, (half + 1) * SPAN)
        for kind, field in enumerate((transmissivity.at[0], transmissivity.at[1], leakage, release, inflow)):
            stacked[pl.ds(half * LANES + kind, SPAN, stride=KINDS), :] = field[part, :]
        tiles[half] = stacked[half * LANES : (half + 1) * LANES, :].T
    odd = parity("north")
    for row in range(HALO):
        upper = top[pl.ds(row, LANES, stride=8), :].T
        lower = bottom[pl.ds(8 - HALO + row, LANES, stride=8), :].T
        give_even[row] = jnp.where(odd == 0, lower, upper)
        give_odd[row] = jnp.where(odd == 0, upper, lower)
    give_even[HALO] = tiles[1 - odd]
    give_odd[HALO] = tiles[odd]


def edges(heads, transmissivity, leakage, release, inflow):
    def rows_at(at):
        return pl.BlockSpec((LANES, 8, COLS), lambda i: (0, at, 0))

    def kernel(top, bottom, *rest):
        edge_kernel(top.reshape(LANES * 8, COLS), bottom.reshape(LANES * 8, COLS), *rest)

    halo = jax.ShapeDtypeStruct((HALO + 1, COLS, LANES), F32)
    return pl.pallas_call(
        kernel,
        grid=(1,),
        out_shape=(jax.ShapeDtypeStruct((2, COLS, LANES), F32), halo, halo),
        in_specs=[rows_at(0), rows_at(ROWS // 8 - 1)] + [VMEM] * 4,
        out_specs=(VMEM, VMEM, VMEM),
        scratch_shapes=[pltpu.VMEM((2 * LANES, COLS), F32)],
        compiler_params=params(),
        name="edges",
    )(heads, heads, transmissivity, leakage, release, inflow)


def turn_kernel(heads, tiles, turned, give_even, give_odd):
    def body(row, carry):
        turned[row] = heads[pl.ds(row, LANES, stride=ROWS), :].T
        return carry

    lax.fori_loop(0, ROWS, body, 0, unroll=16)
    odd = parity("east")
    for give, at in ((give_even, 1 - odd), (give_odd, odd)):
        cols = pl.ds(pl.multiple_of(at * (COLS - EDGE), EDGE), EDGE)
        give[:ROWS] = turned[:, cols, :]
        give[ROWS:] = tiles[:, cols, :]


def turn(heads, tiles):
    strip = jax.ShapeDtypeStruct((ROWS + 2, EDGE, LANES), F32)
    return pl.pallas_call(
        turn_kernel,
        out_shape=(jax.ShapeDtypeStruct((ROWS, COLS, LANES), F32), strip, strip),
        in_specs=[VMEM, VMEM],
        out_specs=(VMEM, VMEM, VMEM),
        compiler_params=params(),
        cost_estimate=weight(4),
        name="turn",
    )(heads, tiles)


def corner_kernel(even_left, even_right, odd_left, odd_right, give_even, give_odd):
    flip_n = parity("north") == 0
    flip_e = parity("east") == 0
    for half, swap_n in enumerate((flip_n, jnp.logical_not(flip_n))):
        left = jnp.where(swap_n, odd_left[...], even_left[...])
        right = jnp.where(swap_n, odd_right[...], even_right[...])
        part = slice(half * (HALO + 1), (half + 1) * (HALO + 1))
        give_even[part] = jnp.where(flip_e, right, left)
        give_odd[part] = jnp.where(flip_e, left, right)


def corners(got_even, got_odd):
    def cut(at):
        return pl.BlockSpec((HALO + 1, EDGE, LANES), lambda i: (0, at, 0))

    last = COLS // EDGE - 1
    whole = pl.BlockSpec((2 * HALO + 2, EDGE, LANES), lambda i: (0, 0, 0))
    shape = jax.ShapeDtypeStruct((2 * HALO + 2, EDGE, LANES), F32)
    return pl.pallas_call(
        corner_kernel,
        grid=(1,),
        out_shape=(shape, shape),
        in_specs=[cut(0), cut(last), cut(0), cut(last)],
        out_specs=(whole, whole),
        compiler_params=params(),
        name="corners",
    )(got_even, got_even, got_odd, got_odd)


def spread_matrix():
    lane = lax.broadcasted_iota(jnp.int32, (2 * LANES, 4 * LANES), 0) % KINDS
    out = lax.broadcasted_iota(jnp.int32, (2 * LANES, 4 * LANES), 1)
    group = out // LANES
    lower = out % LANES >= MEMBERS
    wanted = jnp.where(group == 0, jnp.where(lower, 1, 0), group + 1)
    wanted = jnp.where((group == 3) & lower, KINDS, wanted)
    return (lane == wanted).astype(BF16)


def spread_rows(tiles, coef, matrix, first, rows):
    owner = lax.broadcasted_iota(jnp.int32, (EXT_COLS, LANES), 1) // KINDS
    parts = []
    for row in rows:
        parts.append(jnp.where(owner == (row + SPAN) % SPAN, tiles[(row + SPAN) // SPAN], 0.0))
    tile = jnp.concatenate(parts, axis=0)
    high = tile.astype(BF16)
    low = (tile - high.astype(F32)).astype(BF16)
    wide = jnp.dot(jnp.concatenate([high, low], axis=1), matrix, preferred_element_type=F32)
    for i, row in enumerate(rows):
        for kind in range(4):
            coef[kind, row - first] = wide[i * EXT_COLS : (i + 1) * EXT_COLS, kind * LANES : (kind + 1) * LANES]


def storage(u, around, start, factors):
    lateral, leakage, release, inflow = factors
    exchange = pltpu.roll(u, MEMBERS, 1) - u
    top = lateral * (around - 4.0 * u) + leakage * exchange + inflow
    bottom = release * (1.0 + jnp.tanh(0.5 * u)) + 1.0
    return start + top * pltpu.reciprocal(bottom, approx=True)


def storage_step(src, src_at, start, start_at, dst, dst_at, coef, coef_at, low, high, first, count, unroll=None):
    def strip(tile, carry):
        col = tile * 8 if unroll is None else pl.multiple_of(tile * 8, 8)

        def read(ref, at, row, shift=0):
            return ref[row + at[0], pl.ds(at[1] + 8 * first + shift + col, 8), :]

        above, u = read(src, src_at, low - 1), read(src, src_at, low)
        for row in range(low, high):
            below = read(src, src_at, row + 1)
            around = (above + below) + (read(src, src_at, row, -1) + read(src, src_at, row, 1))
            held = u if start is None else read(start, start_at, row)
            factors = [coef[kind, row + coef_at, pl.ds(EDGE + 8 * first + col, 8), :] for kind in range(4)]
            dst[row + dst_at[0], pl.ds(dst_at[1] + 8 * first + col, 8), :] = storage(u, around, held, factors)
            above, u = u, below
        return carry

    if unroll is None:
        for tile in range(count):
            strip(tile, 0)
    else:
        lax.fori_loop(0, count, strip, 0, unroll=unroll)


def fetch(pairs, sems):
    copies = [pltpu.make_async_copy(a, b, sems.at[i]) for i, (a, b) in enumerate(pairs)]
    for copy in copies:
        copy.start()
    return copies


def wait_for(copies):
    for copy in copies:
        copy.wait()


def first_kernel(
    turned, tiles, ns_even, ns_odd, ew_even, ew_odd, corner_even, corner_odd, marks_in,
    cast, slots, ext_tiles, start, one, two, coef, marks, tile_sems, sems,
):
    odd_n, odd_e = parity("north"), parity("east")
    even_row = (1 - odd_n) * (ROWS + HALO)
    odd_row = odd_n * (ROWS + HALO)
    even_col = (1 - odd_e) * (COLS + EDGE)
    odd_col = odd_e * (COLS + EDGE)
    inner = pl.ds(2 * EDGE, COLS)
    tile_inner = pl.ds(EDGE, COLS)
    moves = [
        (turned, start.at[pl.ds(HALO, ROWS), inner, :]),
        (ns_even.at[pl.ds(0, HALO)], start.at[pl.ds(even_row, HALO), inner, :]),
        (ns_odd.at[pl.ds(0, HALO)], start.at[pl.ds(odd_row, HALO), inner, :]),
    ]
    tile_moves = [
        (tiles, ext_tiles.at[pl.ds(1, 2), tile_inner, :]),
        (ns_even.at[pl.ds(HALO, 1)], ext_tiles.at[pl.ds((1 - odd_n) * 3, 1), tile_inner, :]),
        (ns_odd.at[pl.ds(HALO, 1)], ext_tiles.at[pl.ds(odd_n * 3, 1), tile_inner, :]),
    ]
    for at, strip, corner in ((even_col, ew_even, corner_even), (odd_col, ew_odd, corner_odd)):
        outer = pl.ds(pl.multiple_of(at + EDGE, EDGE), EDGE)
        tile_outer = pl.ds(pl.multiple_of(at, EDGE), EDGE)
        moves += [
            (strip.at[pl.ds(0, ROWS)], start.at[pl.ds(HALO, ROWS), outer, :]),
            (corner.at[pl.ds(0, HALO)], start.at[pl.ds(0, HALO), outer, :]),
            (corner.at[pl.ds(HALO + 1, HALO)], start.at[pl.ds(HALO + ROWS, HALO), outer, :]),
        ]
        tile_moves += [
            (strip.at[pl.ds(ROWS, 2)], ext_tiles.at[pl.ds(1, 2), tile_outer, :]),
            (corner.at[pl.ds(HALO, 1)], ext_tiles.at[pl.ds(0, 1), tile_outer, :]),
            (corner.at[pl.ds(2 * HALO + 1, 1)], ext_tiles.at[pl.ds(3, 1), tile_outer, :]),
        ]
    tile_copies = fetch(tile_moves, tile_sems)
    copies = fetch(moves + [(marks_in, marks)], sems)
    matrix = spread_matrix()
    wait_for(tile_copies)
    for part in range(4):
        spread_rows(ext_tiles, coef, matrix, -HALO, range(-HALO + part * 11, -HALO + part * 11 + 11))
    wait_for(copies)
    at = (HALO, 2 * EDGE)
    count = EXT_COLS // 8
    storage_step(start, at, None, at, one, at, coef, HALO, -5, ROWS + 5, -1, count, 9)
    storage_step(one, at, start, at, two, at, coef, HALO, -4, ROWS + 4, -1, count, 9)
    copies = []
    for part in range(3):
        first = -1 + part * count // 3
        storage_step(two, at, start, at, one, at, coef, HALO, -SKIRT, ROWS + SKIRT, first, count // 3, 6)
        copy = pltpu.make_async_copy(
            one.at[pl.ds(HALO - SKIRT, ROWS + 2 * SKIRT), pl.ds(2 * EDGE + 8 * first, 8 * count // 3), :],
            cast.at[:, pl.ds(EDGE + 8 * first, 8 * count // 3), :],
            sems.at[part],
        )
        copy.start()
        copies.append(copy)
    pick_slots(one, at, marks, 0, slots)
    wait_for(copies)


def first_forecast(pieces, marks):
    return pl.pallas_call(
        first_kernel,
        out_shape=(
            jax.ShapeDtypeStruct((ROWS + 2 * SKIRT, EXT_COLS, LANES), F32),
            jax.ShapeDtypeStruct((OWN, LANES), F32),
            jax.ShapeDtypeStruct((4, EXT_COLS, LANES), F32),
        ),
        in_specs=[HBM] * 9,
        out_specs=(HBM, VMEM, VMEM),
        scratch_shapes=[pltpu.VMEM((EXT_ROWS, WIDE_COLS, LANES), F32)] * 3
        + [pltpu.VMEM((4, EXT_ROWS, EXT_COLS, LANES), F32)]
        + [MARKS, pltpu.SemaphoreType.DMA((9,)), pltpu.SemaphoreType.DMA((10,))],
        compiler_params=params(),
        name="first_forecast",
    )(*pieces, marks)


def pick_slots(src, at, marks, cycle, out):
    for slot in range(OWN):
        cell = (2 + slot // OWN_COLS) * CELL_COLS + 2 + slot % OWN_COLS
        out[slot : slot + 1, :] = src[marks[cycle, cell] + at[0], pl.ds(marks[2 + cycle, cell] + at[1], 1), :]


def serial_slots(cycle, mid, got_even, got_odd, tables, acrosses, members, anomaly, change, beside=None):
    table = tables[cycle, :SLOTS, :]
    across = acrosses[cycle, :, :SLOTS]
    odd = parity("north") == 1
    south = jnp.where(odd, got_odd[...], got_even[...])
    north = jnp.where(odd, got_even[...], got_odd[...])
    flip = parity("east") == 0
    for third, source in enumerate((north, mid[...], south)):
        first, final = source[:OWN], source[2 * OWN :]
        west, east = jnp.where(flip, final, first), jnp.where(flip, first, final)
        for half in range(OWN_ROWS):
            base = (third * OWN_ROWS + half) * CELL_COLS
            own = half * OWN_COLS
            members[base : base + 2, :] = west[own + OWN_COLS - 2 : own + OWN_COLS]
            members[base + 2 : base + 2 + OWN_COLS, :] = source[OWN + own : OWN + own + OWN_COLS]
            members[base + 2 + OWN_COLS : base + CELL_COLS, :] = east[own : own + 2]
    lane = lax.broadcasted_iota(jnp.int32, (SLOTS, LANES), 1)
    prior = members[...]
    prior = jnp.where(lane < MEMBERS, prior, pltpu.roll(prior, MEMBERS, 1))
    value, noise, live = table[:, 0:1], table[:, 1:2], table[:, 2:3]
    near = jnp.maximum(0.0, 1.0 - jnp.abs(table[:, 3:4] - across[3:4, :]) / RADIUS)
    near = near * jnp.maximum(0.0, 1.0 - jnp.abs(table[:, 4:5] - across[4:5, :]) / RADIUS)
    turn_of = table[:, 5:6]
    kept_anomaly = jnp.zeros((SLOTS, LANES), F32)
    kept_change = jnp.zeros((SLOTS, LANES), F32)
    for batch in range(BATCHES):
        if beside is not None:
            beside(batch)
        now = turn_of == float(batch)
        mean = jnp.sum(prior, axis=1, keepdims=True) / LANES
        off = prior - mean
        spread = jnp.sum(off * off, axis=1, keepdims=True) / (2.0 * (MEMBERS - 1))
        gain = live / ((spread + noise) * (MEMBERS - 1))
        shrink = 1.0 / (1.0 + jnp.sqrt(noise / (spread + noise)))
        delta = jnp.where(now, gain * ((value - mean) - shrink * off), 0.0)
        kept_anomaly = jnp.where(now, off, kept_anomaly)
        kept_change = jnp.where(now, delta, kept_change)
        if batch < BATCHES - 1:
            cross = lax.dot_general(
                prior, off, (((1,), (1,)), ((), ())), precision=lax.Precision.HIGHEST, preferred_element_type=F32
            )
            prior = prior + jnp.dot(
                0.5 * near * cross, delta, precision=lax.Precision.HIGHEST, preferred_element_type=F32
            )
    anomaly[...] = kept_anomaly
    change[...] = kept_change


def windows(cycle, marks, state, anomaly, change, skirt):
    lane_in = lax.broadcasted_iota(jnp.int32, (2 * LANES, LANES), 0) % LANES
    lane_out = lax.broadcasted_iota(jnp.int32, (2 * LANES, LANES), 1)
    ones = ((lane_in // MEMBERS) == (lane_out // MEMBERS)).astype(BF16)
    offset = lax.broadcasted_iota(jnp.int32, (2 * RADIUS, LANES), 0) - (RADIUS - 1)
    lane = lax.broadcasted_iota(jnp.int32, (2 * RADIUS, LANES), 1)
    taper = jnp.maximum(0.0, 1.0 - jnp.abs(offset).astype(F32) / RADIUS)
    taper = taper * jnp.where(lane < MEMBERS, 1.0, LOWER_WEIGHT)
    count = CELL_COLS // 2 - 1
    shift = SIDE - (RADIUS - 1)
    reach = RADIUS - 1 + skirt

    def batch_step(batch, carry):
        colour = marks[4 + cycle, batch]
        down, right = colour // 2, colour % 2
        own = (2 + down) * CELL_COLS + 2 - right
        other = (4 - 3 * down) * CELL_COLS + 2 - right
        edge = (1 - down) * (ROWS + skirt - reach) - down * skirt
        held, products, weights, places = [], [], [], []

        def visit(cell, row, col, pattern, height):
            x = state[row + SIDE, pl.ds(col, 2 * RADIUS), :]
            held.append(x)
            products.append(x * pattern)
            weights.append(height)
            places.append((cell, row + SIDE, col))

        for i in range(count):
            cell = own + 2 * i
            row, col = marks[cycle, cell] - (RADIUS - 1), marks[2 + cycle, cell] + shift
            pattern = anomaly[pl.ds(cell, 1), :]
            for step in range(WINDOW):
                visit(cell, row + step, col, pattern, 1.0 - abs(step - (RADIUS - 1)) / RADIUS)
        for i in range(count):
            cell = other + 2 * i
            row, col = marks[cycle, cell], marks[2 + cycle, cell] + shift
            pattern = anomaly[pl.ds(cell, 1), :]
            for step in range(reach):
                height = jnp.maximum(0.0, 1.0 - jnp.abs(edge + step - row).astype(F32) / RADIUS)
                visit(cell, edge + step, col, pattern, height)
        product = jnp.concatenate(products, axis=0)
        high = product.astype(BF16)
        low = (product - high.astype(F32)).astype(BF16)
        moment = jnp.dot(jnp.concatenate([high, low], axis=1), ones, preferred_element_type=F32)
        for n, (cell, row, col) in enumerate(places):
            part = moment[n * 2 * RADIUS : (n + 1) * 2 * RADIUS] * (taper * weights[n])
            state[row, pl.ds(col, 2 * RADIUS), :] = held[n] + part * change[pl.ds(cell, 1), :]
        return carry

    lax.fori_loop(0, BATCHES, batch_step, 0)


GUIDES = [
    pltpu.VMEM((ANALYSES, LANES, LANES), F32),
    pltpu.VMEM((ANALYSES, 8, LANES), F32),
    MARKS,
    pltpu.VMEM((3 * OWN, LANES), F32),
    pltpu.VMEM((3 * OWN, LANES), F32),
    pltpu.VMEM((3 * OWN, LANES), F32),
]


def middle_kernel(*refs):
    guides_in, (ext_in, cast, result, slots), refs = refs[:6], refs[6:10], refs[10:]
    guides, refs = refs[:6], refs[6:]
    tables, acrosses, marks, mid, got_even, got_odd = guides
    ext_tiles, state, members, anomaly, change, one, two, out, coef, sems, late = refs
    copies = fetch([*zip(guides_in, guides), (ext_in, ext_tiles)], sems)
    big_copy = pltpu.make_async_copy(
        cast, state.at[pl.ds(SIDE - SKIRT, ROWS + 2 * SKIRT), pl.ds(SIDE - EDGE, EXT_COLS), :], late.at[0]
    )
    big_copy.start()
    matrix = spread_matrix()
    wait_for(copies)

    def beside(batch):
        spread_rows(ext_tiles, coef, matrix, -2, range(-2 + batch * 9, 7 + batch * 9))

    serial_slots(0, mid, got_even, got_odd, tables, acrosses, members, anomaly, change, beside)
    big_copy.wait()
    windows(0, marks, state, anomaly, change, SKIRT)
    big = (SIDE, SIDE)
    at = (2, 2 * EDGE)
    storage_step(state, big, None, big, one, at, coef, 2, -2, ROWS + 2, -1, EXT_COLS // 8)
    storage_step(one, at, state, big, two, at, coef, 2, -1, ROWS + 1, -1, EXT_COLS // 8)
    copies = []
    for part in range(4):
        cols = pl.ds(part * COLS // 4, COLS // 4)
        storage_step(two, at, state, big, out, (0, 0), coef, 2, 0, ROWS, 4 * part, 4)
        copy = pltpu.make_async_copy(out.at[:, cols, :], result.at[:, cols, :], late.at[part])
        copy.start()
        copies.append(copy)
    pick_slots(out, (0, 0), marks, 1, slots)
    wait_for(copies)


def middle(guides, gathered, ext_tiles, cast):
    return pl.pallas_call(
        middle_kernel,
        out_shape=(
            jax.ShapeDtypeStruct((ROWS, COLS, LANES), F32),
            jax.ShapeDtypeStruct((OWN, LANES), F32),
        ),
        in_specs=[HBM] * 8,
        out_specs=(HBM, VMEM),
        scratch_shapes=GUIDES
        + [pltpu.VMEM((4, EXT_COLS, LANES), F32), pltpu.VMEM((PAD_ROWS, PAD_COLS, LANES), F32)]
        + [pltpu.VMEM((SLOTS, LANES), F32)] * 3
        + [pltpu.VMEM((ROWS + 4, WIDE_COLS, LANES), F32)] * 2
        + [pltpu.VMEM((ROWS, COLS, LANES), F32), pltpu.VMEM((4, ROWS + 4, EXT_COLS, LANES), F32)]
        + [pltpu.SemaphoreType.DMA((7,)), pltpu.SemaphoreType.DMA((4,))],
        compiler_params=params(),
        name="middle",
    )(*guides, *gathered, ext_tiles, cast)


def last_kernel(*refs):
    guides_in, (cast, heads), refs = refs[:6], refs[6:8], refs[8:]
    guides, refs = refs[:6], refs[6:]
    tables, acrosses, marks, mid, got_even, got_odd = guides
    state, members, anomaly, change, out, sems, late = refs
    copies = fetch([*zip(guides_in, guides)], sems)
    big_copy = pltpu.make_async_copy(cast, state.at[pl.ds(SIDE, ROWS), pl.ds(SIDE, COLS), :], late.at[0])
    big_copy.start()
    wait_for(copies)
    serial_slots(1, mid, got_even, got_odd, tables, acrosses, members, anomaly, change)
    big_copy.wait()
    windows(1, marks, state, anomaly, change, 0)
    copies = []
    for part in range(ROWS // 8):
        for i in range(8):
            block = state[part * 8 + i + SIDE, SIDE : SIDE + COLS, :].T
            out.at[part].reshape(LANES * 8, COLS)[pl.ds(i, LANES, stride=8), :] = block
        copy = pltpu.make_async_copy(out.at[part], heads.at[:, pl.ds(part * 8, 8), :], late.at[part])
        copy.start()
        copies.append(copy)
    wait_for(copies)


def last(guides, gathered, cast):
    return pl.pallas_call(
        last_kernel,
        out_shape=jax.ShapeDtypeStruct((LANES, ROWS, COLS), F32),
        in_specs=[HBM] * 7,
        out_specs=HBM,
        scratch_shapes=GUIDES
        + [pltpu.VMEM((PAD_ROWS, PAD_COLS, LANES), F32)]
        + [pltpu.VMEM((SLOTS, LANES), F32)] * 3
        + [pltpu.VMEM((ROWS // 8, LANES, 8, COLS), F32)]
        + [pltpu.SemaphoreType.DMA((6,)), pltpu.SemaphoreType.DMA((4,))],
        compiler_params=params(),
        name="last",
    )(*guides, *gathered, cast)


def swap(x, axis, odd):
    peers = lax.axis_size(axis)
    low = range(odd, peers - 1, 2)
    return lax.ppermute(x, axis, [(i, i + 1) for i in low] + [(i + 1, i) for i in low])


def gather_slots(slots):
    even = swap(slots, "east", 0)
    odd = swap(slots, "east", 1)
    mid = jnp.concatenate([even, slots, odd], axis=0)
    return mid, swap(mid, "north", 0), swap(mid, "north", 1)


def table_kernel(colours, value, noise, spot, live, after, tables, acrosses, marks, stacked):
    tall, wide = value.shape[2:]
    lat_row = lax.axis_index("north") - 1
    lat_col = lax.axis_index("east") * (COLS // (2 * SPAN)) - 1
    top = lax.Precision.HIGHEST
    spread = 2 * CELL_ROWS
    out_row = lax.broadcasted_iota(jnp.int32, (spread, tall), 0)
    in_row = lax.broadcasted_iota(jnp.int32, (spread, tall), 1)
    in_col = lax.broadcasted_iota(jnp.int32, (wide, LANES), 0)
    cell = lax.broadcasted_iota(jnp.int32, (wide, LANES), 1)
    take_col = (in_col == lat_col + cell % CELL_COLS // 2).astype(F32)
    got_row = lax.broadcasted_iota(jnp.int32, (spread, LANES), 0)
    lane = lax.broadcasted_iota(jnp.int32, (spread, LANES), 1)
    kept = (got_row // 2 == lane // CELL_COLS) & (got_row % 2 == lane % CELL_COLS % 2) & (lane < SLOTS)
    index = lax.broadcasted_iota(jnp.int32, (1, LANES), 1)
    cell_row, cell_col = index // CELL_COLS, index % CELL_COLS
    marks[...] = jnp.zeros_like(marks)
    for cycle in range(ANALYSES):
        turn = jnp.zeros((1, LANES), F32)
        rows_of = []
        for batch in range(BATCHES):
            colour = colours[cycle, batch]
            down, right = colour // 2, colour % 2
            wanted = (in_row == lat_row + out_row // 4) & (out_row // 2 % 2 == down) & (out_row % 2 == right)
            rows_of.append(wanted.astype(F32))
            mine = (cell_row % 2 == down) & (cell_col % 2 == right)
            turn = jnp.where(mine, float(batch), turn)
        picker = jnp.concatenate(rows_of, axis=1)
        fields = []
        for source in (value, noise, spot, live):
            whole = jnp.concatenate([source[cycle, batch].astype(F32) for batch in range(BATCHES)], axis=0)
            part = jnp.dot(picker, whole, precision=top, preferred_element_type=F32)
            part = jnp.dot(part, take_col, precision=top, preferred_element_type=F32)
            fields.append(jnp.sum(jnp.where(kept, part, 0.0), axis=0, keepdims=True))
        of_value, of_noise, of_spot, of_live = fields
        of_noise = jnp.where(of_noise > 0.0, of_noise, 1.0)
        place = (of_spot + 0.5).astype(jnp.int32)
        row = (cell_row - 2) * SPAN + place // SPAN
        col = (cell_col - 2) * SPAN + place % SPAN
        marks[cycle : cycle + 1, :] = row
        marks[2 + cycle : 3 + cycle, :] = col
        chosen = jnp.zeros((1, LANES), jnp.int32)
        for batch in range(BATCHES):
            chosen = jnp.where(index == batch, colours[cycle, batch], chosen)
        marks[4 + cycle : 5 + cycle, :] = chosen
        block = jnp.concatenate(
            [of_value, of_noise, of_live, row.astype(F32), col.astype(F32), turn, turn, turn], axis=0
        )
        acrosses[cycle] = block
        stacked[...] = jnp.zeros_like(stacked)
        stacked[:8, :] = block
        tables[cycle] = stacked[...].T


def slot_tables(obs_value, obs_error, obs_spot, obs_live, batch_colour, after):
    return pl.pallas_call(
        table_kernel,
        out_shape=(
            jax.ShapeDtypeStruct((ANALYSES, LANES, LANES), F32),
            jax.ShapeDtypeStruct((ANALYSES, 8, LANES), F32),
            jax.ShapeDtypeStruct((8, LANES), jnp.int32),
        ),
        in_specs=[SMEM] + [VMEM] * 4 + [HBM],
        out_specs=(VMEM, VMEM, VMEM),
        scratch_shapes=[pltpu.VMEM((LANES, LANES), F32)],
        compiler_params=params(),
        cost_estimate=weight(3),
        name="slot_tables",
    )(batch_colour, obs_value, obs_error, obs_spot, obs_live, after)


def shards(
    head_ensemble,
    transmissivity_grid,
    interlayer_leakage_factor,
    specific_porosity_release,
    infiltration_inflow,
    obs_value,
    obs_error,
    obs_spot,
    obs_live,
    batch_colour,
):
    heads = head_ensemble.reshape(LANES, ROWS, COLS)
    tiles, give_even, give_odd = edges(
        heads, transmissivity_grid, interlayer_leakage_factor, specific_porosity_release, infiltration_inflow
    )
    ns_even, ns_odd = swap(give_even, "north", 0), swap(give_odd, "north", 1)
    turned, give_even, give_odd = turn(heads.reshape(LANES * ROWS, COLS), tiles)
    ew_even, ew_odd = swap(give_even, "east", 0), swap(give_odd, "east", 1)
    give_even, give_odd = corners(ns_even, ns_odd)
    corner_even, corner_odd = swap(give_even, "east", 0), swap(give_odd, "east", 1)
    guides = slot_tables(obs_value, obs_error, obs_spot, obs_live, batch_colour, give_even)
    pieces = (turned, tiles, ns_even, ns_odd, ew_even, ew_odd, corner_even, corner_odd)
    cast, slots, ext_tiles = first_forecast(pieces, guides[2])
    gathered = gather_slots(slots)
    cast, slots = middle(guides, gathered, ext_tiles, cast)
    gathered = gather_slots(slots)
    out = last(guides, gathered, cast)
    return out.reshape(2, MEMBERS, ROWS, COLS)


def solution(mesh):
    placed = (
        P(None, None, "north", "east"),
        P(None, "north", "east"),
        P("north", "east"),
        P("north", "east"),
        P("north", "east"),
        P(),
        P(),
        P(),
        P(),
        P(),
    )
    return jax.shard_map(
        shards,
        mesh=mesh,
        in_specs=placed,
        out_specs=P(None, None, "north", "east"),
        check_vma=False,
    )
```

time: 115 us -> 91.3 us (0.79); the launches traced: 113 us -> 90.8 us
  local copies, waits for them, and re-layouts: 14.8 us -> 2.86 us
  Pallas kernels: 51.1 us -> 41.7 us
  starting transfers between devices: 25.2 us -> 30.1 us
  waiting for transfers between devices: 18.8 us -> 15.8 us
  other arithmetic: 2.99 us -> 0 us
    pallas_call x1, Pallas kernels: 18.9 us -> 11.5 us  [middle(): pl.pallas_call(middle_kernel, out_shape=(jax.ShapeDtypeStruct((ROWS, COLS...]
    squeeze x10 -> x0, local copies, waits for them, and re-layouts: 6.4 us -> none  [the longest x1 0.7 us: shards(): live[0]]
    pallas_call x1, Pallas kernels: 17.1 us -> 11.4 us  [first_forecast(): pl.pallas_call(first_kernel, out_shape=(jax.ShapeDtypeStruct((ROWS + 2 *...]
    ppermute x12 -> x14, starting transfers between devices: 25.2 us -> 30.1 us  [swap(): lax.ppermute(x, axis, [(i, i + 1) for i in low] + [(i + 1, i) for i in low])]
    pallas_call x2 -> x4, Pallas kernels: 10.2 us -> 14.6 us  [the longest x1 6.52 us: last(): pl.pallas_call(last_kernel, out_shape=jax.ShapeDtypeStruct((LANES, ROWS,...]
    another operation x20 -> x0, local copies, waits for them, and re-layouts: 3.39 us -> none  [the longest x3 1.58 us: shards(): jnp.stack([transmissivity_grid[0], transmissivity_grid[1], interlayer_lea...]
    ppermute x12 -> x14, waiting for transfers between devices: 18.8 us -> 15.8 us  [swap(): lax.ppermute(x, axis, [(i, i + 1) for i in low] + [(i + 1, i) for i in low])]
    concatenate x2 -> x0, other arithmetic: 1.4 us -> none  [gather_slots(): mid = jnp.concatenate([west, slots, east], axis=0)]
  transfers between devices with their start and end apart: 12 -> 14, of which waited for: 6 -> 7; matrix products, arithmetic and copies ran while one was open for 9% -> 2% of each run, Pallas kernels for 0% -> 11%
where the time goes in v2:
time: 91.3 us; the launch traced here: 90.8 us
  Pallas kernels  41.7 us (46%)
  starting transfers between devices  30.1 us (33%)
  waiting for transfers between devices  15.8 us (17%)
  local copies, waits for them, and re-layouts  2.86 us (3%)
    ppermute x14, starting transfers between devices, swap(): lax.ppermute(x, axis, [(i, i + 1) for i in low] + [(i + 1, i) for i in low])  30.1 us
    ppermute x14, waiting for transfers between devices, swap(): lax.ppermute(x, axis, [(i, i + 1) for i in low] + [(i + 1, i) for i in low])  15.8 us
    pallas_call x1, Pallas kernels, middle(): pl.pallas_call(middle_kernel, out_shape=(jax.ShapeDtypeStruct((ROWS, COLS...  11.5 us
    pallas_call x1, Pallas kernels, first_forecast(): pl.pallas_call(first_kernel, out_shape=(jax.ShapeDtypeStruct((ROWS + 2 *...  11.4 us
    pallas_call x1, Pallas kernels, last(): pl.pallas_call(last_kernel, out_shape=jax.ShapeDtypeStruct((LANES, ROWS,...  6.52 us
    pallas_call x1, Pallas kernels, turn(): pl.pallas_call(turn_kernel, out_shape=(jax.ShapeDtypeStruct((ROWS, COLS,...  4.26 us
    pallas_call x1, Pallas kernels, slot_tables(): pl.pallas_call(table_kernel, out_shape=(jax.ShapeDtypeStruct((ANALYSES, L...  4.08 us
    unnamed x16, local copies, waits for them, and re-layouts  2.86 us
  transfers between devices with their start and end apart: 14, of which 7 were waited for; matrix products, arithmetic and copies ran while one was open for 2% of the time, Pallas kernels for 11%

profile of v2, /device:TPU:26, one launch (start us, length us, event | category | flops | bytes accessed | tf_op | source)
XLA Modules:
  0.0 90.8 jit_solution(7568862119594813421)
XLA Ops:
  0.0 2.5 %edges.1 = (f32[2,128,128]{2,1,0:T(8,128)}, f32[7,128,128]{2,1,0:T(8,128)}, f32[7,128,128]{2,1,0:T(8,128)}) custom-call(f32[128,32,128]{2,1,0:T(8,128)} %bitcast.3, f32[128,32,128]{2,1,0:T(8,128)} %bitcast.4, f32[2,32,128]{2,1,0:T(8,128)} %rest_0_.1, f32[32,128]{1,0:T(8,128)} %rest_1_.1, f32[32,128]{1,0:T(8,128)} %rest_2_.1, f32[32,128]{1,0:T(8,128)} %rest_3_.1), custom_call_target="tpu_custom_call" | custom-call | tf_op jit(solution)/shard_map/edges/pallas_call | solution.py:84
  2.5 1.9 %collective-permute-start = (f32[7,128,128]{2,1,0:T(8,128)}, f32[7,128,128]{2,1,0:T(8,128)}, u32[]{:S(2)}, u32[]{:S(2)}) collective-permute-start(f32[7,128,128]{2,1,0:T(8,128)} %get-tuple-element.21), channel_id=1, source_target_pairs={{0,8},{16,24},{32,40},{48,56},{64,72},{80,88},{96,104},{112,120},{... | collective-permute-start | bytes 1376264 | tf_op jit(solution)/shard_map/ppermute | solution.py:509
  4.5 7.0 %collective-permute-start.1 = (f32[7,128,128]{2,1,0:T(8,128)}, f32[7,128,128]{2,1,0:T(8,128)}, u32[]{:S(2)}, u32[]{:S(2)}) collective-permute-start(f32[7,128,128]{2,1,0:T(8,128)} %get-tuple-element.22), channel_id=1, source_target_pairs={{8,16},{24,32},{40,48},{56,64},{72,80},{88,96},{104,112},{120,128}... | collective-permute-start | bytes 1376264 | tf_op jit(solution)/shard_map/ppermute | solution.py:509
  11.5 4.3 %turn.1 = (f32[32,128,128]{2,1,0:T(8,128)}, f32[34,8,128]{2,1,0:T(8,128)}, f32[34,8,128]{2,1,0:T(8,128)}) custom-call(f32[4096,128]{1,0:T(8,128)} %bitcast.5, f32[2,128,128]{2,1,0:T(8,128)} %get-tuple-element.27.tiles), custom_call_target="tpu_custom_call" | custom-call | bytes 14000000 | tf_op jit(solution)/shard_map/turn/pallas_call | solution.py:111
  15.7 0.0 collective-permute-start.2
  15.7 2.5 %collective-permute-start.3 = (f32[34,8,128]{2,1,0:T(8,128)}, f32[34,8,128]{2,1,0:T(8,128)}, u32[]{:S(2)}, u32[]{:S(2)}) collective-permute-start(f32[34,8,128]{2,1,0:T(8,128)} %get-tuple-element.30), channel_id=1, source_target_pairs={{1,2},{3,4},{5,6},{2,1},{4,3},{6,5},{9,10},{11,12},{13,14},{10,9},... | collective-permute-start | bytes 417800 | tf_op jit(solution)/shard_map/ppermute | solution.py:509
  18.3 0.0 collective-permute-done.even_left.even_right.ns_even
  18.3 3.7 %collective-permute-done.1.odd_left.odd_right.ns_odd = f32[7,128,128]{2,1,0:T(8,128)} collective-permute-done((f32[7,128,128]{2,1,0:T(8,128)}, f32[7,128,128]{2,1,0:T(8,128)}, u32[]{:S(2)}, u32[]{:S(2)}) %collective-permute-start.1) | collective-permute-done | bytes 458784 | tf_op jit(solution)/shard_map/ppermute | solution.py:509
  22.0 1.4 %corners.1 = (f32[14,8,128]{2,1,0:T(8,128)}, f32[14,8,128]{2,1,0:T(8,128)}) custom-call(f32[7,128,128]{2,1,0:T(8,128)} %collective-permute-done.even_left.even_right.ns_even, f32[7,128,128]{2,1,0:T(8,128)} %collective-permute-done.even_left.even_right.ns_even, f32[7,128,128]{2,1,0:T(8,128)} %collective-permute-done.1.odd_left.odd_right.ns_odd, ...), custom_call_target="tpu_custom_call" | custom-call | tf_op jit(solution)/shard_map/corners/pallas_call | solution.py:140
  23.5 1.9 %collective-permute-start.5 = (f32[14,8,128]{2,1,0:T(8,128)}, f32[14,8,128]{2,1,0:T(8,128)}, u32[]{:S(2)}, u32[]{:S(2)}) collective-permute-start(f32[14,8,128]{2,1,0:T(8,128)} %get-tuple-element.31), channel_id=1, source_target_pairs={{1,2},{3,4},{5,6},{2,1},{4,3},{6,5},{9,10},{11,12},{13,14},{10,9},... | collective-permute-start | bytes 172040 | tf_op jit(solution)/shard_map/ppermute | solution.py:509
  25.4 1.7 %collective-permute-start.4 = (f32[14,8,128]{2,1,0:T(8,128)}, f32[14,8,128]{2,1,0:T(8,128)}, u32[]{:S(2)}, u32[]{:S(2)}) collective-permute-start(f32[14,8,128]{2,1,0:T(8,128)} %get-tuple-element.23.after), channel_id=1, source_target_pairs={{0,1},{2,3},{4,5},{6,7},{1,0},{3,2},{5,4},{7,6},{8,9},{10,11},{12,... | collective-permute-start | bytes 172040 | tf_op jit(solution)/shard_map/ppermute | solution.py:509
  27.1 4.1 %slot_tables.1 = (f32[2,128,128]{2,1,0:T(8,128)}, f32[2,8,128]{2,1,0:T(8,128)}, s32[8,128]{1,0:T(8,128)}) custom-call(s32[2,4]{1,0:T(2,128)} %colours.1, f32[2,4,32,32]{3,2,1,0:T(8,128)} %value.1, f32[2,4,32,32]{3,2,1,0:T(8,128)} %noise.1, s32[2,4,32,32]{3,2,1,0:T(8,128)} %spot.1, s32[2,4,32,32]{3,2,1,0:T(8,128)} %live.1, f32[14,8,128]{2,1,0:T(8,128)} %get-tuple-element.23.after), custom_call_target="tpu_custom_call" | custom-call | bytes 10500000 | tf_op jit(solution)/shard_map/slot_tables/pallas_call | solution.py:574
  31.2 0.0 collective-permute-done.2.ew_even
  31.2 0.0 collective-permute-done.3.ew_odd
  31.2 0.0 collective-permute-done.5.corner_odd
  31.2 0.0 collective-permute-done.4.corner_even
  31.2 11.4 %first_forecast.1 = (f32[38,144,128]{2,1,0:T(8,128)}, f32[16,128]{1,0:T(8,128)}, f32[4,144,128]{2,1,0:T(8,128)}) custom-call(f32[32,128,128]{2,1,0:T(8,128)} %get-tuple-element.28.turned, f32[2,128,128]{2,1,0:T(8,128)} %get-tuple-element.27.tiles, f32[7,128,128]{2,1,0:T(8,128)} %collective-permute-done.even_left.even_right.ns_even, ...), custom_call_target="tpu_custom_call" | custom-call | tf_op jit(solution)/shard_map/first_forecast/pallas_call | solution.py:280
  42.6 0.1 collective-permute-start.6
  42.7 2.5 %collective-permute-start.7 = (f32[16,128]{1,0:T(8,128)}, f32[16,128]{1,0:T(8,128)S(1)}, u32[]{:S(2)}, u32[]{:S(2)}) collective-permute-start(f32[16,128]{1,0:T(8,128)} %get-tuple-element.32), channel_id=1, source_target_pairs={{1,2},{3,4},{5,6},{2,1},{4,3},{6,5},{9,10},{11,12},{13,14},{10,9},... | collective-permute-start | bytes 24584 | tf_op jit(solution)/shard_map/ppermute | solution.py:509
  45.2 0.0 collective-permute-done.6
  45.2 0.7 constant_dynamic-update-slice_fusion.1
  46.0 1.9 %collective-permute-done.7 = f32[16,128]{1,0:T(8,128)S(1)} collective-permute-done((f32[16,128]{1,0:T(8,128)}, f32[16,128]{1,0:T(8,128)S(1)}, u32[]{:S(2)}, u32[]{:S(2)}) %collective-permute-start.7) | collective-permute-done | bytes 8224 | tf_op jit(solution)/shard_map/ppermute | solution.py:509
  47.9 0.0 copy-start
  47.9 5.7 %collective-permute-start.9 = (f32[48,128]{1,0:T(8,128)S(1)}, f32[48,128]{1,0:T(8,128)S(1)}, u32[]{:S(2)}, u32[]{:S(2)}) collective-permute-start(f32[48,128]{1,0:T(8,128)S(1)} %constant_dynamic-update-slice_fusion.refs_3_), channel_id=1, source_target_pairs={{8,16},{24,32},{40,48},{56,64},{72,80},{88,96},{104,112},{120,128}... | collective-permute-start | bytes 73736 | tf_op jit(solution)/shard_map/ppermute | solution.py:509
  53.6 0.0 copy-done
  53.6 0.3 collective-permute-start.8
  53.9 1.8 %collective-permute-done.9.refs_5_ = f32[48,128]{1,0:T(8,128)S(1)} collective-permute-done((f32[48,128]{1,0:T(8,128)S(1)}, f32[48,128]{1,0:T(8,128)S(1)}, u32[]{:S(2)}, u32[]{:S(2)}) %collective-permute-start.9) | collective-permute-done | bytes 24608 | tf_op jit(solution)/shard_map/ppermute | solution.py:509
  55.7 0.0 copy-start.2
  55.7 2.0 %collective-permute-done.8.refs_4_ = f32[48,128]{1,0:T(8,128)S(1)} collective-permute-done((f32[48,128]{1,0:T(8,128)S(1)}, f32[48,128]{1,0:T(8,128)S(1)}, u32[]{:S(2)}, u32[]{:S(2)}) %collective-permute-start.8) | collective-permute-done | bytes 24608 | tf_op jit(solution)/shard_map/ppermute | solution.py:509
  57.7 0.0 copy-done.2
  57.7 0.0 copy-start.4
  57.7 0.6 copy-done.4
  58.3 11.5 %middle.1 = (f32[32,128,128]{2,1,0:T(8,128)}, f32[16,128]{1,0:T(8,128)}) custom-call(f32[2,128,128]{2,1,0:T(8,128)} %get-tuple-element.24.refs_0_, f32[2,8,128]{2,1,0:T(8,128)} %get-tuple-element.25.refs_1_, s32[8,128]{1,0:T(8,128)} %get-tuple-element.26.marks_in.refs_2_, f32[48,128]{1,0:T(8,128)} %copy-done, f32[48,128]{1,0:T(8,128)} %copy-done.4, ...), custom_call_target="tpu_custom_call" | custom-call | tf_op jit(solution)/shard_map/middle/pallas_call | solution.py:448
  69.8 0.1 collective-permute-start.10
  69.9 1.9 %collective-permute-start.11 = (f32[16,128]{1,0:T(8,128)}, f32[16,128]{1,0:T(8,128)S(1)}, u32[]{:S(2)}, u32[]{:S(2)}) collective-permute-start(f32[16,128]{1,0:T(8,128)} %get-tuple-element.35), channel_id=1, source_target_pairs={{1,2},{3,4},{5,6},{2,1},{4,3},{6,5},{9,10},{11,12},{13,14},{10,9},... | collective-permute-start | bytes 24584 | tf_op jit(solution)/shard_map/ppermute | solution.py:509
  71.8 0.0 collective-permute-done.10
  71.9 0.7 constant_dynamic-update-slice_fusion.4
  72.6 2.5 %collective-permute-done.11 = f32[16,128]{1,0:T(8,128)S(1)} collective-permute-done((f32[16,128]{1,0:T(8,128)}, f32[16,128]{1,0:T(8,128)S(1)}, u32[]{:S(2)}, u32[]{:S(2)}) %collective-permute-start.11) | collective-permute-done | bytes 8224 | tf_op jit(solution)/shard_map/ppermute | solution.py:509
  75.1 0.0 copy-start.1
  75.1 4.3 %collective-permute-start.13 = (f32[48,128]{1,0:T(8,128)S(1)}, f32[48,128]{1,0:T(8,128)S(1)}, u32[]{:S(2)}, u32[]{:S(2)}) collective-permute-start(f32[48,128]{1,0:T(8,128)S(1)} %constant_dynamic-update-slice_fusion.3.refs_3_), channel_id=1, source_target_pairs={{8,16},{24,32},{40,48},{56,64},{72,80},{88,96},{104,112},{120,128}... | collective-permute-start | bytes 73736 | tf_op jit(solution)/shard_map/ppermute | solution.py:509
  79.4 0.0 copy-done.1
  79.4 0.1 collective-permute-start.12
  79.5 3.4 %collective-permute-done.13.refs_5_ = f32[48,128]{1,0:T(8,128)S(1)} collective-permute-done((f32[48,128]{1,0:T(8,128)S(1)}, f32[48,128]{1,0:T(8,128)S(1)}, u32[]{:S(2)}, u32[]{:S(2)}) %collective-permute-start.13) | collective-permute-done | bytes 24608 | tf_op jit(solution)/shard_map/ppermute | solution.py:509
  82.9 0.0 copy-start.3
  82.9 0.4 collective-permute-done.12.refs_4_
  83.3 0.2 copy-done.3
  83.5 0.0 copy-start.5
  83.5 0.6 copy-done.5
  84.1 6.5 %last.1 = f32[128,32,128]{2,1,0:T(8,128)} custom-call(f32[2,128,128]{2,1,0:T(8,128)} %get-tuple-element.24.refs_0_, f32[2,8,128]{2,1,0:T(8,128)} %get-tuple-element.25.refs_1_, s32[8,128]{1,0:T(8,128)} %get-tuple-element.26.marks_in.refs_2_, f32[48,128]{1,0:T(8,128)} %copy-done.1, f32[48,128]{1,0:T(8,128)} %copy-done.5, f32[48,128]{1,0:T(8,128)} %copy-done.3, ...), custom_call_target="tpu_custom_call" | custom-call | tf_op jit(solution)/shard_map/last/pallas_call | solution.py:491
  (4 shorter events, 0.0 us)
Async XLA Ops:
  2.5 15.8 %collective-permute-start = (f32[7,128,128]{2,1,0:T(8,128)}, f32[7,128,128]{2,1,0:T(8,128)}, u32[]{:S(2)}, u32[]{:S(2)}) collective-permute-start(f32[7,128,128]{2,1,0:T(8,128)} %get-tuple-element.21), channel_id=1, source_target_pairs={{0,8},{16,24},{32,40},{48,56},{64,72},{80,88},{96,104},{112,120},{... | collective-permute-start | bytes 1376264 | tf_op jit(solution)/shard_map/ppermute | solution.py:509
  4.5 17.6 %collective-permute-start.1 = (f32[7,128,128]{2,1,0:T(8,128)}, f32[7,128,128]{2,1,0:T(8,128)}, u32[]{:S(2)}, u32[]{:S(2)}) collective-permute-start(f32[7,128,128]{2,1,0:T(8,128)} %get-tuple-element.22), channel_id=1, source_target_pairs={{8,16},{24,32},{40,48},{56,64},{72,80},{88,96},{104,112},{120,128}... | collective-permute-start | bytes 1376264 | tf_op jit(solution)/shard_map/ppermute | solution.py:509
  15.7 15.4 %collective-permute-start.2 = (f32[34,8,128]{2,1,0:T(8,128)}, f32[34,8,128]{2,1,0:T(8,128)}, u32[]{:S(2)}, u32[]{:S(2)}) collective-permute-start(f32[34,8,128]{2,1,0:T(8,128)} %get-tuple-element.29), channel_id=1, source_target_pairs={{0,1},{2,3},{4,5},{6,7},{1,0},{3,2},{5,4},{7,6},{8,9},{10,11},{12,... | collective-permute-start | bytes 417800 | tf_op jit(solution)/shard_map/ppermute | solution.py:509
  15.7 15.4 %collective-permute-start.3 = (f32[34,8,128]{2,1,0:T(8,128)}, f32[34,8,128]{2,1,0:T(8,128)}, u32[]{:S(2)}, u32[]{:S(2)}) collective-permute-start(f32[34,8,128]{2,1,0:T(8,128)} %get-tuple-element.30), channel_id=1, source_target_pairs={{1,2},{3,4},{5,6},{2,1},{4,3},{6,5},{9,10},{11,12},{13,14},{10,9},... | collective-permute-start | bytes 417800 | tf_op jit(solution)/shard_map/ppermute | solution.py:509
  23.5 7.7 %collective-permute-start.5 = (f32[14,8,128]{2,1,0:T(8,128)}, f32[14,8,128]{2,1,0:T(8,128)}, u32[]{:S(2)}, u32[]{:S(2)}) collective-permute-start(f32[14,8,128]{2,1,0:T(8,128)} %get-tuple-element.31), channel_id=1, source_target_pairs={{1,2},{3,4},{5,6},{2,1},{4,3},{6,5},{9,10},{11,12},{13,14},{10,9},... | collective-permute-start | bytes 172040 | tf_op jit(solution)/shard_map/ppermute | solution.py:509
  25.4 5.8 %collective-permute-start.4 = (f32[14,8,128]{2,1,0:T(8,128)}, f32[14,8,128]{2,1,0:T(8,128)}, u32[]{:S(2)}, u32[]{:S(2)}) collective-permute-start(f32[14,8,128]{2,1,0:T(8,128)} %get-tuple-element.23.after), channel_id=1, source_target_pairs={{0,1},{2,3},{4,5},{6,7},{1,0},{3,2},{5,4},{7,6},{8,9},{10,11},{12,... | collective-permute-start | bytes 172040 | tf_op jit(solution)/shard_map/ppermute | solution.py:509
  42.6 2.6 %collective-permute-start.6 = (f32[16,128]{1,0:T(8,128)}, f32[16,128]{1,0:T(8,128)S(1)}, u32[]{:S(2)}, u32[]{:S(2)}) collective-permute-start(f32[16,128]{1,0:T(8,128)} %get-tuple-element.32), channel_id=1, source_target_pairs={{0,1},{2,3},{4,5},{6,7},{1,0},{3,2},{5,4},{7,6},{8,9},{10,11},{12,... | collective-permute-start | bytes 24584 | tf_op jit(solution)/shard_map/ppermute | solution.py:509
  42.7 5.2 %collective-permute-start.7 = (f32[16,128]{1,0:T(8,128)}, f32[16,128]{1,0:T(8,128)S(1)}, u32[]{:S(2)}, u32[]{:S(2)}) collective-permute-start(f32[16,128]{1,0:T(8,128)} %get-tuple-element.32), channel_id=1, source_target_pairs={{1,2},{3,4},{5,6},{2,1},{4,3},{6,5},{9,10},{11,12},{13,14},{10,9},... | collective-permute-start | bytes 24584 | tf_op jit(solution)/shard_map/ppermute | solution.py:509
  47.9 5.8 %copy-start = (f32[48,128]{1,0:T(8,128)}, f32[48,128]{1,0:T(8,128)S(1)}, u32[]{:S(2)}) copy-start(f32[48,128]{1,0:T(8,128)S(1)} %constant_dynamic-update-slice_fusion.refs_3_) | copy-start | bytes 73732
  47.9 7.8 %collective-permute-start.9 = (f32[48,128]{1,0:T(8,128)S(1)}, f32[48,128]{1,0:T(8,128)S(1)}, u32[]{:S(2)}, u32[]{:S(2)}) collective-permute-start(f32[48,128]{1,0:T(8,128)S(1)} %constant_dynamic-update-slice_fusion.refs_3_), channel_id=1, source_target_pairs={{8,16},{24,32},{40,48},{56,64},{72,80},{88,96},{104,112},{120,128}... | collective-permute-start | bytes 73736 | tf_op jit(solution)/shard_map/ppermute | solution.py:509
  53.6 4.1 %collective-permute-start.8 = (f32[48,128]{1,0:T(8,128)S(1)}, f32[48,128]{1,0:T(8,128)S(1)}, u32[]{:S(2)}, u32[]{:S(2)}) collective-permute-start(f32[48,128]{1,0:T(8,128)S(1)} %constant_dynamic-update-slice_fusion.refs_3_), channel_id=1, source_target_pairs={{0,8},{16,24},{32,40},{48,56},{64,72},{80,88},{96,104},{112,120},{... | collective-permute-start | bytes 73736 | tf_op jit(solution)/shard_map/ppermute | solution.py:509
  55.7 2.0 %copy-start.2 = (f32[48,128]{1,0:T(8,128)}, f32[48,128]{1,0:T(8,128)S(1)}, u32[]{:S(2)}) copy-start(f32[48,128]{1,0:T(8,128)S(1)} %collective-permute-done.9.refs_5_) | copy-start | bytes 73732
  57.7 0.6 copy-start.4
  69.8 2.0 %collective-permute-start.10 = (f32[16,128]{1,0:T(8,128)}, f32[16,128]{1,0:T(8,128)S(1)}, u32[]{:S(2)}, u32[]{:S(2)}) collective-permute-start(f32[16,128]{1,0:T(8,128)} %get-tuple-element.35), channel_id=1, source_target_pairs={{0,1},{2,3},{4,5},{6,7},{1,0},{3,2},{5,4},{7,6},{8,9},{10,11},{12,... | collective-permute-start | bytes 24584 | tf_op jit(solution)/shard_map/ppermute | solution.py:509
  69.9 5.2 %collective-permute-start.11 = (f32[16,128]{1,0:T(8,128)}, f32[16,128]{1,0:T(8,128)S(1)}, u32[]{:S(2)}, u32[]{:S(2)}) collective-permute-start(f32[16,128]{1,0:T(8,128)} %get-tuple-element.35), channel_id=1, source_target_pairs={{1,2},{3,4},{5,6},{2,1},{4,3},{6,5},{9,10},{11,12},{13,14},{10,9},... | collective-permute-start | bytes 24584 | tf_op jit(solution)/shard_map/ppermute | solution.py:509
  75.1 4.3 %copy-start.1 = (f32[48,128]{1,0:T(8,128)}, f32[48,128]{1,0:T(8,128)S(1)}, u32[]{:S(2)}) copy-start(f32[48,128]{1,0:T(8,128)S(1)} %constant_dynamic-update-slice_fusion.3.refs_3_) | copy-start | bytes 73732
  75.1 7.8 %collective-permute-start.13 = (f32[48,128]{1,0:T(8,128)S(1)}, f32[48,128]{1,0:T(8,128)S(1)}, u32[]{:S(2)}, u32[]{:S(2)}) collective-permute-start(f32[48,128]{1,0:T(8,128)S(1)} %constant_dynamic-update-slice_fusion.3.refs_3_), channel_id=1, source_target_pairs={{8,16},{24,32},{40,48},{56,64},{72,80},{88,96},{104,112},{120,128}... | collective-permute-start | bytes 73736 | tf_op jit(solution)/shard_map/ppermute | solution.py:509
  79.4 3.9 %collective-permute-start.12 = (f32[48,128]{1,0:T(8,128)S(1)}, f32[48,128]{1,0:T(8,128)S(1)}, u32[]{:S(2)}, u32[]{:S(2)}) collective-permute-start(f32[48,128]{1,0:T(8,128)S(1)} %constant_dynamic-update-slice_fusion.3.refs_3_), channel_id=1, source_target_pairs={{0,8},{16,24},{32,40},{48,56},{64,72},{80,88},{96,104},{112,120},{... | collective-permute-start | bytes 73736 | tf_op jit(solution)/shard_map/ppermute | solution.py:509
  82.9 0.6 copy-start.3
  83.5 0.6 copy-start.5

commit v3 on v2

--- a/solution.py
+++ b/solution.py
@@ -31,6 +31,7 @@
 OWN_ROWS = 2
 OWN_COLS = 8
 OWN = OWN_ROWS * OWN_COLS
+GROUP_COLS = 48
 KINDS = 8
 WINDOW = 2 * RADIUS - 1
 
@@ -40,7 +41,7 @@
 BF16 = jnp.bfloat16
 SMEM = pl.BlockSpec(memory_space=pltpu.SMEM)
 VMEM = pl.BlockSpec(memory_space=pltpu.VMEM)
-HBM = pl.BlockSpec(memory_space=pl.ANY)
+HBM = pl.BlockSpec(memory_space=pltpu.HBM)
 MARKS = pltpu.SMEM((8, LANES), jnp.int32)
 
 
@@ -254,12 +255,40 @@
     copies = fetch(moves + [(marks_in, marks)], sems)
     matrix = spread_matrix()
     wait_for(tile_copies)
-    for part in range(4):
-        spread_rows(ext_tiles, coef, matrix, -HALO, range(-HALO + part * 11, -HALO + part * 11 + 11))
     wait_for(copies)
     at = (HALO, 2 * EDGE)
     count = EXT_COLS // 8
-    storage_step(start, at, None, at, one, at, coef, HALO, -5, ROWS + 5, -1, count, 9)
+    owner = lax.broadcasted_iota(jnp.int32, (GROUP_COLS, LANES), 1) // KINDS
+
+    def body(group, carry):
+        col = pl.multiple_of(group * GROUP_COLS, GROUP_COLS)
+        needed = range(1 - HALO, ROWS + HALO - 1)
+        parts = []
+        for row in needed:
+            tile = ext_tiles[(row + SPAN) // SPAN, pl.ds(col, GROUP_COLS), :]
+            parts.append(jnp.where(owner == (row + SPAN) % SPAN, tile, 0.0))
+        tile = jnp.concatenate(parts, axis=0)
+        high = tile.astype(BF16)
+        low = (tile - high.astype(F32)).astype(BF16)
+        wide = jnp.dot(jnp.concatenate([high, low], axis=1), matrix, preferred_element_type=F32)
+        for piece in range(GROUP_COLS // 8):
+            aside = EDGE + 8 * piece
+            above = start[0, pl.ds(col + aside, 8), :]
+            u = start[1, pl.ds(col + aside, 8), :]
+            for i, row in enumerate(needed):
+                at_row = row + HALO
+                below = start[at_row + 1, pl.ds(col + aside, 8), :]
+                left = start[at_row, pl.ds(col + aside - 1, 8), :]
+                right = start[at_row, pl.ds(col + aside + 1, 8), :]
+                block = i * GROUP_COLS + 8 * piece
+                factors = [wide[block : block + 8, kind * LANES : (kind + 1) * LANES] for kind in range(4)]
+                for kind in range(4):
+                    coef[kind, at_row, pl.ds(col + 8 * piece, 8), :] = factors[kind]
+                one[at_row, pl.ds(col + aside, 8), :] = storage(u, (above + below) + (left + right), u, factors)
+                above, u = u, below
+        return carry
+
+    lax.fori_loop(0, EXT_COLS // GROUP_COLS, body, 0)
     storage_step(one, at, start, at, two, at, coef, HALO, -4, ROWS + 4, -1, count, 9)
     copies = []
     for part in range(3):
@@ -300,16 +329,21 @@
         out[slot : slot + 1, :] = src[marks[cycle, cell] + at[0], pl.ds(marks[2 + cycle, cell] + at[1], 1), :]
 
 
+def halves(x):
+    high = x.astype(BF16)
+    return high, (x - high.astype(F32)).astype(BF16)
+
+
 def serial_slots(cycle, mid, got_even, got_odd, tables, acrosses, members, anomaly, change, beside=None):
     table = tables[cycle, :SLOTS, :]
-    across = acrosses[cycle, :, :SLOTS]
+    across = acrosses[cycle]
     odd = parity("north") == 1
     south = jnp.where(odd, got_odd[...], got_even[...])
     north = jnp.where(odd, got_even[...], got_odd[...])
     flip = parity("east") == 0
     for third, source in enumerate((north, mid[...], south)):
         first, final = source[:OWN], source[2 * OWN :]
-        west, east = jnp.where(flip, final, first), jnp.where(flip, first, final)
+        west, east = jnp.where(flip, first, final), jnp.where(flip, final, first)
         for half in range(OWN_ROWS):
             base = (third * OWN_ROWS + half) * CELL_COLS
             own = half * OWN_COLS
@@ -323,6 +357,7 @@
     near = jnp.maximum(0.0, 1.0 - jnp.abs(table[:, 3:4] - across[3:4, :]) / RADIUS)
     near = near * jnp.maximum(0.0, 1.0 - jnp.abs(table[:, 4:5] - across[4:5, :]) / RADIUS)
     turn_of = table[:, 5:6]
+    spare = jnp.zeros((LANES - SLOTS, LANES), F32)
     kept_anomaly = jnp.zeros((SLOTS, LANES), F32)
     kept_change = jnp.zeros((SLOTS, LANES), F32)
     for batch in range(BATCHES):
@@ -338,11 +373,20 @@
         kept_anomaly = jnp.where(now, off, kept_anomaly)
         kept_change = jnp.where(now, delta, kept_change)
         if batch < BATCHES - 1:
+            high, low = halves(prior)
+            off_high, off_low = halves(jnp.concatenate([off, spare], axis=0))
             cross = lax.dot_general(
-                prior, off, (((1,), (1,)), ((), ())), precision=lax.Precision.HIGHEST, preferred_element_type=F32
+                jnp.concatenate([high, high, low], axis=1),
+                jnp.concatenate([off_high, off_low, off_high], axis=1),
+                (((1,), (1,)), ((), ())),
+                preferred_element_type=F32,
             )
+            high, low = halves(0.5 * near * cross)
+            delta_high, delta_low = halves(jnp.concatenate([delta, spare], axis=0))
             prior = prior + jnp.dot(
-                0.5 * near * cross, delta, precision=lax.Precision.HIGHEST, preferred_element_type=F32
+                jnp.concatenate([high, high, low], axis=1),
+                jnp.concatenate([delta_high, delta_low, delta_high], axis=0),
+                preferred_element_type=F32,
             )
     anomaly[...] = kept_anomaly
     change[...] = kept_change
@@ -510,9 +554,9 @@
 
 
 def gather_slots(slots):
+    odd = swap(slots, "east", 1)
     even = swap(slots, "east", 0)
-    odd = swap(slots, "east", 1)
-    mid = jnp.concatenate([even, slots, odd], axis=0)
+    mid = jnp.concatenate([odd, slots, even], axis=0)
     return mid, swap(mid, "north", 0), swap(mid, "north", 1)
 
 
@@ -603,11 +647,11 @@
     tiles, give_even, give_odd = edges(
         heads, transmissivity_grid, interlayer_leakage_factor, specific_porosity_release, infiltration_inflow
     )
-    ns_even, ns_odd = swap(give_even, "north", 0), swap(give_odd, "north", 1)
+    ns_odd, ns_even = swap(give_odd, "north", 1), swap(give_even, "north", 0)
     turned, give_even, give_odd = turn(heads.reshape(LANES * ROWS, COLS), tiles)
-    ew_even, ew_odd = swap(give_even, "east", 0), swap(give_odd, "east", 1)
+    ew_odd, ew_even = swap(give_odd, "east", 1), swap(give_even, "east", 0)
     give_even, give_odd = corners(ns_even, ns_odd)
-    corner_even, corner_odd = swap(give_even, "east", 0), swap(give_odd, "east", 1)
+    corner_odd, corner_even = swap(give_odd, "east", 1), swap(give_even, "east", 0)
     guides = slot_tables(obs_value, obs_error, obs_spot, obs_live, batch_colour, give_even)
     pieces = (turned, tiles, ns_even, ns_odd, ew_even, ew_odd, corner_even, corner_odd)
     cast, slots, ext_tiles = first_forecast(pieces, guides[2])

time: 91.3 us -> 91.3 us (level)
  starting transfers between devices: 30.1 us -> 32.1 us
  Pallas kernels: 41.7 us -> 40.4 us
    ppermute x14, starting transfers between devices: 30.1 us -> 32.1 us  [swap(): lax.ppermute(x, axis, [(i, i + 1) for i in low] + [(i + 1, i) for i in low])]
where the time goes in v3:
time: 91.3 us; the launch traced here: 90.7 us
  Pallas kernels  40.4 us (44%)
  starting transfers between devices  32.1 us (35%)
  waiting for transfers between devices  15.1 us (17%)
  local copies, waits for them, and re-layouts  2.84 us (3%)
    ppermute x14, starting transfers between devices, swap(): lax.ppermute(x, axis, [(i, i + 1) for i in low] + [(i + 1, i) for i in low])  32.1 us
    ppermute x14, waiting for transfers between devices, swap(): lax.ppermute(x, axis, [(i, i + 1) for i in low] + [(i + 1, i) for i in low])  15.1 us
    pallas_call x1, Pallas kernels, middle(): pl.pallas_call(middle_kernel, out_shape=(jax.ShapeDtypeStruct((ROWS, COLS...  11.2 us
    pallas_call x1, Pallas kernels, first_forecast(): pl.pallas_call(first_kernel, out_shape=(jax.ShapeDtypeStruct((ROWS + 2 *...  10.5 us
    pallas_call x1, Pallas kernels, last(): pl.pallas_call(last_kernel, out_shape=jax.ShapeDtypeStruct((LANES, ROWS,...  6.36 us
    pallas_call x1, Pallas kernels, turn(): pl.pallas_call(turn_kernel, out_shape=(jax.ShapeDtypeStruct((ROWS, COLS,...  4.26 us
    pallas_call x1, Pallas kernels, slot_tables(): pl.pallas_call(table_kernel, out_shape=(jax.ShapeDtypeStruct((ANALYSES, L...  4.08 us
    unnamed x16, local copies, waits for them, and re-layouts  2.83 us
  transfers between devices with their start and end apart: 14, of which 7 were waited for; matrix products, arithmetic and copies ran while one was open for 2% of the time, Pallas kernels for 11%

profile of v3, /device:TPU:26, one launch (start us, length us, event | category | flops | bytes accessed | tf_op | source)
XLA Modules:
  0.0 90.7 jit_solution(4864668610443901680)
XLA Ops:
  0.0 2.5 %edges.1 = (f32[2,128,128]{2,1,0:T(8,128)}, f32[7,128,128]{2,1,0:T(8,128)}, f32[7,128,128]{2,1,0:T(8,128)}) custom-call(f32[128,32,128]{2,1,0:T(8,128)} %bitcast.3, f32[128,32,128]{2,1,0:T(8,128)} %bitcast.4, f32[2,32,128]{2,1,0:T(8,128)} %rest_0_.1, f32[32,128]{1,0:T(8,128)} %rest_1_.1, f32[32,128]{1,0:T(8,128)} %rest_2_.1, f32[32,128]{1,0:T(8,128)} %rest_3_.1), custom_call_target="tpu_custom_call" | custom-call | tf_op jit(solution)/shard_map/edges/pallas_call | solution.py:85
  2.5 1.9 %collective-permute-start = (f32[7,128,128]{2,1,0:T(8,128)}, f32[7,128,128]{2,1,0:T(8,128)}, u32[]{:S(2)}, u32[]{:S(2)}) collective-permute-start(f32[7,128,128]{2,1,0:T(8,128)} %get-tuple-element.21), channel_id=1, source_target_pairs={{0,8},{16,24},{32,40},{48,56},{64,72},{80,88},{96,104},{112,120},{... | collective-permute-start | bytes 1376264 | tf_op jit(solution)/shard_map/ppermute | solution.py:553
  4.5 7.0 %collective-permute-start.1 = (f32[7,128,128]{2,1,0:T(8,128)}, f32[7,128,128]{2,1,0:T(8,128)}, u32[]{:S(2)}, u32[]{:S(2)}) collective-permute-start(f32[7,128,128]{2,1,0:T(8,128)} %get-tuple-element.22), channel_id=1, source_target_pairs={{8,16},{24,32},{40,48},{56,64},{72,80},{88,96},{104,112},{120,128}... | collective-permute-start | bytes 1376264 | tf_op jit(solution)/shard_map/ppermute | solution.py:553
  11.5 4.3 %turn.1 = (f32[32,128,128]{2,1,0:T(8,128)}, f32[34,8,128]{2,1,0:T(8,128)}, f32[34,8,128]{2,1,0:T(8,128)}) custom-call(f32[4096,128]{1,0:T(8,128)} %bitcast.5, f32[2,128,128]{2,1,0:T(8,128)} %get-tuple-element.27.tiles), custom_call_target="tpu_custom_call" | custom-call | bytes 14000000 | tf_op jit(solution)/shard_map/turn/pallas_call | solution.py:112
  15.7 0.0 collective-permute-start.2
  15.7 2.5 %collective-permute-start.3 = (f32[34,8,128]{2,1,0:T(8,128)}, f32[34,8,128]{2,1,0:T(8,128)}, u32[]{:S(2)}, u32[]{:S(2)}) collective-permute-start(f32[34,8,128]{2,1,0:T(8,128)} %get-tuple-element.30), channel_id=1, source_target_pairs={{1,2},{3,4},{5,6},{2,1},{4,3},{6,5},{9,10},{11,12},{13,14},{10,9},... | collective-permute-start | bytes 417800 | tf_op jit(solution)/shard_map/ppermute | solution.py:553
  18.3 0.0 collective-permute-done.even_left.even_right.ns_even
  18.3 3.7 %collective-permute-done.1.odd_left.odd_right.ns_odd = f32[7,128,128]{2,1,0:T(8,128)} collective-permute-done((f32[7,128,128]{2,1,0:T(8,128)}, f32[7,128,128]{2,1,0:T(8,128)}, u32[]{:S(2)}, u32[]{:S(2)}) %collective-permute-start.1) | collective-permute-done | bytes 458784 | tf_op jit(solution)/shard_map/ppermute | solution.py:553
  22.0 1.4 %corners.1 = (f32[14,8,128]{2,1,0:T(8,128)}, f32[14,8,128]{2,1,0:T(8,128)}) custom-call(f32[7,128,128]{2,1,0:T(8,128)} %collective-permute-done.even_left.even_right.ns_even, f32[7,128,128]{2,1,0:T(8,128)} %collective-permute-done.even_left.even_right.ns_even, f32[7,128,128]{2,1,0:T(8,128)} %collective-permute-done.1.odd_left.odd_right.ns_odd, ...), custom_call_target="tpu_custom_call" | custom-call | tf_op jit(solution)/shard_map/corners/pallas_call | solution.py:141
  23.5 1.9 %collective-permute-start.5 = (f32[14,8,128]{2,1,0:T(8,128)}, f32[14,8,128]{2,1,0:T(8,128)}, u32[]{:S(2)}, u32[]{:S(2)}) collective-permute-start(f32[14,8,128]{2,1,0:T(8,128)} %get-tuple-element.31), channel_id=1, source_target_pairs={{1,2},{3,4},{5,6},{2,1},{4,3},{6,5},{9,10},{11,12},{13,14},{10,9},... | collective-permute-start | bytes 172040 | tf_op jit(solution)/shard_map/ppermute | solution.py:553
  25.4 1.7 %collective-permute-start.4 = (f32[14,8,128]{2,1,0:T(8,128)}, f32[14,8,128]{2,1,0:T(8,128)}, u32[]{:S(2)}, u32[]{:S(2)}) collective-permute-start(f32[14,8,128]{2,1,0:T(8,128)} %get-tuple-element.23.after), channel_id=1, source_target_pairs={{0,1},{2,3},{4,5},{6,7},{1,0},{3,2},{5,4},{7,6},{8,9},{10,11},{12,... | collective-permute-start | bytes 172040 | tf_op jit(solution)/shard_map/ppermute | solution.py:553
  27.1 4.1 %slot_tables.1 = (f32[2,128,128]{2,1,0:T(8,128)}, f32[2,8,128]{2,1,0:T(8,128)}, s32[8,128]{1,0:T(8,128)}) custom-call(s32[2,4]{1,0:T(2,128)} %colours.1, f32[2,4,32,32]{3,2,1,0:T(8,128)} %value.1, f32[2,4,32,32]{3,2,1,0:T(8,128)} %noise.1, s32[2,4,32,32]{3,2,1,0:T(8,128)} %spot.1, s32[2,4,32,32]{3,2,1,0:T(8,128)} %live.1, f32[14,8,128]{2,1,0:T(8,128)} %get-tuple-element.23.after), custom_call_target="tpu_custom_call" | custom-call | bytes 10500000 | tf_op jit(solution)/shard_map/slot_tables/pallas_call | solution.py:618
  31.2 0.0 collective-permute-done.2.ew_even
  31.2 0.0 collective-permute-done.3.ew_odd
  31.2 0.0 collective-permute-done.5.corner_odd
  31.2 0.0 collective-permute-done.4.corner_even
  31.2 10.5 %first_forecast.1 = (f32[38,144,128]{2,1,0:T(8,128)}, f32[16,128]{1,0:T(8,128)}, f32[4,144,128]{2,1,0:T(8,128)}) custom-call(f32[32,128,128]{2,1,0:T(8,128)} %get-tuple-element.28.turned, f32[2,128,128]{2,1,0:T(8,128)} %get-tuple-element.27.tiles, f32[7,128,128]{2,1,0:T(8,128)} %collective-permute-done.even_left.even_right.ns_even, ...), custom_call_target="tpu_custom_call" | custom-call | tf_op jit(solution)/shard_map/first_forecast/pallas_call | solution.py:309
  41.7 2.1 %collective-permute-start.6 = (f32[16,128]{1,0:T(8,128)}, f32[16,128]{1,0:T(8,128)S(1)}, u32[]{:S(2)}, u32[]{:S(2)}) collective-permute-start(f32[16,128]{1,0:T(8,128)} %get-tuple-element.32), channel_id=1, source_target_pairs={{1,2},{3,4},{5,6},{2,1},{4,3},{6,5},{9,10},{11,12},{13,14},{10,9},... | collective-permute-start | bytes 24584 | tf_op jit(solution)/shard_map/ppermute | solution.py:553
  43.8 1.2 %collective-permute-start.7 = (f32[16,128]{1,0:T(8,128)}, f32[16,128]{1,0:T(8,128)S(1)}, u32[]{:S(2)}, u32[]{:S(2)}) collective-permute-start(f32[16,128]{1,0:T(8,128)} %get-tuple-element.32), channel_id=1, source_target_pairs={{0,1},{2,3},{4,5},{6,7},{1,0},{3,2},{5,4},{7,6},{8,9},{10,11},{12,... | collective-permute-start | bytes 24584 | tf_op jit(solution)/shard_map/ppermute | solution.py:553
  45.0 1.9 %collective-permute-done.6 = f32[16,128]{1,0:T(8,128)S(1)} collective-permute-done((f32[16,128]{1,0:T(8,128)}, f32[16,128]{1,0:T(8,128)S(1)}, u32[]{:S(2)}, u32[]{:S(2)}) %collective-permute-start.6) | collective-permute-done | bytes 8224 | tf_op jit(solution)/shard_map/ppermute | solution.py:553
  46.9 0.7 constant_dynamic-update-slice_fusion.1
  47.6 0.0 collective-permute-done.7
  47.6 0.0 copy-start
  47.6 5.8 %collective-permute-start.9 = (f32[48,128]{1,0:T(8,128)S(1)}, f32[48,128]{1,0:T(8,128)S(1)}, u32[]{:S(2)}, u32[]{:S(2)}) collective-permute-start(f32[48,128]{1,0:T(8,128)S(1)} %constant_dynamic-update-slice_fusion.refs_3_), channel_id=1, source_target_pairs={{8,16},{24,32},{40,48},{56,64},{72,80},{88,96},{104,112},{120,128}... | collective-permute-start | bytes 73736 | tf_op jit(solution)/shard_map/ppermute | solution.py:553
  53.3 0.0 copy-done
  53.3 0.3 collective-permute-start.8
  53.6 1.8 %collective-permute-done.9.refs_5_ = f32[48,128]{1,0:T(8,128)S(1)} collective-permute-done((f32[48,128]{1,0:T(8,128)S(1)}, f32[48,128]{1,0:T(8,128)S(1)}, u32[]{:S(2)}, u32[]{:S(2)}) %collective-permute-start.9) | collective-permute-done | bytes 24608 | tf_op jit(solution)/shard_map/ppermute | solution.py:553
  55.4 0.0 copy-start.2
  55.4 2.0 %collective-permute-done.8.refs_4_ = f32[48,128]{1,0:T(8,128)S(1)} collective-permute-done((f32[48,128]{1,0:T(8,128)S(1)}, f32[48,128]{1,0:T(8,128)S(1)}, u32[]{:S(2)}, u32[]{:S(2)}) %collective-permute-start.8) | collective-permute-done | bytes 24608 | tf_op jit(solution)/shard_map/ppermute | solution.py:553
  57.4 0.0 copy-done.2
  57.4 0.0 copy-start.4
  57.4 0.6 copy-done.4
  58.0 11.2 %middle.1 = (f32[32,128,128]{2,1,0:T(8,128)}, f32[16,128]{1,0:T(8,128)}) custom-call(f32[2,128,128]{2,1,0:T(8,128)} %get-tuple-element.24.refs_0_, f32[2,8,128]{2,1,0:T(8,128)} %get-tuple-element.25.refs_1_, s32[8,128]{1,0:T(8,128)} %get-tuple-element.26.marks_in.refs_2_, f32[48,128]{1,0:T(8,128)} %copy-done, f32[48,128]{1,0:T(8,128)} %copy-done.4, ...), custom_call_target="tpu_custom_call" | custom-call | tf_op jit(solution)/shard_map/middle/pallas_call | solution.py:492
  69.3 1.9 %collective-permute-start.10 = (f32[16,128]{1,0:T(8,128)}, f32[16,128]{1,0:T(8,128)S(1)}, u32[]{:S(2)}, u32[]{:S(2)}) collective-permute-start(f32[16,128]{1,0:T(8,128)} %get-tuple-element.35), channel_id=1, source_target_pairs={{1,2},{3,4},{5,6},{2,1},{4,3},{6,5},{9,10},{11,12},{13,14},{10,9},... | collective-permute-start | bytes 24584 | tf_op jit(solution)/shard_map/ppermute | solution.py:553
  71.2 1.4 %collective-permute-start.11 = (f32[16,128]{1,0:T(8,128)}, f32[16,128]{1,0:T(8,128)S(1)}, u32[]{:S(2)}, u32[]{:S(2)}) collective-permute-start(f32[16,128]{1,0:T(8,128)} %get-tuple-element.35), channel_id=1, source_target_pairs={{0,1},{2,3},{4,5},{6,7},{1,0},{3,2},{5,4},{7,6},{8,9},{10,11},{12,... | collective-permute-start | bytes 24584 | tf_op jit(solution)/shard_map/ppermute | solution.py:553
  72.6 1.9 %collective-permute-done.10 = f32[16,128]{1,0:T(8,128)S(1)} collective-permute-done((f32[16,128]{1,0:T(8,128)}, f32[16,128]{1,0:T(8,128)S(1)}, u32[]{:S(2)}, u32[]{:S(2)}) %collective-permute-start.10) | collective-permute-done | bytes 8224 | tf_op jit(solution)/shard_map/ppermute | solution.py:553
  74.5 0.7 constant_dynamic-update-slice_fusion.4
  75.2 0.0 collective-permute-done.11
  75.2 0.0 copy-start.1
  75.2 4.3 %collective-permute-start.13 = (f32[48,128]{1,0:T(8,128)S(1)}, f32[48,128]{1,0:T(8,128)S(1)}, u32[]{:S(2)}, u32[]{:S(2)}) collective-permute-start(f32[48,128]{1,0:T(8,128)S(1)} %constant_dynamic-update-slice_fusion.3.refs_3_), channel_id=1, source_target_pairs={{8,16},{24,32},{40,48},{56,64},{72,80},{88,96},{104,112},{120,128}... | collective-permute-start | bytes 73736 | tf_op jit(solution)/shard_map/ppermute | solution.py:553
  79.5 0.0 copy-done.1
  79.5 0.1 collective-permute-start.12
  79.6 3.4 %collective-permute-done.13.refs_5_ = f32[48,128]{1,0:T(8,128)S(1)} collective-permute-done((f32[48,128]{1,0:T(8,128)S(1)}, f32[48,128]{1,0:T(8,128)S(1)}, u32[]{:S(2)}, u32[]{:S(2)}) %collective-permute-start.13) | collective-permute-done | bytes 24608 | tf_op jit(solution)/shard_map/ppermute | solution.py:553
  83.0 0.0 copy-start.3
  83.0 0.4 collective-permute-done.12.refs_4_
  83.4 0.2 copy-done.3
  83.6 0.0 copy-start.5
  83.6 0.6 copy-done.5
  84.2 6.4 %last.1 = f32[128,32,128]{2,1,0:T(8,128)} custom-call(f32[2,128,128]{2,1,0:T(8,128)} %get-tuple-element.24.refs_0_, f32[2,8,128]{2,1,0:T(8,128)} %get-tuple-element.25.refs_1_, s32[8,128]{1,0:T(8,128)} %get-tuple-element.26.marks_in.refs_2_, f32[48,128]{1,0:T(8,128)} %copy-done.1, f32[48,128]{1,0:T(8,128)} %copy-done.5, f32[48,128]{1,0:T(8,128)} %copy-done.3, ...), custom_call_target="tpu_custom_call" | custom-call | tf_op jit(solution)/shard_map/last/pallas_call | solution.py:535
  (4 shorter events, 0.0 us)
Async XLA Ops:
  2.5 15.8 %collective-permute-start = (f32[7,128,128]{2,1,0:T(8,128)}, f32[7,128,128]{2,1,0:T(8,128)}, u32[]{:S(2)}, u32[]{:S(2)}) collective-permute-start(f32[7,128,128]{2,1,0:T(8,128)} %get-tuple-element.21), channel_id=1, source_target_pairs={{0,8},{16,24},{32,40},{48,56},{64,72},{80,88},{96,104},{112,120},{... | collective-permute-start | bytes 1376264 | tf_op jit(solution)/shard_map/ppermute | solution.py:553
  4.5 17.6 %collective-permute-start.1 = (f32[7,128,128]{2,1,0:T(8,128)}, f32[7,128,128]{2,1,0:T(8,128)}, u32[]{:S(2)}, u32[]{:S(2)}) collective-permute-start(f32[7,128,128]{2,1,0:T(8,128)} %get-tuple-element.22), channel_id=1, source_target_pairs={{8,16},{24,32},{40,48},{56,64},{72,80},{88,96},{104,112},{120,128}... | collective-permute-start | bytes 1376264 | tf_op jit(solution)/shard_map/ppermute | solution.py:553
  15.7 15.4 %collective-permute-start.2 = (f32[34,8,128]{2,1,0:T(8,128)}, f32[34,8,128]{2,1,0:T(8,128)}, u32[]{:S(2)}, u32[]{:S(2)}) collective-permute-start(f32[34,8,128]{2,1,0:T(8,128)} %get-tuple-element.29), channel_id=1, source_target_pairs={{0,1},{2,3},{4,5},{6,7},{1,0},{3,2},{5,4},{7,6},{8,9},{10,11},{12,... | collective-permute-start | bytes 417800 | tf_op jit(solution)/shard_map/ppermute | solution.py:553
  15.7 15.4 %collective-permute-start.3 = (f32[34,8,128]{2,1,0:T(8,128)}, f32[34,8,128]{2,1,0:T(8,128)}, u32[]{:S(2)}, u32[]{:S(2)}) collective-permute-start(f32[34,8,128]{2,1,0:T(8,128)} %get-tuple-element.30), channel_id=1, source_target_pairs={{1,2},{3,4},{5,6},{2,1},{4,3},{6,5},{9,10},{11,12},{13,14},{10,9},... | collective-permute-start | bytes 417800 | tf_op jit(solution)/shard_map/ppermute | solution.py:553
  23.5 7.7 %collective-permute-start.5 = (f32[14,8,128]{2,1,0:T(8,128)}, f32[14,8,128]{2,1,0:T(8,128)}, u32[]{:S(2)}, u32[]{:S(2)}) collective-permute-start(f32[14,8,128]{2,1,0:T(8,128)} %get-tuple-element.31), channel_id=1, source_target_pairs={{1,2},{3,4},{5,6},{2,1},{4,3},{6,5},{9,10},{11,12},{13,14},{10,9},... | collective-permute-start | bytes 172040 | tf_op jit(solution)/shard_map/ppermute | solution.py:553
  25.4 5.8 %collective-permute-start.4 = (f32[14,8,128]{2,1,0:T(8,128)}, f32[14,8,128]{2,1,0:T(8,128)}, u32[]{:S(2)}, u32[]{:S(2)}) collective-permute-start(f32[14,8,128]{2,1,0:T(8,128)} %get-tuple-element.23.after), channel_id=1, source_target_pairs={{0,1},{2,3},{4,5},{6,7},{1,0},{3,2},{5,4},{7,6},{8,9},{10,11},{12,... | collective-permute-start | bytes 172040 | tf_op jit(solution)/shard_map/ppermute | solution.py:553
  41.7 5.2 %collective-permute-start.6 = (f32[16,128]{1,0:T(8,128)}, f32[16,128]{1,0:T(8,128)S(1)}, u32[]{:S(2)}, u32[]{:S(2)}) collective-permute-start(f32[16,128]{1,0:T(8,128)} %get-tuple-element.32), channel_id=1, source_target_pairs={{1,2},{3,4},{5,6},{2,1},{4,3},{6,5},{9,10},{11,12},{13,14},{10,9},... | collective-permute-start | bytes 24584 | tf_op jit(solution)/shard_map/ppermute | solution.py:553
  43.8 3.8 %collective-permute-start.7 = (f32[16,128]{1,0:T(8,128)}, f32[16,128]{1,0:T(8,128)S(1)}, u32[]{:S(2)}, u32[]{:S(2)}) collective-permute-start(f32[16,128]{1,0:T(8,128)} %get-tuple-element.32), channel_id=1, source_target_pairs={{0,1},{2,3},{4,5},{6,7},{1,0},{3,2},{5,4},{7,6},{8,9},{10,11},{12,... | collective-permute-start | bytes 24584 | tf_op jit(solution)/shard_map/ppermute | solution.py:553
  47.6 5.8 %copy-start = (f32[48,128]{1,0:T(8,128)}, f32[48,128]{1,0:T(8,128)S(1)}, u32[]{:S(2)}) copy-start(f32[48,128]{1,0:T(8,128)S(1)} %constant_dynamic-update-slice_fusion.refs_3_) | copy-start | bytes 73732
  47.6 7.8 %collective-permute-start.9 = (f32[48,128]{1,0:T(8,128)S(1)}, f32[48,128]{1,0:T(8,128)S(1)}, u32[]{:S(2)}, u32[]{:S(2)}) collective-permute-start(f32[48,128]{1,0:T(8,128)S(1)} %constant_dynamic-update-slice_fusion.refs_3_), channel_id=1, source_target_pairs={{8,16},{24,32},{40,48},{56,64},{72,80},{88,96},{104,112},{120,128}... | collective-permute-start | bytes 73736 | tf_op jit(solution)/shard_map/ppermute | solution.py:553
  53.3 4.1 %collective-permute-start.8 = (f32[48,128]{1,0:T(8,128)S(1)}, f32[48,128]{1,0:T(8,128)S(1)}, u32[]{:S(2)}, u32[]{:S(2)}) collective-permute-start(f32[48,128]{1,0:T(8,128)S(1)} %constant_dynamic-update-slice_fusion.refs_3_), channel_id=1, source_target_pairs={{0,8},{16,24},{32,40},{48,56},{64,72},{80,88},{96,104},{112,120},{... | collective-permute-start | bytes 73736 | tf_op jit(solution)/shard_map/ppermute | solution.py:553
  55.4 2.0 %copy-start.2 = (f32[48,128]{1,0:T(8,128)}, f32[48,128]{1,0:T(8,128)S(1)}, u32[]{:S(2)}) copy-start(f32[48,128]{1,0:T(8,128)S(1)} %collective-permute-done.9.refs_5_) | copy-start | bytes 73732
  57.4 0.6 copy-start.4
  69.3 5.2 %collective-permute-start.10 = (f32[16,128]{1,0:T(8,128)}, f32[16,128]{1,0:T(8,128)S(1)}, u32[]{:S(2)}, u32[]{:S(2)}) collective-permute-start(f32[16,128]{1,0:T(8,128)} %get-tuple-element.35), channel_id=1, source_target_pairs={{1,2},{3,4},{5,6},{2,1},{4,3},{6,5},{9,10},{11,12},{13,14},{10,9},... | collective-permute-start | bytes 24584 | tf_op jit(solution)/shard_map/ppermute | solution.py:553
  71.2 4.0 %collective-permute-start.11 = (f32[16,128]{1,0:T(8,128)}, f32[16,128]{1,0:T(8,128)S(1)}, u32[]{:S(2)}, u32[]{:S(2)}) collective-permute-start(f32[16,128]{1,0:T(8,128)} %get-tuple-element.35), channel_id=1, source_target_pairs={{0,1},{2,3},{4,5},{6,7},{1,0},{3,2},{5,4},{7,6},{8,9},{10,11},{12,... | collective-permute-start | bytes 24584 | tf_op jit(solution)/shard_map/ppermute | solution.py:553
  75.2 4.3 %copy-start.1 = (f32[48,128]{1,0:T(8,128)}, f32[48,128]{1,0:T(8,128)S(1)}, u32[]{:S(2)}) copy-start(f32[48,128]{1,0:T(8,128)S(1)} %constant_dynamic-update-slice_fusion.3.refs_3_) | copy-start | bytes 73732
  75.2 7.8 %collective-permute-start.13 = (f32[48,128]{1,0:T(8,128)S(1)}, f32[48,128]{1,0:T(8,128)S(1)}, u32[]{:S(2)}, u32[]{:S(2)}) collective-permute-start(f32[48,128]{1,0:T(8,128)S(1)} %constant_dynamic-update-slice_fusion.3.refs_3_), channel_id=1, source_target_pairs={{8,16},{24,32},{40,48},{56,64},{72,80},{88,96},{104,112},{120,128}... | collective-permute-start | bytes 73736 | tf_op jit(solution)/shard_map/ppermute | solution.py:553
  79.5 3.9 %collective-permute-start.12 = (f32[48,128]{1,0:T(8,128)S(1)}, f32[48,128]{1,0:T(8,128)S(1)}, u32[]{:S(2)}, u32[]{:S(2)}) collective-permute-start(f32[48,128]{1,0:T(8,128)S(1)} %constant_dynamic-update-slice_fusion.3.refs_3_), channel_id=1, source_target_pairs={{0,8},{16,24},{32,40},{48,56},{64,72},{80,88},{96,104},{112,120},{... | collective-permute-start | bytes 73736 | tf_op jit(solution)/shard_map/ppermute | solution.py:553
  83.0 0.6 copy-start.3
  83.6 0.6 copy-start.5

commit v4 on v3

--- a/solution.py
+++ b/solution.py
@@ -120,7 +120,7 @@
     )(heads, tiles)
 
 
-def corner_kernel(even_left, even_right, odd_left, odd_right, give_even, give_odd):
+def corner_kernel(even_left, even_right, odd_left, odd_right, after, give_even, give_odd):
     flip_n = parity("north") == 0
     flip_e = parity("east") == 0
     for half, swap_n in enumerate((flip_n, jnp.logical_not(flip_n))):
@@ -131,7 +131,7 @@
         give_odd[part] = jnp.where(flip_e, left, right)
 
 
-def corners(got_even, got_odd):
+def corners(got_even, got_odd, after):
     def cut(at):
         return pl.BlockSpec((HALO + 1, EDGE, LANES), lambda i: (0, at, 0))
 
@@ -142,11 +142,11 @@
         corner_kernel,
         grid=(1,),
         out_shape=(shape, shape),
-        in_specs=[cut(0), cut(last), cut(0), cut(last)],
+        in_specs=[cut(0), cut(last), cut(0), cut(last), HBM],
         out_specs=(whole, whole),
         compiler_params=params(),
         name="corners",
-    )(got_even, got_even, got_odd, got_odd)
+    )(got_even, got_even, got_odd, got_odd, after)
 
 
 def spread_matrix():
@@ -343,7 +343,7 @@
     flip = parity("east") == 0
     for third, source in enumerate((north, mid[...], south)):
         first, final = source[:OWN], source[2 * OWN :]
-        west, east = jnp.where(flip, first, final), jnp.where(flip, final, first)
+        west, east = jnp.where(flip, final, first), jnp.where(flip, first, final)
         for half in range(OWN_ROWS):
             base = (third * OWN_ROWS + half) * CELL_COLS
             own = half * OWN_COLS
@@ -556,7 +556,7 @@
 def gather_slots(slots):
     odd = swap(slots, "east", 1)
     even = swap(slots, "east", 0)
-    mid = jnp.concatenate([odd, slots, even], axis=0)
+    mid = jnp.concatenate([even, slots, odd], axis=0)
     return mid, swap(mid, "north", 0), swap(mid, "north", 1)
 
 
@@ -650,9 +650,9 @@
     ns_odd, ns_even = swap(give_odd, "north", 1), swap(give_even, "north", 0)
     turned, give_even, give_odd = turn(heads.reshape(LANES * ROWS, COLS), tiles)
     ew_odd, ew_even = swap(give_odd, "east", 1), swap(give_even, "east", 0)
-    give_even, give_odd = corners(ns_even, ns_odd)
+    guides = slot_tables(obs_value, obs_error, obs_spot, obs_live, batch_colour, give_even)
+    give_even, give_odd = corners(ns_even, ns_odd, guides[2])
     corner_odd, corner_even = swap(give_odd, "east", 1), swap(give_even, "east", 0)
-    guides = slot_tables(obs_value, obs_error, obs_spot, obs_live, batch_colour, give_even)
     pieces = (turned, tiles, ns_even, ns_odd, ew_even, ew_odd, corner_even, corner_odd)
     cast, slots, ext_tiles = first_forecast(pieces, guides[2])
     gathered = gather_slots(slots)

time: 91.3 us -> 88.6 us (0.970)
  starting transfers between devices: 32.1 us -> 28.7 us
    ppermute x14, starting transfers between devices: 32.1 us -> 28.7 us  [swap(): lax.ppermute(x, axis, [(i, i + 1) for i in low] + [(i + 1, i) for i in low])]
where the time goes in v4:
time: 88.6 us; the launch traced here: 88.1 us
  Pallas kernels  40.4 us (46%)
  starting transfers between devices  28.7 us (32%)
  waiting for transfers between devices  15.7 us (18%)
  local copies, waits for them, and re-layouts  2.86 us (3%)
    ppermute x14, starting transfers between devices, swap(): lax.ppermute(x, axis, [(i, i + 1) for i in low] + [(i + 1, i) for i in low])  28.7 us
    ppermute x14, waiting for transfers between devices, swap(): lax.ppermute(x, axis, [(i, i + 1) for i in low] + [(i + 1, i) for i in low])  15.7 us
    pallas_call x1, Pallas kernels, middle(): pl.pallas_call(middle_kernel, out_shape=(jax.ShapeDtypeStruct((ROWS, COLS...  11.2 us
    pallas_call x1, Pallas kernels, first_forecast(): pl.pallas_call(first_kernel, out_shape=(jax.ShapeDtypeStruct((ROWS + 2 *...  10.5 us
    pallas_call x1, Pallas kernels, last(): pl.pallas_call(last_kernel, out_shape=jax.ShapeDtypeStruct((LANES, ROWS,...  6.36 us
    pallas_call x1, Pallas kernels, turn(): pl.pallas_call(turn_kernel, out_shape=(jax.ShapeDtypeStruct((ROWS, COLS,...  4.26 us
    pallas_call x1, Pallas kernels, slot_tables(): pl.pallas_call(table_kernel, out_shape=(jax.ShapeDtypeStruct((ANALYSES, L...  4.08 us
    unnamed x16, local copies, waits for them, and re-layouts  2.86 us
  transfers between devices with their start and end apart: 14, of which 7 were waited for; matrix products, arithmetic and copies ran while one was open for 2% of the time, Pallas kernels for 11%

profile of v4, /device:TPU:26, one launch (start us, length us, event | category | flops | bytes accessed | tf_op | source)
XLA Modules:
  0.0 88.1 jit_solution(5169059775691029119)
XLA Ops:
  0.0 2.5 %edges.1 = (f32[2,128,128]{2,1,0:T(8,128)}, f32[7,128,128]{2,1,0:T(8,128)}, f32[7,128,128]{2,1,0:T(8,128)}) custom-call(f32[128,32,128]{2,1,0:T(8,128)} %bitcast.3, f32[128,32,128]{2,1,0:T(8,128)} %bitcast.4, f32[2,32,128]{2,1,0:T(8,128)} %rest_0_.1, f32[32,128]{1,0:T(8,128)} %rest_1_.1, f32[32,128]{1,0:T(8,128)} %rest_2_.1, f32[32,128]{1,0:T(8,128)} %rest_3_.1), custom_call_target="tpu_custom_call" | custom-call | tf_op jit(solution)/shard_map/edges/pallas_call | solution.py:85
  2.5 1.9 %collective-permute-start = (f32[7,128,128]{2,1,0:T(8,128)}, f32[7,128,128]{2,1,0:T(8,128)}, u32[]{:S(2)}, u32[]{:S(2)}) collective-permute-start(f32[7,128,128]{2,1,0:T(8,128)} %get-tuple-element.27), channel_id=1, source_target_pairs={{0,8},{16,24},{32,40},{48,56},{64,72},{80,88},{96,104},{112,120},{... | collective-permute-start | bytes 1376264 | tf_op jit(solution)/shard_map/ppermute | solution.py:553
  4.5 7.0 %collective-permute-start.1 = (f32[7,128,128]{2,1,0:T(8,128)}, f32[7,128,128]{2,1,0:T(8,128)}, u32[]{:S(2)}, u32[]{:S(2)}) collective-permute-start(f32[7,128,128]{2,1,0:T(8,128)} %get-tuple-element.28), channel_id=1, source_target_pairs={{8,16},{24,32},{40,48},{56,64},{72,80},{88,96},{104,112},{120,128}... | collective-permute-start | bytes 1376264 | tf_op jit(solution)/shard_map/ppermute | solution.py:553
  11.5 4.3 %turn.1 = (f32[32,128,128]{2,1,0:T(8,128)}, f32[34,8,128]{2,1,0:T(8,128)}, f32[34,8,128]{2,1,0:T(8,128)}) custom-call(f32[4096,128]{1,0:T(8,128)} %bitcast.5, f32[2,128,128]{2,1,0:T(8,128)} %get-tuple-element.21.tiles), custom_call_target="tpu_custom_call" | custom-call | bytes 14000000 | tf_op jit(solution)/shard_map/turn/pallas_call | solution.py:112
  15.7 1.9 %collective-permute-start.3 = (f32[34,8,128]{2,1,0:T(8,128)}, f32[34,8,128]{2,1,0:T(8,128)}, u32[]{:S(2)}, u32[]{:S(2)}) collective-permute-start(f32[34,8,128]{2,1,0:T(8,128)} %get-tuple-element.29), channel_id=1, source_target_pairs={{1,2},{3,4},{5,6},{2,1},{4,3},{6,5},{9,10},{11,12},{13,14},{10,9},... | collective-permute-start | bytes 417800 | tf_op jit(solution)/shard_map/ppermute | solution.py:553
  17.7 1.7 %collective-permute-start.2 = (f32[34,8,128]{2,1,0:T(8,128)}, f32[34,8,128]{2,1,0:T(8,128)}, u32[]{:S(2)}, u32[]{:S(2)}) collective-permute-start(f32[34,8,128]{2,1,0:T(8,128)} %get-tuple-element.22.after), channel_id=1, source_target_pairs={{0,1},{2,3},{4,5},{6,7},{1,0},{3,2},{5,4},{7,6},{8,9},{10,11},{12,... | collective-permute-start | bytes 417800 | tf_op jit(solution)/shard_map/ppermute | solution.py:553
  19.3 4.1 %slot_tables.1 = (f32[2,128,128]{2,1,0:T(8,128)}, f32[2,8,128]{2,1,0:T(8,128)}, s32[8,128]{1,0:T(8,128)}) custom-call(s32[2,4]{1,0:T(2,128)} %colours.1, f32[2,4,32,32]{3,2,1,0:T(8,128)} %value.1, f32[2,4,32,32]{3,2,1,0:T(8,128)} %noise.1, s32[2,4,32,32]{3,2,1,0:T(8,128)} %spot.1, s32[2,4,32,32]{3,2,1,0:T(8,128)} %live.1, f32[34,8,128]{2,1,0:T(8,128)} %get-tuple-element.22.after), custom_call_target="tpu_custom_call" | custom-call | bytes 10500000 | tf_op jit(solution)/shard_map/slot_tables/pallas_call | solution.py:618
  23.4 0.0 collective-permute-done.even_left.even_right.ns_even
  23.4 0.0 collective-permute-done.1.odd_left.odd_right.ns_odd
  23.4 1.5 %corners.1 = (f32[14,8,128]{2,1,0:T(8,128)}, f32[14,8,128]{2,1,0:T(8,128)}) custom-call(f32[7,128,128]{2,1,0:T(8,128)} %collective-permute-done.even_left.even_right.ns_even, f32[7,128,128]{2,1,0:T(8,128)} %collective-permute-done.even_left.even_right.ns_even, f32[7,128,128]{2,1,0:T(8,128)} %collective-permute-done.1.odd_left.odd_right.ns_odd, ...), custom_call_target="tpu_custom_call" | custom-call | tf_op jit(solution)/shard_map/corners/pallas_call | solution.py:141
  24.9 0.0 collective-permute-start.4
  24.9 2.5 %collective-permute-start.5 = (f32[14,8,128]{2,1,0:T(8,128)}, f32[14,8,128]{2,1,0:T(8,128)}, u32[]{:S(2)}, u32[]{:S(2)}) collective-permute-start(f32[14,8,128]{2,1,0:T(8,128)} %get-tuple-element.31), channel_id=1, source_target_pairs={{1,2},{3,4},{5,6},{2,1},{4,3},{6,5},{9,10},{11,12},{13,14},{10,9},... | collective-permute-start | bytes 172040 | tf_op jit(solution)/shard_map/ppermute | solution.py:553
  27.4 0.0 collective-permute-done.3.ew_odd
  27.4 0.0 collective-permute-done.2.ew_even
  27.5 0.0 collective-permute-done.4.corner_even
  27.5 3.2 %collective-permute-done.5.corner_odd = f32[14,8,128]{2,1,0:T(8,128)} collective-permute-done((f32[14,8,128]{2,1,0:T(8,128)}, f32[14,8,128]{2,1,0:T(8,128)}, u32[]{:S(2)}, u32[]{:S(2)}) %collective-permute-start.5) | collective-permute-done | bytes 57376 | tf_op jit(solution)/shard_map/ppermute | solution.py:553
  30.7 10.5 %first_forecast.1 = (f32[38,144,128]{2,1,0:T(8,128)}, f32[16,128]{1,0:T(8,128)}, f32[4,144,128]{2,1,0:T(8,128)}) custom-call(f32[32,128,128]{2,1,0:T(8,128)} %get-tuple-element.26.turned, f32[2,128,128]{2,1,0:T(8,128)} %get-tuple-element.21.tiles, f32[7,128,128]{2,1,0:T(8,128)} %collective-permute-done.even_left.even_right.ns_even, ...), custom_call_target="tpu_custom_call" | custom-call | tf_op jit(solution)/shard_map/first_forecast/pallas_call | solution.py:309
  41.2 0.6 collective-permute-start.6
  41.8 2.1 %collective-permute-start.7 = (f32[16,128]{1,0:T(8,128)}, f32[16,128]{1,0:T(8,128)S(1)}, u32[]{:S(2)}, u32[]{:S(2)}) collective-permute-start(f32[16,128]{1,0:T(8,128)} %get-tuple-element.32), channel_id=1, source_target_pairs={{1,2},{3,4},{5,6},{2,1},{4,3},{6,5},{9,10},{11,12},{13,14},{10,9},... | collective-permute-start | bytes 24584 | tf_op jit(solution)/shard_map/ppermute | solution.py:553
  43.9 0.0 collective-permute-done.6
  43.9 0.7 constant_dynamic-update-slice_fusion.1
  44.6 2.4 %collective-permute-done.7 = f32[16,128]{1,0:T(8,128)S(1)} collective-permute-done((f32[16,128]{1,0:T(8,128)}, f32[16,128]{1,0:T(8,128)S(1)}, u32[]{:S(2)}, u32[]{:S(2)}) %collective-permute-start.7) | collective-permute-done | bytes 8224 | tf_op jit(solution)/shard_map/ppermute | solution.py:553
  47.0 0.0 copy-start
  47.0 4.3 %collective-permute-start.9 = (f32[48,128]{1,0:T(8,128)S(1)}, f32[48,128]{1,0:T(8,128)S(1)}, u32[]{:S(2)}, u32[]{:S(2)}) collective-permute-start(f32[48,128]{1,0:T(8,128)S(1)} %constant_dynamic-update-slice_fusion.refs_3_), channel_id=1, source_target_pairs={{8,16},{24,32},{40,48},{56,64},{72,80},{88,96},{104,112},{120,128}... | collective-permute-start | bytes 73736 | tf_op jit(solution)/shard_map/ppermute | solution.py:553
  51.3 0.0 copy-done
  51.3 0.3 collective-permute-start.8
  51.6 3.2 %collective-permute-done.9.refs_5_ = f32[48,128]{1,0:T(8,128)S(1)} collective-permute-done((f32[48,128]{1,0:T(8,128)S(1)}, f32[48,128]{1,0:T(8,128)S(1)}, u32[]{:S(2)}, u32[]{:S(2)}) %collective-permute-start.9) | collective-permute-done | bytes 24608 | tf_op jit(solution)/shard_map/ppermute | solution.py:553
  54.8 0.0 copy-start.2
  54.8 0.6 collective-permute-done.8.refs_4_
  55.4 0.0 copy-done.2
  55.4 0.0 copy-start.4
  55.4 0.6 copy-done.4
  56.0 11.2 %middle.1 = (f32[32,128,128]{2,1,0:T(8,128)}, f32[16,128]{1,0:T(8,128)}) custom-call(f32[2,128,128]{2,1,0:T(8,128)} %get-tuple-element.23.refs_0_, f32[2,8,128]{2,1,0:T(8,128)} %get-tuple-element.24.refs_1_, s32[8,128]{1,0:T(8,128)} %get-tuple-element.25.after.marks_in.refs_2_, f32[48,128]{1,0:T(8,128)} %copy-done, f32[48,128]{1,0:T(8,128)} %copy-done.4, ...), custom_call_target="tpu_custom_call" | custom-call | tf_op jit(solution)/shard_map/middle/pallas_call | solution.py:492
  67.3 0.1 collective-permute-start.10
  67.4 1.9 %collective-permute-start.11 = (f32[16,128]{1,0:T(8,128)}, f32[16,128]{1,0:T(8,128)S(1)}, u32[]{:S(2)}, u32[]{:S(2)}) collective-permute-start(f32[16,128]{1,0:T(8,128)} %get-tuple-element.35), channel_id=1, source_target_pairs={{1,2},{3,4},{5,6},{2,1},{4,3},{6,5},{9,10},{11,12},{13,14},{10,9},... | collective-permute-start | bytes 24584 | tf_op jit(solution)/shard_map/ppermute | solution.py:553
  69.3 0.0 collective-permute-done.10
  69.3 0.7 constant_dynamic-update-slice_fusion.4
  70.0 2.5 %collective-permute-done.11 = f32[16,128]{1,0:T(8,128)S(1)} collective-permute-done((f32[16,128]{1,0:T(8,128)}, f32[16,128]{1,0:T(8,128)S(1)}, u32[]{:S(2)}, u32[]{:S(2)}) %collective-permute-start.11) | collective-permute-done | bytes 8224 | tf_op jit(solution)/shard_map/ppermute | solution.py:553
  72.5 0.0 copy-start.1
  72.5 4.3 %collective-permute-start.13 = (f32[48,128]{1,0:T(8,128)S(1)}, f32[48,128]{1,0:T(8,128)S(1)}, u32[]{:S(2)}, u32[]{:S(2)}) collective-permute-start(f32[48,128]{1,0:T(8,128)S(1)} %constant_dynamic-update-slice_fusion.3.refs_3_), channel_id=1, source_target_pairs={{8,16},{24,32},{40,48},{56,64},{72,80},{88,96},{104,112},{120,128}... | collective-permute-start | bytes 73736 | tf_op jit(solution)/shard_map/ppermute | solution.py:553
  76.9 0.0 copy-done.1
  76.9 0.1 collective-permute-start.12
  77.0 3.4 %collective-permute-done.13.refs_5_ = f32[48,128]{1,0:T(8,128)S(1)} collective-permute-done((f32[48,128]{1,0:T(8,128)S(1)}, f32[48,128]{1,0:T(8,128)S(1)}, u32[]{:S(2)}, u32[]{:S(2)}) %collective-permute-start.13) | collective-permute-done | bytes 24608 | tf_op jit(solution)/shard_map/ppermute | solution.py:553
  80.4 0.0 copy-start.3
  80.4 0.4 collective-permute-done.12.refs_4_
  80.8 0.2 copy-done.3
  81.0 0.0 copy-start.5
  81.0 0.6 copy-done.5
  81.6 6.4 %last.1 = f32[128,32,128]{2,1,0:T(8,128)} custom-call(f32[2,128,128]{2,1,0:T(8,128)} %get-tuple-element.23.refs_0_, f32[2,8,128]{2,1,0:T(8,128)} %get-tuple-element.24.refs_1_, s32[8,128]{1,0:T(8,128)} %get-tuple-element.25.after.marks_in.refs_2_, f32[48,128]{1,0:T(8,128)} %copy-done.1, f32[48,128]{1,0:T(8,128)} %copy-done.5, f32[48,128]{1,0:T(8,128)} %copy-done.3, ...), custom_call_target="tpu_custom_call" | custom-call | tf_op jit(solution)/shard_map/last/pallas_call | solution.py:535
  (4 shorter events, 0.0 us)
Async XLA Ops:
  2.5 20.9 %collective-permute-start = (f32[7,128,128]{2,1,0:T(8,128)}, f32[7,128,128]{2,1,0:T(8,128)}, u32[]{:S(2)}, u32[]{:S(2)}) collective-permute-start(f32[7,128,128]{2,1,0:T(8,128)} %get-tuple-element.27), channel_id=1, source_target_pairs={{0,8},{16,24},{32,40},{48,56},{64,72},{80,88},{96,104},{112,120},{... | collective-permute-start | bytes 1376264 | tf_op jit(solution)/shard_map/ppermute | solution.py:553
  4.5 19.0 %collective-permute-start.1 = (f32[7,128,128]{2,1,0:T(8,128)}, f32[7,128,128]{2,1,0:T(8,128)}, u32[]{:S(2)}, u32[]{:S(2)}) collective-permute-start(f32[7,128,128]{2,1,0:T(8,128)} %get-tuple-element.28), channel_id=1, source_target_pairs={{8,16},{24,32},{40,48},{56,64},{72,80},{88,96},{104,112},{120,128}... | collective-permute-start | bytes 1376264 | tf_op jit(solution)/shard_map/ppermute | solution.py:553
  15.7 11.7 %collective-permute-start.3 = (f32[34,8,128]{2,1,0:T(8,128)}, f32[34,8,128]{2,1,0:T(8,128)}, u32[]{:S(2)}, u32[]{:S(2)}) collective-permute-start(f32[34,8,128]{2,1,0:T(8,128)} %get-tuple-element.29), channel_id=1, source_target_pairs={{1,2},{3,4},{5,6},{2,1},{4,3},{6,5},{9,10},{11,12},{13,14},{10,9},... | collective-permute-start | bytes 417800 | tf_op jit(solution)/shard_map/ppermute | solution.py:553
  17.7 9.8 %collective-permute-start.2 = (f32[34,8,128]{2,1,0:T(8,128)}, f32[34,8,128]{2,1,0:T(8,128)}, u32[]{:S(2)}, u32[]{:S(2)}) collective-permute-start(f32[34,8,128]{2,1,0:T(8,128)} %get-tuple-element.22.after), channel_id=1, source_target_pairs={{0,1},{2,3},{4,5},{6,7},{1,0},{3,2},{5,4},{7,6},{8,9},{10,11},{12,... | collective-permute-start | bytes 417800 | tf_op jit(solution)/shard_map/ppermute | solution.py:553
  24.9 2.6 %collective-permute-start.4 = (f32[14,8,128]{2,1,0:T(8,128)}, f32[14,8,128]{2,1,0:T(8,128)}, u32[]{:S(2)}, u32[]{:S(2)}) collective-permute-start(f32[14,8,128]{2,1,0:T(8,128)} %get-tuple-element.30), channel_id=1, source_target_pairs={{0,1},{2,3},{4,5},{6,7},{1,0},{3,2},{5,4},{7,6},{8,9},{10,11},{12,... | collective-permute-start | bytes 172040 | tf_op jit(solution)/shard_map/ppermute | solution.py:553
  24.9 5.8 %collective-permute-start.5 = (f32[14,8,128]{2,1,0:T(8,128)}, f32[14,8,128]{2,1,0:T(8,128)}, u32[]{:S(2)}, u32[]{:S(2)}) collective-permute-start(f32[14,8,128]{2,1,0:T(8,128)} %get-tuple-element.31), channel_id=1, source_target_pairs={{1,2},{3,4},{5,6},{2,1},{4,3},{6,5},{9,10},{11,12},{13,14},{10,9},... | collective-permute-start | bytes 172040 | tf_op jit(solution)/shard_map/ppermute | solution.py:553
  41.2 2.7 %collective-permute-start.6 = (f32[16,128]{1,0:T(8,128)}, f32[16,128]{1,0:T(8,128)S(1)}, u32[]{:S(2)}, u32[]{:S(2)}) collective-permute-start(f32[16,128]{1,0:T(8,128)} %get-tuple-element.32), channel_id=1, source_target_pairs={{0,1},{2,3},{4,5},{6,7},{1,0},{3,2},{5,4},{7,6},{8,9},{10,11},{12,... | collective-permute-start | bytes 24584 | tf_op jit(solution)/shard_map/ppermute | solution.py:553
  41.8 5.2 %collective-permute-start.7 = (f32[16,128]{1,0:T(8,128)}, f32[16,128]{1,0:T(8,128)S(1)}, u32[]{:S(2)}, u32[]{:S(2)}) collective-permute-start(f32[16,128]{1,0:T(8,128)} %get-tuple-element.32), channel_id=1, source_target_pairs={{1,2},{3,4},{5,6},{2,1},{4,3},{6,5},{9,10},{11,12},{13,14},{10,9},... | collective-permute-start | bytes 24584 | tf_op jit(solution)/shard_map/ppermute | solution.py:553
  47.0 4.3 %copy-start = (f32[48,128]{1,0:T(8,128)}, f32[48,128]{1,0:T(8,128)S(1)}, u32[]{:S(2)}) copy-start(f32[48,128]{1,0:T(8,128)S(1)} %constant_dynamic-update-slice_fusion.refs_3_) | copy-start | bytes 73732
  47.0 7.8 %collective-permute-start.9 = (f32[48,128]{1,0:T(8,128)S(1)}, f32[48,128]{1,0:T(8,128)S(1)}, u32[]{:S(2)}, u32[]{:S(2)}) collective-permute-start(f32[48,128]{1,0:T(8,128)S(1)} %constant_dynamic-update-slice_fusion.refs_3_), channel_id=1, source_target_pairs={{8,16},{24,32},{40,48},{56,64},{72,80},{88,96},{104,112},{120,128}... | collective-permute-start | bytes 73736 | tf_op jit(solution)/shard_map/ppermute | solution.py:553
  51.3 4.1 %collective-permute-start.8 = (f32[48,128]{1,0:T(8,128)S(1)}, f32[48,128]{1,0:T(8,128)S(1)}, u32[]{:S(2)}, u32[]{:S(2)}) collective-permute-start(f32[48,128]{1,0:T(8,128)S(1)} %constant_dynamic-update-slice_fusion.refs_3_), channel_id=1, source_target_pairs={{0,8},{16,24},{32,40},{48,56},{64,72},{80,88},{96,104},{112,120},{... | collective-permute-start | bytes 73736 | tf_op jit(solution)/shard_map/ppermute | solution.py:553
  54.8 0.6 copy-start.2
  55.4 0.6 copy-start.4
  67.3 2.0 %collective-permute-start.10 = (f32[16,128]{1,0:T(8,128)}, f32[16,128]{1,0:T(8,128)S(1)}, u32[]{:S(2)}, u32[]{:S(2)}) collective-permute-start(f32[16,128]{1,0:T(8,128)} %get-tuple-element.35), channel_id=1, source_target_pairs={{0,1},{2,3},{4,5},{6,7},{1,0},{3,2},{5,4},{7,6},{8,9},{10,11},{12,... | collective-permute-start | bytes 24584 | tf_op jit(solution)/shard_map/ppermute | solution.py:553
  67.4 5.2 %collective-permute-start.11 = (f32[16,128]{1,0:T(8,128)}, f32[16,128]{1,0:T(8,128)S(1)}, u32[]{:S(2)}, u32[]{:S(2)}) collective-permute-start(f32[16,128]{1,0:T(8,128)} %get-tuple-element.35), channel_id=1, source_target_pairs={{1,2},{3,4},{5,6},{2,1},{4,3},{6,5},{9,10},{11,12},{13,14},{10,9},... | collective-permute-start | bytes 24584 | tf_op jit(solution)/shard_map/ppermute | solution.py:553
  72.5 4.3 %copy-start.1 = (f32[48,128]{1,0:T(8,128)}, f32[48,128]{1,0:T(8,128)S(1)}, u32[]{:S(2)}) copy-start(f32[48,128]{1,0:T(8,128)S(1)} %constant_dynamic-update-slice_fusion.3.refs_3_) | copy-start | bytes 73732
  72.5 7.8 %collective-permute-start.13 = (f32[48,128]{1,0:T(8,128)S(1)}, f32[48,128]{1,0:T(8,128)S(1)}, u32[]{:S(2)}, u32[]{:S(2)}) collective-permute-start(f32[48,128]{1,0:T(8,128)S(1)} %constant_dynamic-update-slice_fusion.3.refs_3_), channel_id=1, source_target_pairs={{8,16},{24,32},{40,48},{56,64},{72,80},{88,96},{104,112},{120,128}... | collective-permute-start | bytes 73736 | tf_op jit(solution)/shard_map/ppermute | solution.py:553
  76.9 3.9 %collective-permute-start.12 = (f32[48,128]{1,0:T(8,128)S(1)}, f32[48,128]{1,0:T(8,128)S(1)}, u32[]{:S(2)}, u32[]{:S(2)}) collective-permute-start(f32[48,128]{1,0:T(8,128)S(1)} %constant_dynamic-update-slice_fusion.3.refs_3_), channel_id=1, source_target_pairs={{0,8},{16,24},{32,40},{48,56},{64,72},{80,88},{96,104},{112,120},{... | collective-permute-start | bytes 73736 | tf_op jit(solution)/shard_map/ppermute | solution.py:553
  80.4 0.6 copy-start.3
  81.0 0.6 copy-start.5
